TPU v7x, 32 devices: a whole 2x2x4 slice. The times are simulated.
32 devices in a mesh: section: 2 (over x), edge: 8 (over z, y), mp: 2 (over core).
Axes of the slice: x: 2, y: 2, z: 4, core: 2. Of those that a mesh axis runs over, the one named last changes fastest.
Arguments:
- edge_vectors: float32 [3, 3, 3072], P(None, None, 'edge'), as said below
- edge_species: int32 [3, 2, 3072], P(None, None, 'edge'), may hold values from 0 to 3
- centres: int32 [3, 3072], P(None, 'edge'), may hold values from 0 to 319, as said below
- edge_mask: int32 [3, 3072], P(None, 'edge'), may hold values 0 or 1
- structures: int32 [3, 3072], P(None, 'edge'), may hold values from 0 to 15, never falling along the last dimension, each value on 1 to 384 neighbouring positions
- energy_cot: float32 [3, 16], replicated, may hold values from -6 to 6
- embed_in: float32 [16, 1024], replicated, may hold values from -1.5 to 1.5
- section_head: float32 [2, 1024, 1024], P('section', None, 'mp'), may hold values from -0.5 to 0.5
- env_weight: float32 [2, 1024, 64], P('section'), may hold values from -0.375 to 0.375
- mix_weight: float32 [3, 64, 64], replicated, may hold values from -0.75 to 0.75
- w_in: float32 [2, 1216, 1024], P('section', None, 'mp'), may hold values from -0.15625 to 0.15625
- w_out: float32 [2, 1024, 1024], P('section', 'mp'), may hold values from -0.1875 to 0.1875
- read_weight: float32 [1024], replicated, may hold values from -0.046875 to 0.046875
Outputs:
- energies: float32 [3, 16], replicated
- edge_forces: float32 [3, 3, 3072], P(None, None, 'edge')
- embed_grad: float32 [16, 1024], replicated
- head_grad: float32 [2, 1024, 1024], P('section', None, 'mp')
- env_grad: float32 [2, 1024, 64], P('section')
- mix_grad: float32 [3, 64, 64], replicated
- w_in_grad: float32 [2, 1216, 1024], P('section', None, 'mp')
- w_out_grad: float32 [2, 1024, 1024], P('section', 'mp')
- read_grad: float32 [1024], replicated
Inputs may be any that keep to these rules, and one draw needn't show every extreme that they name: `edge_vectors`: every edge vector is 0.4 to 5.3 long. `centres`: an edge in the block b of 384 edges of a micro-batch has its centre among atoms (b - 1) * 40 to (b + 2) * 40 - 1.
All inputs are finite; a program needn't handle non-finite values. No bound on the sum of `edge_mask` on one device may be relied on, other than what follows from the above.
Results may differ from a plain program's by a relative error of at most 0.0003.
Values sent between devices are 32-bit elements; how exact they have to be, the bound alone decides.
No kernel may reach another device: no remote copies, remote signals or barrier semaphores. Data moves between devices by JAX's collectives and lax.ppermute only.
A program may use at most 192 MiB of HBM per device.

v0:
```python
from functools import partial

import jax
import jax.numpy as jnp
from jax import lax
from jax.sharding import PartitionSpec as P

NBES = 8
NSPEC = 4
ATOM_DEV = 40
STRUCTS = 16


CUTOFF = 5.0
ENV_SCALE = 0.25
HIGHEST = lax.Precision.HIGHEST
ROOT_THREE = 1.7320508075688772
ROOT_FIVE = 2.23606797749979
ROOT_FIFTEEN = 3.872983346207417


def extended(block, sides, width):
    for axis, dim in sides:
        count = lax.axis_size(axis)
        forward = [(i, i + 1) for i in range(count - 1)]
        backward = [(target, source) for source, target in forward]
        low = lax.ppermute(
            lax.slice_in_dim(block, block.shape[dim] - width, None, axis=dim), axis, forward
        )
        high = lax.ppermute(lax.slice_in_dim(block, 0, width, axis=dim), axis, backward)
        block = jnp.concatenate([low, block, high], axis=dim)
    return block


def shifted(value, axis, steps):
    count = lax.axis_size(axis)
    first, last = (max(0, -steps), min(count, count - steps))
    return lax.ppermute(value, axis, [(source, source + steps) for source in range(first, last)])


def matmul(left, right):
    return jnp.dot(left, right, precision=HIGHEST, preferred_element_type=jnp.float32)


def geometry(vectors, edge_live):
    squares = jnp.maximum(jnp.sum(vectors * vectors, axis=0), 0.25)
    length = jnp.sqrt(squares)
    unit_x = vectors[0] / length
    unit_y = vectors[1] / length
    unit_z = vectors[2] / length
    edge_ratio = jnp.minimum(length / CUTOFF, 1.0)
    envelope = (
        1.0 - 28.0 * edge_ratio**6 + 48.0 * edge_ratio**7 - 21.0 * edge_ratio**8
    ) * edge_live
    orders = jnp.arange(1, NBES + 1).astype(jnp.float32)
    bessel = (
        jnp.sqrt(2.0 / CUTOFF)
        * jnp.sin(orders[None, :] * (jnp.pi / CUTOFF) * length[:, None])
        / length[:, None]
    )
    harmonics = jnp.stack(
        [
            jnp.ones_like(unit_x),
            ROOT_THREE * unit_x,
            ROOT_THREE * unit_y,
            ROOT_THREE * unit_z,
            ROOT_FIFTEEN * unit_x * unit_y,
            ROOT_FIFTEEN * unit_y * unit_z,
            0.5 * ROOT_FIVE * (3.0 * unit_z * unit_z - 1.0),
            ROOT_FIFTEEN * unit_x * unit_z,
            0.5 * ROOT_FIFTEEN * (unit_x * unit_x - unit_y * unit_y),
        ],
        axis=1,
    )
    return (harmonics, envelope, bessel)


def couple(edge_tensor, env_flat, mix_weight):
    chan_count = mix_weight.shape[1]
    own_tensor = edge_tensor.reshape(-1, 9, chan_count)
    env_tensor = env_flat.reshape(-1, 9, chan_count)
    paired = own_tensor * env_tensor
    scalars = jnp.concatenate(
        [paired[:, 0], jnp.sum(paired[:, 1:4], axis=1), jnp.sum(paired[:, 4:9], axis=1)], axis=1
    )
    coupled = own_tensor * env_tensor[:, 0:1] + own_tensor[:, 0:1] * env_tensor
    order_zero = jnp.einsum("emc,cd->emd", coupled[:, 0:1], mix_weight[0], precision=HIGHEST)
    order_one = jnp.einsum("emc,cd->emd", coupled[:, 1:4], mix_weight[1], precision=HIGHEST)
    order_two = jnp.einsum("emc,cd->emd", coupled[:, 4:9], mix_weight[2], precision=HIGHEST)
    updated = jnp.concatenate([order_zero, order_one, order_two], axis=1)
    return (scalars, updated.reshape(-1, 9 * chan_count))


def front(bessel, envelope, embed_in, head_local, kinds_hot):
    features = jnp.concatenate([kinds_hot, bessel], axis=1)
    return envelope[:, None] * matmul(jax.nn.silu(matmul(features, embed_in)), head_local)


def contribute(latent_full, harmonics, envelope, env_local, centre_hot):
    weight = matmul(latent_full, env_local)
    contribution = (
        (ENV_SCALE * envelope)[:, None, None] * harmonics[:, :, None] * weight[:, None, :]
    )
    flat_terms = contribution.reshape(weight.shape[0], -1)
    return (weight, matmul(centre_hot.T, flat_terms))


def tensor_step(tensor_full, env_window, weight, harmonics, mix_weight, centre_hot, is_first):
    start_tensor = (harmonics[:, :, None] * weight[:, None, :]).reshape(weight.shape[0], -1)
    edge_tensor = jnp.where(is_first, start_tensor, tensor_full)
    env_flat = matmul(centre_hot, env_window)
    return couple(edge_tensor, env_flat, mix_weight)


def perceptron(latent_full, scalars, in_local, out_local):
    hidden = jax.nn.silu(matmul(jnp.concatenate([latent_full, scalars], axis=1), in_local))
    return matmul(hidden, out_local)


def readout(latent_full, envelope, head_local, read_half):
    return envelope * matmul(jax.nn.silu(matmul(latent_full, head_local)), read_half)


def per_device(
    edge_vectors,
    edge_species,
    centres,
    edge_mask,
    structures,
    energy_cot,
    embed_in,
    section_head,
    env_weight,
    mix_weight,
    w_in,
    w_out,
    read_weight,
):
    section_index = lax.axis_index("section")
    core_index = lax.axis_index("mp")
    edge_index = lax.axis_index("edge")
    is_first = section_index == 0
    last_flag = (section_index == 1).astype(jnp.float32)
    batch_count = edge_vectors.shape[0]
    shard_width = w_out.shape[1]
    tensor_cols = 9 * env_weight.shape[2]
    tensor_half = tensor_cols // 2
    atoms_dev = ATOM_DEV
    head_local = section_head[0]
    env_local = env_weight[0]
    in_local = w_in[0]
    out_local = w_out[0]
    read_half = lax.dynamic_slice_in_dim(read_weight, core_index * shard_width, shard_width, 0)
    core_lead = (core_index == 0).astype(jnp.float32)
    edge_count = edge_vectors.shape[2]
    centre_slots = jnp.arange(3 * atoms_dev)
    labels = jnp.arange(STRUCTS)
    species_range = jnp.arange(NSPEC)
    batch_range = jnp.arange(batch_count)

    def reduce_rims(pieces):
        widened = extended(pieces, (("edge", 0),), atoms_dev)
        return (
            widened[:atoms_dev] + widened[2 * atoms_dev : 3 * atoms_dev] + widened[4 * atoms_dev :]
        )

    def window_rows(totals):
        return extended(totals, (("edge", 0),), atoms_dev)

    def collect(partial_rows):
        return lax.psum_scatter(partial_rows, "mp", scatter_dimension=1, tiled=True)

    def batch_data(batch_index):
        vectors = lax.dynamic_index_in_dim(edge_vectors, batch_index, 0, keepdims=False)
        kind_ids = lax.dynamic_index_in_dim(edge_species, batch_index, 0, keepdims=False)
        owners = lax.dynamic_index_in_dim(centres, batch_index, 0, keepdims=False)
        edge_live = lax.dynamic_index_in_dim(edge_mask, batch_index, 0, keepdims=False).astype(
            jnp.float32
        )
        groups = lax.dynamic_index_in_dim(structures, batch_index, 0, keepdims=False)
        kinds_hot = jnp.concatenate(
            [
                kind_ids[0][:, None] == species_range[None, :],
                kind_ids[1][:, None] == species_range[None, :],
            ],
            axis=1,
        ).astype(jnp.float32)
        local_slot = owners - (edge_index - 1) * atoms_dev
        centre_hot = (local_slot[:, None] == centre_slots[None, :]).astype(jnp.float32)
        group_hot = (groups[:, None] == labels[None, :]).astype(jnp.float32)
        return (vectors, edge_live, kinds_hot, centre_hot, group_hot)

    recv_latent = jnp.zeros((edge_count, shard_width), jnp.float32)
    recv_tensor = jnp.zeros((edge_count, tensor_half), jnp.float32)
    energies = jnp.zeros((batch_count, STRUCTS), jnp.float32)
    kept_state = []
    for step_index in range(batch_count + 1):
        batch_raw = step_index - section_index
        batch_index = jnp.clip(batch_raw, 0, batch_count - 1)
        is_valid = ((batch_raw >= 0) & (batch_raw < batch_count)).astype(jnp.float32)
        vectors, edge_live, kinds_hot, centre_hot, group_hot = batch_data(batch_index)
        harmonics, envelope, bessel = geometry(vectors, edge_live)
        latent_half = lax.cond(
            is_first,
            lambda: front(bessel, envelope, embed_in, head_local, kinds_hot),
            lambda: recv_latent,
        )
        latent_full, tensor_full = (
            lax.all_gather(latent_half, "mp", axis=1, tiled=True),
            lax.all_gather(recv_tensor, "mp", axis=1, tiled=True),
        )
        weight, part_sums = contribute(latent_full, harmonics, envelope, env_local, centre_hot)
        env_window = window_rows(reduce_rims(part_sums))
        scalars, updated = tensor_step(
            tensor_full, env_window, weight, harmonics, mix_weight, centre_hot, is_first
        )
        branch_out = perceptron(latent_full, scalars, in_local, out_local)
        summed = lax.psum_scatter(branch_out, "mp", scatter_dimension=1, tiled=True)
        tensor_own = lax.dynamic_slice_in_dim(updated, core_index * tensor_half, tensor_half, 1)
        next_half = latent_half + summed
        recv_latent, recv_tensor = shifted((next_half, tensor_own), "section", 1)
        next_full = lax.all_gather(next_half, "mp", axis=1, tiled=True)
        edge_energy = readout(next_full, envelope, head_local, read_half)
        batch_slot = (batch_range == batch_index).astype(jnp.float32) * is_valid * last_flag
        energies = (
            energies
            + batch_slot[:, None] * jnp.dot(edge_energy, group_hot, precision=HIGHEST)[None, :]
        )
        kept_state.append((latent_full, tensor_full, env_window, next_full))
    kept_latent = jnp.stack([entry[0] for entry in kept_state])
    kept_tensor = jnp.stack([entry[1] for entry in kept_state])
    kept_window = jnp.stack([entry[2] for entry in kept_state])
    kept_next = jnp.stack([entry[3] for entry in kept_state])
    grad_head = jnp.zeros_like(head_local)
    grad_env = jnp.zeros_like(env_local)
    grad_in = jnp.zeros_like(in_local)
    grad_out = jnp.zeros_like(out_local)
    grad_mix = jnp.zeros_like(mix_weight)
    grad_embed = jnp.zeros_like(embed_in)
    grad_read = jnp.zeros_like(read_half)
    forces = jnp.zeros((batch_count, 3, edge_count), jnp.float32)
    recv_grad = jnp.zeros((edge_count, shard_width), jnp.float32)
    recv_tgrad = jnp.zeros((edge_count, tensor_half), jnp.float32)
    for step_index in range(batch_count + 1):
        batch_raw = step_index - 1 + section_index
        batch_index = jnp.clip(batch_raw, 0, batch_count - 1)
        is_valid = ((batch_raw >= 0) & (batch_raw < batch_count)).astype(jnp.float32)
        saved_index = jnp.clip(batch_raw + section_index, 0, batch_count)
        latent_full = lax.dynamic_index_in_dim(kept_latent, saved_index, 0, keepdims=False)
        tensor_full = lax.dynamic_index_in_dim(kept_tensor, saved_index, 0, keepdims=False)
        env_window = lax.dynamic_index_in_dim(kept_window, saved_index, 0, keepdims=False)
        next_full = lax.dynamic_index_in_dim(kept_next, saved_index, 0, keepdims=False)
        vectors, edge_live, kinds_hot, centre_hot, group_hot = batch_data(batch_index)
        (harmonics, envelope, bessel), geometry_pull = jax.vjp(
            partial(geometry, edge_live=edge_live), vectors
        )
        batch_cot = lax.dynamic_index_in_dim(energy_cot, batch_index, 0, keepdims=False)
        energy_rows = jnp.dot(group_hot, batch_cot, precision=HIGHEST) * (is_valid * last_flag)
        _, read_pull = jax.vjp(readout, next_full, envelope, head_local, read_half)
        d_next_read, d_env_read, g_head_read, g_read = read_pull(energy_rows)
        d_next_half = jnp.where(is_first, recv_grad, collect(d_next_read))
        d_out_full, d_updated = (
            lax.all_gather(d_next_half, "mp", axis=1, tiled=True),
            lax.all_gather(recv_tgrad, "mp", axis=1, tiled=True),
        )
        (weight, part_sums), contribute_pull = jax.vjp(
            partial(contribute, centre_hot=centre_hot), latent_full, harmonics, envelope, env_local
        )
        (scalars, updated), tensor_pull = jax.vjp(
            partial(tensor_step, centre_hot=centre_hot, is_first=is_first),
            tensor_full,
            env_window,
            weight,
            harmonics,
            mix_weight,
        )
        _, perceptron_pull = jax.vjp(perceptron, latent_full, scalars, in_local, out_local)
        d_latent_mlp, d_scalar_part, g_in, g_out = perceptron_pull(d_out_full)
        d_scalars = lax.psum(d_scalar_part, "mp")
        d_tensor, d_window, d_weight, d_harm_tensor, g_mix = tensor_pull((d_scalars, d_updated))
        d_parts = window_rows(reduce_rims(d_window))
        d_latent_env, d_harm_env, d_envelope_env, g_env = contribute_pull((d_weight, d_parts))
        d_latent_own = (
            collect(d_latent_mlp)
            + lax.dynamic_slice_in_dim(d_latent_env, core_index * shard_width, shard_width, 1)
            + d_next_half
        )
        d_tensor_own = lax.dynamic_slice_in_dim(d_tensor, core_index * tensor_half, tensor_half, 1)
        recv_grad, recv_tgrad = shifted((d_latent_own, d_tensor_own), "section", -1)

        def front_pull(cotangent):
            _, pull_back = jax.vjp(
                partial(front, kinds_hot=kinds_hot), bessel, envelope, embed_in, head_local
            )
            return pull_back(cotangent)

        def front_none(cotangent):
            return (
                jnp.zeros_like(bessel),
                jnp.zeros_like(envelope),
                jnp.zeros_like(embed_in),
                jnp.zeros_like(head_local),
            )

        d_bessel, d_envelope_front, g_embed, g_head_front = lax.cond(
            is_first, front_pull, front_none, d_latent_own
        )
        d_harmonics = core_lead * (d_harm_tensor + d_harm_env)
        d_envelope = core_lead * d_envelope_env + d_env_read + d_envelope_front
        d_vectors = geometry_pull((d_harmonics, d_envelope, d_bessel))[0]
        batch_slot = (batch_range == batch_index).astype(jnp.float32) * is_valid
        forces = forces + batch_slot[:, None, None] * d_vectors[None]
        grad_head = grad_head + is_valid * (g_head_read + g_head_front)
        grad_env = grad_env + is_valid * g_env
        grad_in = grad_in + is_valid * g_in
        grad_out = grad_out + is_valid * g_out
        grad_mix = grad_mix + is_valid * g_mix
        grad_embed = grad_embed + is_valid * g_embed
        grad_read = grad_read + is_valid * g_read
    grad_head, grad_env, grad_in, grad_out = lax.psum(
        (grad_head, grad_env, grad_in, grad_out), "edge"
    )
    read_full = lax.dynamic_update_slice_in_dim(
        jnp.zeros_like(read_weight), grad_read, core_index * shard_width, 0
    )
    energies, grad_embed, grad_mix, read_full = lax.psum(
        (energies, grad_embed, core_lead * grad_mix, read_full), ("section", "edge", "mp")
    )
    forces = lax.psum(forces, ("section", "mp"))
    return (
        energies,
        -forces,
        grad_embed,
        grad_head[None],
        grad_env[None],
        grad_mix,
        grad_in[None],
        grad_out[None],
        read_full,
    )


def solution(mesh):
    placed = (
        P(None, None, "edge"),
        P(None, None, "edge"),
        P(None, "edge"),
        P(None, "edge"),
        P(None, "edge"),
        P(),
        P(),
        P("section", None, "mp"),
        P("section", None, None),
        P(),
        P("section", None, "mp"),
        P("section", "mp", None),
        P(),
    )
    return jax.shard_map(
        per_device,
        mesh=mesh,
        in_specs=placed,
        out_specs=(
            P(),
            P(None, None, "edge"),
            P(),
            P("section", None, "mp"),
            P("section", None, None),
            P(),
            P("section", None, "mp"),
            P("section", "mp", None),
            P(),
        ),
        check_vma=False,
    )
```

profile of v0, /device:TPU:0, one launch (start us, length us, event | category | flops | bytes accessed | tf_op | source)
XLA Modules:
  0.0 1490.6 jit_solution(14867634360148534815)
XLA Ops:
  46.6 11.3 collective-permute-done
  107.0 15.9 %collective-permute-done.4 = f32[384,512]{1,0:T(8,128)} collective-permute-done((f32[384,512]{1,0:T(8,128)}, f32[384,512]{1,0:T(8,128)}, u32[]{:S(2)}, u32[]{:S(2)}) %collective-permute-start.4) | collective-permute-done | bytes 786464 | tf_op jit(solution)/shard_map/ppermute | solution.py:38
  159.9 11.7 collective-permute-done.6
  204.9 11.6 reduce-scatter.15.cloned.1.call-done
  223.6 16.6 %collective-permute-done.10 = f32[384,512]{1,0:T(8,128)} collective-permute-done((f32[384,512]{1,0:T(8,128)}, f32[384,512]{1,0:T(8,128)}, u32[]{:S(2)}, u32[]{:S(2)}) %collective-permute-start.10) | collective-permute-done | bytes 786464 | tf_op jit(solution)/shard_map/ppermute | solution.py:38
  276.0 11.7 collective-permute-done.12
  321.0 11.6 reduce-scatter.17.cloned.1.call-done
  339.7 16.5 %collective-permute-done.16 = f32[384,512]{1,0:T(8,128)} collective-permute-done((f32[384,512]{1,0:T(8,128)}, f32[384,512]{1,0:T(8,128)}, u32[]{:S(2)}, u32[]{:S(2)}) %collective-permute-start.16) | collective-permute-done | bytes 786464 | tf_op jit(solution)/shard_map/ppermute | solution.py:38
  382.8 11.7 collective-permute-done.18
  453.4 12.4 all-gather.19.cloned.1.call-done
  465.8 12.6 all-gather.23.cloned.1.call-done
  478.4 13.0 all-gather.27.cloned.1.call-done
  589.5 10.3 collective-permute-done.22
  632.5 14.7 collective-permute-done.27
  770.5 14.3 collective-permute-done.33
  879.5 17.6 %conditional.12 = (f32[384,8]{0,1:T(8,128)S(1)}, f32[384]{0:T(512)S(1)}, f32[16,1024]{1,0:T(8,128)S(1)}, f32[1024,512]{1,0:T(8,128)S(1)}) conditional(s32[]{:T(128)} %convert_element_type.208, () %tuple.97, (f32[384]{0:T(512)S(1)}, f32[384,512]{1,0:T(8,128)}, f32[1024,512]{1,0:T(8,128)S(1)}, f32[384]{0:T(512)S(1)}, f32[384,8]{0,1:T(8,128)S(1)}, ...), branch_computations={%region_38.39_spmd, %region_39.41_spmd} | conditional | flops 7443986944 | bytes 19916832 | solution.py:305
  923.8 17.7 %conditional.13 = (f32[384,8]{0,1:T(8,128)S(1)}, f32[384]{0:T(512)S(1)}, f32[16,1024]{1,0:T(8,128)S(1)}, f32[1024,512]{1,0:T(8,128)S(1)}) conditional(s32[]{:T(128)} %convert_element_type.208, () %tuple.99, (f32[384]{0:T(512)S(1)}, f32[384,512]{1,0:T(8,128)}, f32[1024,512]{1,0:T(8,128)S(1)}, f32[384]{0:T(512)S(1)}, f32[384,8]{0,1:T(8,128)S(1)}, ...), branch_computations={%region_56.57_spmd, %region_57.59_spmd} | conditional | flops 7443986944 | bytes 19916832 | solution.py:305
  983.3 10.8 collective-permute-done.39
  1027.1 20.6 %conditional.14 = (f32[384,8]{0,1:T(8,128)S(1)}, f32[384]{0:T(512)S(1)}, f32[16,1024]{1,0:T(8,128)}, f32[1024,512]{1,0:T(8,128)}) conditional(s32[]{:T(128)} %convert_element_type.208, () %tuple.101, (f32[384]{0:T(512)S(1)}, f32[384,512]{1,0:T(8,128)}, f32[1024,512]{1,0:T(8,128)}, f32[384]{0:T(512)S(1)}, f32[384,8]{0,1:T(8,128)S(1)}, ...), branch_computations={%region_74.75_spmd, %region_75.77_spmd} | conditional | flops 7443986944 | bytes 28305468 | solution.py:305
  1096.0 21.3 %conditional.15 = (f32[384,8]{0,1:T(8,128)}, f32[384]{0:T(512)}, f32[16,1024]{1,0:T(8,128)S(1)}, f32[1024,512]{1,0:T(8,128)}) conditional(s32[]{:T(128)} %convert_element_type.208, () %tuple.103, (f32[384]{0:T(512)}, f32[384,1024]{1,0:T(8,128)}, s32[]{:T(128)}, f32[384,512]{0,1:T(8,128)}, f32[384,512]{1,0:T(8,128)S(1)}, ...), branch_computations={%region_92.93_spmd, %region_93.95_spmd} | conditional | flops 7444380160 | bytes 33401520 | solution.py:305
  1139.0 41.9 %all-reduce.56 = (f32[3,16]{1,0:T(4,128)}, f32[3,64,64]{2,1,0:T(8,128)}, f32[1024]{0:T(1024)}) all-reduce(f32[3,16]{1,0:T(4,128)S(1)} %copy-done.323, f32[3,64,64]{2,1,0:T(8,128)S(1)} %add_multiply_fusion, f32[1024]{0:T(1024)S(1)} %add_dynamic-update-slice_fusion), channel_id=1, replica_groups=mesh['section'=2,'edge'=8,'mp'=2] {'section','edge','mp'}, use_global_device_ids=true, to_apply=%region_24.25 | all-reduce | flops 13360 | bytes 106880 | tf_op jit(solution)/shard_map/psum | solution.py:326
  1186.1 10.3 psum.96
  1197.0 38.4 %all-reduce.73.cloned.1.call-done = f32[16,1024]{1,0:T(8,128)} async-done(((f32[16,1024]{1,0:T(8,128)}), f32[16,1024]{1,0:T(8,128)}) %all-reduce.73.cloned.1.call-update) | async-done | bytes 65552 | tf_op jit(solution)/shard_map/psum | solution.py:326
  1235.3 238.9 %all-reduce.75.cloned.1.call-done = (f32[1,1024,512]{2,1,0:T(8,128)}, f32[1,1024,64]{1,2,0:T(8,128)}, f32[1,1216,512]{2,1,0:T(8,128)}, f32[1,512,1024]{2,1,0:T(8,128)}) async-done(((f32[1,1024,512]{2,1,0:T(8,128)}, f32[1,1024,64]{1,2,0:T(8,128)}, f32[1,1216,512]{2,1,0:T(8,128)}, f32[1,512,1024]{2,1,0:T(8,128)}), (f32[1,1024,512]{2,1,0:T(8,128)}, f32[1,1024,64]{1,2,0:T(8,128)}, f32[1,1216,512]{2,1,0:T(8,128)}, ...) | async-done | bytes 6946832 | tf_op jit(solution)/shard_map/psum | solution.py:320
  (1488 shorter events, 962.5 us)
Async XLA Ops:
  21.8 77.8 %reduce-scatter.13.cloned.1.call-start = ((), (), s32[]{:S(2)}) async-start(), calls=%async_computation.13 | async-start | bytes 2359296 | tf_op jit(solution)/shard_map/reduce_scatter | solution.py:218
  89.7 61.5 %all-gather.17.cloned.1.call-start = ((), (), s32[]{:S(2)}) async-start(), calls=%async_computation.15 | async-start | bytes 2359296 | tf_op jit(solution)/shard_map/all_gather | solution.py:209
  131.5 85.0 %reduce-scatter.15.cloned.1.call-start = ((), (), s32[]{:S(2)}) async-start(), calls=%async_computation.16 | async-start | bytes 2359296 | tf_op jit(solution)/shard_map/reduce_scatter | solution.py:218
  204.9 62.4 %all-gather.21.cloned.1.call-start = ((), (), s32[]{:S(2)}) async-start(), calls=%async_computation.18 | async-start | bytes 2359296 | tf_op jit(solution)/shard_map/all_gather | solution.py:209
  248.0 84.6 %reduce-scatter.17.cloned.1.call-start = ((), (), s32[]{:S(2)}) async-start(), calls=%async_computation.19 | async-start | bytes 2359296 | tf_op jit(solution)/shard_map/reduce_scatter | solution.py:218
  363.9 76.3 %reduce-scatter.19.cloned.1.call-start = ((), (), s32[]{:S(2)}) async-start(), calls=%async_computation.22 | async-start | bytes 2359296 | tf_op jit(solution)/shard_map/reduce_scatter | solution.py:218
  431.9 59.5 %all-gather.27.cloned.1.call-start = ((), (), s32[]{:S(2)}) async-start(), calls=%async_computation.23 | async-start | bytes 2359296 | tf_op jit(solution)/shard_map/all_gather | solution.py:222
  442.7 80.1 %reduce-scatter.21.cloned.1.call-start = ((), (), s32[]{:S(2)}) async-start(), calls=%async_computation.24 | async-start | bytes 2359296 | tf_op jit(solution)/shard_map/reduce_scatter | solution.py:171
  523.8 55.5 %all-reduce.65.cloned.1.call-start = ((), (), s32[]{:S(2)}) async-start(), calls=%async_computation.26 | async-start | bytes 589824 | tf_op jit(solution)/shard_map/psum | solution.py:279
  553.6 68.9 %reduce-scatter.23.cloned.1.call-start = ((), (), s32[]{:S(2)}) async-start(), calls=%async_computation.27 | async-start | bytes 2359296 | tf_op jit(solution)/shard_map/reduce_scatter | solution.py:171
  561.2 71.2 %reduce-scatter.25.cloned.1.call-start = ((), (), s32[]{:S(2)}) async-start(), calls=%async_computation.28 | async-start | bytes 2359296 | tf_op jit(solution)/shard_map/reduce_scatter | solution.py:171
  579.2 86.7 %all-gather.31.cloned.1.call-start = ((), (), s32[]{:S(2)}) async-start(), calls=%async_computation.29 | async-start | bytes 2359296 | tf_op jit(solution)/shard_map/all_gather | solution.py:263
  649.4 68.6 %all-reduce.67.cloned.1.call-start = ((), (), s32[]{:S(2)}) async-start(), calls=%async_computation.30 | async-start | bytes 589824 | tf_op jit(solution)/shard_map/psum | solution.py:279
  677.3 83.2 %reduce-scatter.27.cloned.1.call-start = ((), (), s32[]{:S(2)}) async-start(), calls=%async_computation.31 | async-start | bytes 2359296 | tf_op jit(solution)/shard_map/reduce_scatter | solution.py:171
  685.4 85.1 %reduce-scatter.29.cloned.1.call-start = ((), (), s32[]{:S(2)}) async-start(), calls=%async_computation.32 | async-start | bytes 2359296 | tf_op jit(solution)/shard_map/reduce_scatter | solution.py:171
  717.9 85.7 %all-gather.33.cloned.1.call-start = ((), (), s32[]{:S(2)}) async-start(), calls=%async_computation.33 | async-start | bytes 2359296 | tf_op jit(solution)/shard_map/all_gather | solution.py:263
  787.0 124.0 %all-reduce.69.cloned.1.call-start = ((), (), s32[]{:S(2)}) async-start(), calls=%async_computation.34 | async-start | bytes 589824 | tf_op jit(solution)/shard_map/psum | solution.py:279
  815.0 151.8 %reduce-scatter.31.cloned.1.call-start = ((), (), s32[]{:S(2)}) async-start(), calls=%async_computation.35 | async-start | bytes 2359296 | tf_op jit(solution)/shard_map/reduce_scatter | solution.py:171
  824.8 158.5 %reduce-scatter.33.cloned.1.call-start = ((), (), s32[]{:S(2)}) async-start(), calls=%async_computation.36 | async-start | bytes 2359296 | tf_op jit(solution)/shard_map/reduce_scatter | solution.py:171
  865.8 147.3 %all-gather.35.cloned.1.call-start = ((), (), s32[]{:S(2)}) async-start(), calls=%async_computation.37 | async-start | bytes 2359296 | tf_op jit(solution)/shard_map/all_gather | solution.py:263
  996.3 54.1 %all-reduce.71.cloned.1.call-start = ((), (), s32[]{:S(2)}) async-start(), calls=%async_computation.38 | async-start | bytes 589824 | tf_op jit(solution)/shard_map/psum | solution.py:279
  1025.2 70.8 %reduce-scatter.35.cloned.1.call-start = ((), (), s32[]{:S(2)}) async-start(), calls=%async_computation.39 | async-start | bytes 2359296 | tf_op jit(solution)/shard_map/reduce_scatter | solution.py:171
  1050.3 185.0 %all-reduce.73.cloned.1.call-start = ((), (), s32[]{:S(2)}) async-start(), calls=%async_computation.40 | async-start | bytes 131072 | tf_op jit(solution)/shard_map/psum | solution.py:326
  1118.8 355.3 %all-reduce.75.cloned.1.call-start = ((), (), s32[]{:S(2)}) async-start(), calls=%async_computation.41 | async-start | bytes 13893632 | tf_op jit(solution)/shard_map/psum | solution.py:320
  (481 other events, 6219.2 us)
Sparse Core Ops, SparseCore 0:
  21.9 11.5 all-gather.12
  131.6 9.8 all-gather.16
  204.9 11.5 reduce-scatter.14
  248.1 9.7 all-gather.20
  321.1 11.5 reduce-scatter.16
  429.8 10.4 reduce-scatter.18
  442.4 10.9 all-gather.14
  454.8 10.9 all-gather.18
  467.4 10.9 all-gather.22
  480.3 10.9 all-gather.26
  505.0 10.2 reduce-scatter.20
  523.9 12.0 all-gather.28
  553.7 20.3 all-reduce.64
  576.9 10.2 reduce-scatter.22
  589.2 10.2 reduce-scatter.24
  649.5 9.8 all-gather.30
  677.5 18.2 all-reduce.66
  698.6 10.2 reduce-scatter.26
  787.1 9.8 all-gather.32
  815.1 18.2 all-reduce.68
  835.6 10.2 reduce-scatter.30
  1025.3 17.5 all-reduce.70
  1119.0 116.3 all-reduce.72
  1240.4 233.7 all-reduce.74
  (6 shorter events, 54.5 us)
where the time goes:
time: 1500 us; the launch traced here: 1490 us
  waiting for transfers between devices  607 us (40%)
  matrix products  423 us (28%)
  local copies, waits for them, and re-layouts  126 us (8%)
  starting transfers between devices  126 us (8%)
  other arithmetic  114 us (8%)
  blocking collectives  71.1 us (5%)
  between operations  21.5 us (1%)
    dot_general x124, matrix products, matmul(): jnp.dot(left, right, precision=HIGHEST, preferred_element_type=jnp.float32)  377 us
    psum x1, waiting for transfers between devices, per_device(): lax.psum((grad_head, grad_env, grad_in, grad_out), 'edge')  239 us
    ppermute x16, waiting for transfers between devices, extended(): lax.ppermute(lax.slice_in_dim(block, block.shape[dim] - width, None, axis...  117 us
    ppermute x12, waiting for transfers between devices, shifted(): lax.ppermute(value, axis, [(source, source + steps) for source in range(f...  106 us
    ppermute x16, starting transfers between devices, extended(): lax.ppermute(lax.slice_in_dim(block, block.shape[dim] - width, None, axis...  73.8 us
    unnamed x857, local copies, waits for them, and re-layouts  47.9 us
    all_gather x4, waiting for transfers between devices, per_device(): next_full = lax.all_gather(next_half, 'mp', axis=1, tiled=True)  43 us
    psum x1, blocking collectives, per_device(): lax.psum((energies, grad_embed, core_lead * grad_mix, read_full), ('secti...  41.9 us
  transfers between devices with their start and end apart: 74, of which 41 were waited for; matrix products, arithmetic and copies ran while one was open for 29% of the time, Pallas kernels for 0%

commit v1 on v0

--- a/solution.py
+++ b/solution.py
@@ -3,6 +3,8 @@
 import jax
 import jax.numpy as jnp
 from jax import lax
+from jax.experimental import pallas as pl
+from jax.experimental.pallas import tpu as pltpu
 from jax.sharding import PartitionSpec as P
 
 NBES = 8
@@ -121,7 +123,7 @@
     return envelope * matmul(jax.nn.silu(matmul(latent_full, head_local)), read_half)
 
 
-def per_device(
+def general_device(
     edge_vectors,
     edge_species,
     centres,
@@ -340,6 +342,845 @@
     )
 
 
+CHUNKS = (160, 160, 160)
+LANES = 128
+F32 = jnp.float32
+BF16 = jnp.bfloat16
+BESSEL_SCALE = (2.0 / CUTOFF) ** 0.5
+ANGLE = 3.141592653589793 / CUTOFF
+
+
+def dot_nn(left, right):
+    return jnp.dot(left, right, preferred_element_type=F32)
+
+
+def dot_nt(left, right):
+    return lax.dot_general(left, right, (((1,), (1,)), ((), ())), preferred_element_type=F32)
+
+
+def dot_tn(left, right):
+    return lax.dot_general(left, right, (((0,), (0,)), ((), ())), preferred_element_type=F32)
+
+
+def split_two(value):
+    high = value.astype(BF16)
+    return high, (value - high.astype(F32)).astype(BF16)
+
+
+def split_three(value):
+    high = value.astype(BF16)
+    rest = value - high.astype(F32)
+    middle = rest.astype(BF16)
+    return high, middle, (rest - middle.astype(F32)).astype(BF16)
+
+
+def six_pass(left, right):
+    rows = left.shape[0]
+    high, middle, low = split_three(left)
+    three = dot_nn(jnp.concatenate([high, middle, low], axis=0), right[0])
+    two = dot_nn(jnp.concatenate([high, middle], axis=0), right[1])
+    small = three[2 * rows :] + two[rows:] + dot_nn(high, right[2])
+    return three[:rows] + (three[rows : 2 * rows] + two[:rows] + small)
+
+
+def three_pass(dot, left, right):
+    rows = left.shape[0]
+    high, low = split_two(left)
+    both = dot(jnp.concatenate([high, low], axis=0), right[0])
+    return both[:rows] + both[rows:] + dot(high, right[1])
+
+
+def three_pass_tn(left, right):
+    left_high, left_low = split_two(left)
+    right_high, right_low = split_two(right)
+    return dot_tn(
+        jnp.concatenate([left_high, left_low, left_high], axis=0),
+        jnp.concatenate([right_high, right_high, right_low], axis=0),
+    )
+
+
+def sigmoid(value):
+    return 1.0 / (1.0 + jnp.exp(-value))
+
+
+def order_of(component):
+    return 0 if component == 0 else (1 if component < 4 else 2)
+
+
+def same_sum(same, parts):
+    high, middle, low = split_three(jnp.concatenate(parts, axis=1))
+    summed = dot_nn(same, high) + (dot_nn(same, middle) + dot_nn(same, low))
+    return [summed[:, LANES * m : LANES * (m + 1)] for m in range(len(parts))]
+
+
+def place_columns(columns, first, width=LANES):
+    lane = lax.broadcasted_iota(jnp.int32, (columns[0].shape[0], width), 1)
+    out = jnp.zeros((columns[0].shape[0], width), F32)
+    for i, column in enumerate(columns):
+        out = jnp.where(lane == first + i, column, out)
+    return out
+
+
+def waves(length):
+    turn = length * ANGLE - 1.5707963267948966
+    square = turn * turn
+    even, odd, term_even, term_odd = 1.0, 1.0, 1.0, 1.0
+    coefficients_even, coefficients_odd = [], []
+    for n in range(1, 9):
+        term_even = -term_even / ((2 * n - 1) * (2 * n))
+        term_odd = -term_odd / ((2 * n) * (2 * n + 1))
+        coefficients_even.append(term_even)
+        coefficients_odd.append(term_odd)
+    even = jnp.full_like(turn, coefficients_even[-1])
+    odd = jnp.full_like(turn, coefficients_odd[-1])
+    for n in range(6, -1, -1):
+        even = even * square + coefficients_even[n]
+        odd = odd * square + coefficients_odd[n]
+    sines = {1: even * square + 1.0}
+    cosines = {1: -turn * (odd * square + 1.0)}
+    for total, left, right in ((2, 1, 1), (3, 2, 1), (4, 2, 2), (5, 4, 1), (6, 4, 2), (7, 4, 3), (8, 4, 4)):
+        sines[total] = sines[left] * cosines[right] + cosines[left] * sines[right]
+        cosines[total] = cosines[left] * cosines[right] - sines[left] * sines[right]
+    return [sines[k] for k in range(1, 9)], [cosines[k] for k in range(1, 9)]
+
+
+def edge_values(edges, key_row, first, rows, full):
+    block = edges[first : first + rows, :]
+    vector = [block[:, i : i + 1] for i in range(3)]
+    live = block[:, 6:7]
+    squares = vector[0] * vector[0] + vector[1] * vector[1] + vector[2] * vector[2]
+    length = jnp.sqrt(jnp.maximum(squares, 0.25))
+    ux, uy, uz = (v / length for v in vector)
+    ratio = jnp.minimum(length / CUTOFF, 1.0)
+    second = ratio * ratio
+    sixth = second * second * second
+    envelope = (1.0 - 28.0 * sixth + 48.0 * (sixth * ratio) - 21.0 * (sixth * second)) * live
+    harmonics = [
+        jnp.ones_like(ux),
+        ROOT_THREE * ux,
+        ROOT_THREE * uy,
+        ROOT_THREE * uz,
+        ROOT_FIFTEEN * ux * uy,
+        ROOT_FIFTEEN * uy * uz,
+        0.5 * ROOT_FIVE * (3.0 * uz * uz - 1.0),
+        ROOT_FIFTEEN * ux * uz,
+        0.5 * ROOT_FIFTEEN * (ux * ux - uy * uy),
+    ]
+    same = jnp.where(block[:, 5:6] == key_row, 1.0, 0.0).astype(BF16)
+    g = dict(
+        env=envelope, harm=harmonics, same=same, squares=squares, length=length, ratio=ratio,
+        unit=(ux, uy, uz), live=live, group=block[:, 7:8],
+    )
+    if full:
+        sines, g["cosines"] = waves(length)
+        g["bessel"] = [BESSEL_SCALE * value / length for value in sines]
+        lane = lax.broadcasted_iota(jnp.int32, (rows, 16), 1).astype(F32)
+        kinds = jnp.where(
+            lane < NSPEC,
+            jnp.where(block[:, 3:4] == lane, live, 0.0),
+            jnp.where(block[:, 4:5] + NSPEC == lane, live, 0.0),
+        )
+        g["feat"] = kinds + place_columns(g["bessel"], 2 * NSPEC, 16)
+    return g
+
+
+def vector_pull(g, d_bessel, d_harm, d_envelope):
+    ux, uy, uz = g["unit"]
+    length, ratio = g["length"], g["ratio"]
+    dx = ROOT_THREE * d_harm[1] + ROOT_FIFTEEN * (uy * d_harm[4] + uz * d_harm[7] + ux * d_harm[8])
+    dy = ROOT_THREE * d_harm[2] + ROOT_FIFTEEN * (ux * d_harm[4] + uz * d_harm[5] - uy * d_harm[8])
+    dz = (
+        ROOT_THREE * d_harm[3]
+        + ROOT_FIFTEEN * (uy * d_harm[5] + ux * d_harm[7])
+        + (3.0 * ROOT_FIVE) * uz * d_harm[6]
+    )
+    left = 1.0 - ratio
+    fourth = (ratio * ratio) * (ratio * ratio)
+    d_length = (-168.0 / CUTOFF) * (fourth * ratio) * (left * left) * g["live"] * d_envelope
+    d_length = d_length - (dx * ux + dy * uy + dz * uz) / length
+    for k in range(NBES):
+        slope = (BESSEL_SCALE * ANGLE * (k + 1)) * g["cosines"][k] - g["bessel"][k]
+        d_length = d_length + d_bessel[k] * (slope / length)
+    bound = jnp.where(g["squares"] > 0.25, 1.0, jnp.where(g["squares"] == 0.25, 0.5, 0.0))
+    d_length = d_length * bound
+    return [d / length + d_length * u for d, u in ((dx, ux), (dy, uy), (dz, uz))]
+
+
+def env_terms(g, weight):
+    scaled = ENV_SCALE * g["env"] * weight
+    return same_sum(g["same"], [y * scaled for y in g["harm"]])
+
+
+def pack_scalars(tensor, env):
+    sums = [tensor[0] * env[0], tensor[1] * env[1], tensor[4] * env[4]]
+    for m in (2, 3):
+        sums[1] = sums[1] + tensor[m] * env[m]
+    for m in (5, 6, 7, 8):
+        sums[2] = sums[2] + tensor[m] * env[m]
+    return jnp.concatenate([sums[0] + pltpu.roll(sums[1], 64, 1), sums[2]], axis=1)
+
+
+def unpack_scalars(packed):
+    first = packed[:, :LANES]
+    return [first, pltpu.roll(first, 64, 1), packed[:, LANES:]]
+
+
+def swap_order(lead, left, right):
+    return jnp.where(lead, left, right), jnp.where(lead, right, left)
+
+
+def env_pull(g, weight, d_env):
+    d_terms = same_sum(g["same"], d_env)
+    d_weight, d_harm, inner = None, [], None
+    for m in range(9):
+        part = g["harm"][m] * d_terms[m]
+        d_weight = part if m == 0 else d_weight + part
+        d_harm.append(jnp.sum(weight * d_terms[m], axis=1, keepdims=True))
+        step = g["harm"][m] * d_harm[m]
+        inner = step if m == 0 else inner + step
+    scale = ENV_SCALE * g["env"]
+    return scale * d_weight, [scale * d for d in d_harm], ENV_SCALE * inner
+
+
+class Fetched:
+    def __init__(self, source, buffer, semaphore):
+        rows = source.shape[0]
+        self.buffer, self.shape = buffer, buffer.shape
+        target = buffer if rows == buffer.shape[0] else buffer.at[pl.ds(0, rows)]
+        self.copy = pltpu.make_async_copy(source, target, semaphore)
+        self.copy.start()
+        self.arrived, self.pieces = False, {}
+        if rows < buffer.shape[0]:
+            buffer[rows:, :] = jnp.zeros((buffer.shape[0] - rows, buffer.shape[1]), F32)
+
+    def __getitem__(self, where):
+        if not self.arrived:
+            self.copy.wait()
+            self.arrived = True
+        return self.buffer[where]
+
+    def split(self, parts):
+        if parts not in self.pieces:
+            value = self[...]
+            self.pieces[parts] = split_three(value) if parts == 3 else split_two(value)
+        return self.pieces[parts]
+
+
+class Stored:
+    def __init__(self, target, buffer, semaphore):
+        self.target, self.buffer, self.semaphore = target, buffer, semaphore
+        self.shape, self.copy = buffer.shape, None
+
+    def __setitem__(self, where, value):
+        self.buffer[where] = value
+        if where is Ellipsis:
+            self.send()
+
+    def __getitem__(self, where):
+        return self.buffer[where]
+
+    def send(self):
+        self.copy = pltpu.make_async_copy(self.buffer, self.target, self.semaphore)
+        self.copy.start()
+
+
+def forward_pair(value, own, other):
+    return [six_pass(value, own.split(3)), six_pass(value, other.split(3))]
+
+
+def backward_pair(value, own, other, parts):
+    return [three_pass(dot_nt, value, own.split(parts)), three_pass(dot_nt, value, other.split(parts))]
+
+
+def first_forward(
+    first, edges, key_row, lead_flag, embed,
+    head_o, head_x, env_w, in_o, in_x, out_o, out_x,
+    sent, soft_out, layer_in, slope_out, hidden,
+):
+    rows = sent.shape[0]
+    lead = lead_flag[0:1, 0:1] > 0.5
+    g = edge_values(edges, key_row[...], first, rows, True)
+    pre = six_pass(g["feat"], split_three(embed[...]))
+    soft = pre * sigmoid(pre)
+    soft_out[...] = soft
+    own, other = forward_pair(soft, head_o, head_x)
+    latent = g["env"] * jnp.concatenate(swap_order(lead, own, other), axis=1)
+    weight = six_pass(latent, env_w.split(3))
+    env = env_terms(g, weight)
+    scalars = pack_scalars([y * weight for y in g["harm"]], env)
+    full = jnp.concatenate([latent, scalars], axis=1)
+    layer_in[...] = full
+    pre = jnp.concatenate(forward_pair(full, in_o, in_x), axis=1)
+    gate = sigmoid(pre)
+    slope_out[...] = gate * (1.0 + pre * (1.0 - gate))
+    hid = pre * gate
+    hidden[...] = hid
+    half = hid.shape[1] // 2
+    width = latent.shape[1]
+    sent[:, :width] = (
+        latent + six_pass(hid[:, :half], out_o.split(3)) + six_pass(hid[:, half:], out_x.split(3))
+    )
+    sent[:, width:] = weight
+    sent.send()
+
+
+def second_both(
+    first, edges, key_row, mix, read, cot_row,
+    arrived, env_w, in_o, in_x, out_o, out_x, head_o, head_x, env_wt,
+    back, layer_in, d_pre_hidden, hidden, d_latent_out, latent_out, d_pre_read, d_weight_out,
+    read_grad, mix_grad, energy_out,
+):
+    rows = back.shape[0]
+    width = arrived.shape[1] - LANES
+    half = width // 2
+    g = edge_values(edges, key_row[...], first, rows, False)
+    lane = lax.broadcasted_iota(jnp.int32, (rows, LANES), 1).astype(F32)
+    group_hot = jnp.where(g["group"] == lane, g["live"], 0.0)
+    cot = jnp.sum(group_hot * cot_row[...], axis=1, keepdims=True)
+    mixes = [split_three(mix[i]) for i in range(3)]
+    latent = arrived[:, :width]
+    weight_first = arrived[:, width:]
+    env_first = env_terms(g, weight_first)
+    start = [y * weight_first for y in g["harm"]]
+    coupled = [start[m] * env_first[0] + start[0] * env_first[m] for m in range(9)]
+    members = ((0,), (1, 2, 3), (4, 5, 6, 7, 8))
+    tensor = []
+    for order in range(3):
+        mixed = six_pass(jnp.concatenate([coupled[m] for m in members[order]], axis=0), mixes[order])
+        tensor += [mixed[rows * i : rows * (i + 1)] for i in range(len(members[order]))]
+    weight = six_pass(latent, env_w.split(3))
+    env = env_terms(g, weight)
+    full = jnp.concatenate([latent, pack_scalars(tensor, env)], axis=1)
+    layer_in[...] = full
+    pre = jnp.concatenate(forward_pair(full, in_o, in_x), axis=1)
+    gate = sigmoid(pre)
+    slope = gate * (1.0 + pre * (1.0 - gate))
+    hid = pre * gate
+    hidden[...] = hid
+    latent_next = (
+        latent + six_pass(hid[:, :half], out_o.split(3)) + six_pass(hid[:, half:], out_x.split(3))
+    )
+    latent_out[...] = latent_next
+    pre_read = jnp.concatenate(forward_pair(latent_next, head_o, head_x), axis=1)
+    gate = sigmoid(pre_read)
+    soft = pre_read * gate
+    line = read[...]
+    inner = jnp.sum(soft * line, axis=1, keepdims=True)
+    energy_out[...] = jnp.broadcast_to(
+        jnp.sum(group_hot * (g["env"] * inner), axis=0, keepdims=True), energy_out.shape
+    )
+    scaled_cot = cot * g["env"]
+    read_grad[...] = jnp.broadcast_to(
+        jnp.sum(scaled_cot * soft, axis=0, keepdims=True), read_grad.shape
+    )
+    d_envelope = cot * inner
+    d_read = scaled_cot * line * (gate * (1.0 + pre_read * (1.0 - gate)))
+    d_pre_read[...] = d_read
+    d_latent_out[...] = three_pass(dot_nt, d_read[:, :half], head_o.split(3)) + three_pass(
+        dot_nt, d_read[:, half:], head_x.split(3)
+    )
+    d_hid = jnp.concatenate(backward_pair(d_latent_out[...], out_o, out_x, 3), axis=1)
+    d_pre = d_hid * slope
+    d_pre_hidden[...] = d_pre
+    d_full = three_pass(dot_nt, d_pre[:, :half], in_o.split(3)) + three_pass(
+        dot_nt, d_pre[:, half:], in_x.split(3)
+    )
+    d_scalars = unpack_scalars(d_full[:, width:])
+    d_tensor = [d_scalars[order_of(m)] * env[m] for m in range(9)]
+    d_env = [d_scalars[order_of(m)] * tensor[m] for m in range(9)]
+    d_weight, d_harm, d_more = env_pull(g, weight, d_env)
+    d_envelope = d_envelope + d_more
+    d_weight_out[...] = d_weight
+    back[:, :width] = (
+        three_pass(dot_nn, d_weight_out[...], env_wt.split(2))
+        + d_latent_out[...]
+        + d_full[:, :width]
+    )
+    d_coupled = []
+    for order in range(3):
+        joined = jnp.concatenate([d_tensor[m] for m in members[order]], axis=0)
+        mix_grad[order] = three_pass_tn(
+            jnp.concatenate([coupled[m] for m in members[order]], axis=0), joined
+        )
+        mixed = three_pass(dot_nt, joined, mixes[order])
+        d_coupled += [mixed[rows * i : rows * (i + 1)] for i in range(len(members[order]))]
+    mix_grad.send()
+    d_env_first = [d_coupled[m] * start[0] for m in range(9)]
+    d_start = [d_coupled[m] * env_first[0] for m in range(9)]
+    for m in range(9):
+        d_env_first[0] = d_env_first[0] + d_coupled[m] * start[m]
+        d_start[0] = d_start[0] + d_coupled[m] * env_first[m]
+    d_first, d_harm_first, d_more = env_pull(g, weight_first, d_env_first)
+    for m in range(9):
+        d_first = d_first + g["harm"][m] * d_start[m]
+        d_harm[m] = (
+            d_harm[m]
+            + d_harm_first[m]
+            + jnp.sum(weight_first * d_start[m], axis=1, keepdims=True)
+        )
+    d_envelope = d_envelope + d_more
+    back[:, width:] = d_first + place_columns(d_harm + [d_envelope], 64)
+    back.send()
+
+
+def first_backward(
+    first, edges, key_row, lead_flag, embed,
+    layer_in, env_w, arrived, out_o, out_x, slope_in, in_o, in_x, env_wt, head_o, head_x,
+    d_vector, d_head, d_pre_hidden, d_weight_out, embed_grad,
+):
+    rows = arrived.shape[0]
+    width = arrived.shape[1] - LANES
+    half = width // 2
+    lead = lead_flag[0:1, 0:1] > 0.5
+    g = edge_values(edges, key_row[...], first, rows, True)
+    embed_pair = split_two(embed[...])
+    latent = layer_in[:, :width]
+    weight = three_pass(dot_nn, latent, env_w.split(2))
+    env = env_terms(g, weight)
+    extra = arrived[:, width:]
+    lane = lax.broadcasted_iota(jnp.int32, extra.shape, 1)
+    d_weight = jnp.where(lane < 64, extra, 0.0)
+    d_harm = [extra[:, 64 + m : 65 + m] for m in range(9)]
+    d_envelope = extra[:, 73:74]
+    d_hid = jnp.concatenate(backward_pair(arrived[:, :width], out_o, out_x, 2), axis=1)
+    d_pre = d_hid * slope_in[...]
+    d_pre_hidden[...] = d_pre
+    d_full = three_pass(dot_nt, d_pre[:, :half], in_o.split(2)) + three_pass(
+        dot_nt, d_pre[:, half:], in_x.split(2)
+    )
+    d_scalars = unpack_scalars(d_full[:, width:])
+    d_start = [d_scalars[order_of(m)] * env[m] for m in range(9)]
+    d_env = [d_scalars[order_of(m)] * (g["harm"][m] * weight) for m in range(9)]
+    d_more_weight, d_more_harm, d_more = env_pull(g, weight, d_env)
+    d_weight = d_weight + d_more_weight
+    d_envelope = d_envelope + d_more
+    for m in range(9):
+        d_weight = d_weight + g["harm"][m] * d_start[m]
+        d_harm[m] = (
+            d_harm[m] + d_more_harm[m] + jnp.sum(weight * d_start[m], axis=1, keepdims=True)
+        )
+    d_weight_out[...] = d_weight
+    d_latent = (
+        three_pass(dot_nn, d_weight_out[...], env_wt.split(2))
+        + arrived[:, :width]
+        + d_full[:, :width]
+    )
+    d_own, d_other = swap_order(lead, d_latent[:, :half], d_latent[:, half:])
+    d_head[:, :half] = g["env"] * d_own
+    d_head[:, half:] = g["env"] * d_other
+    d_head.send()
+    d_soft = three_pass(dot_nt, d_own, head_o.split(2)) + three_pass(dot_nt, d_other, head_x.split(2))
+    pre = three_pass(dot_nn, g["feat"], embed_pair)
+    gate = sigmoid(pre)
+    d_envelope = d_envelope + jnp.sum(pre * gate * d_soft, axis=1, keepdims=True)
+    d_pre = g["env"] * d_soft * (gate * (1.0 + pre * (1.0 - gate)))
+    d_feat = three_pass(dot_nt, d_pre, embed_pair)
+    embed_grad[...] = three_pass_tn(g["feat"], d_pre)
+    d_bessel = [d_feat[:, 2 * NSPEC + k : 2 * NSPEC + 1 + k] for k in range(NBES)]
+    d_vector[...] = place_columns(vector_pull(g, d_bessel, d_harm, d_envelope), 0)
+
+
+def outer_sum(split_left, chosen, *refs):
+    count = len(CHUNKS)
+    extra = len(refs) > 4 * count + 8
+    kinds = 3 if extra else 2
+    sources = [
+        [refs[(kinds * side + i) * count : (kinds * side + i + 1) * count] for i in range(kinds)]
+        for side in range(2)
+    ]
+    rest = refs[2 * kinds * count :]
+    outs = [Stored(rest[i], rest[kinds + i], rest[-1].at[i]) for i in range(kinds)]
+    buffers = rest[2 * kinds : 3 * kinds]
+    semaphores = rest[-2]
+
+    def copies(side):
+        for i in range(kinds):
+            start = 0
+            for k, source in enumerate(sources[side][i]):
+                rows, columns = source.shape[0], buffers[i].shape[1]
+                yield pltpu.make_async_copy(
+                    source.at[:, pl.ds(0, columns)],
+                    buffers[i].at[pl.ds(start, rows)],
+                    semaphores.at[i * count + k],
+                )
+                start += rows
+
+    for side in range(2):
+
+        @pl.when(chosen[0] == side)
+        def _(side=side):
+            for copy in copies(side):
+                copy.start()
+
+    for copy in copies(0):
+        copy.wait()
+    left_high, left_low = split_two(buffers[0][...])
+    right_high, right_low = split_two(buffers[1][...])
+    left = jnp.concatenate([left_high, left_low, left_high], axis=0)
+    right = jnp.concatenate([right_high, right_high, right_low], axis=0)
+    if split_left:
+        half = left.shape[1] // 2
+        outs[1][...] = dot_tn(left[:, half:], right)
+        outs[0][...] = dot_tn(left[:, :half], right)
+    else:
+        half = right.shape[1] // 2
+        outs[1][...] = dot_tn(left, right[:, half:])
+        outs[0][...] = dot_tn(left, right[:, :half])
+    if extra:
+        right_high, right_low = split_two(buffers[2][...])
+        right = jnp.concatenate([right_high, right_high, right_low], axis=0)
+        outs[2][...] = dot_tn(left[:, : outs[2].shape[0]], right)
+    for out in outs:
+        out.copy.wait()
+
+
+def on_core(body, outs, flops, args, fetched, chosen):
+    here = pl.BlockSpec(memory_space=pltpu.VMEM)
+    there = pl.BlockSpec(memory_space=pl.ANY)
+    pad = 2 * LANES
+    tall = [(m.shape[0] + pad - 1) // pad * pad if m.shape[0] > pad else m.shape[0] for m in fetched]
+    scratch = [pltpu.VMEM((rows, m.shape[1]), F32) for rows, m in zip(tall, fetched)]
+    scratch += [pltpu.VMEM(shape, F32) for shape in outs]
+    scratch.append(pltpu.SemaphoreType.DMA((len(fetched),)))
+    scratch.append(pltpu.SemaphoreType.DMA((len(outs),)))
+
+    def guarded(flag, *refs):
+        @pl.when(flag[0] == 1)
+        def _():
+            small, rest = refs[: len(args)], refs[len(args) :]
+            sources, rest = rest[: len(fetched)], rest[len(fetched) :]
+            targets, rest = rest[: len(outs)], rest[len(outs) :]
+            buffers, rest = rest[: len(fetched)], rest[len(fetched) :]
+            kept, (arrivals, departures) = rest[: len(outs)], rest[len(outs) :]
+            inputs = [Fetched(s, b, arrivals.at[i]) for i, (s, b) in enumerate(zip(sources, buffers))]
+            outputs = [Stored(t, b, departures.at[i]) for i, (t, b) in enumerate(zip(targets, kept))]
+            body(*small, *inputs, *outputs)
+            for output in outputs:
+                output.copy.wait()
+
+    return pl.pallas_call(
+        guarded,
+        out_shape=tuple(jax.ShapeDtypeStruct(shape, F32) for shape in outs),
+        in_specs=[pl.BlockSpec(memory_space=pltpu.SMEM)] + [here] * len(args) + [there] * len(fetched),
+        out_specs=tuple(there for _ in outs),
+        scratch_shapes=scratch,
+        compiler_params=pltpu.CompilerParams(vmem_limit_bytes=60 * 2**20),
+        cost_estimate=pl.CostEstimate(flops=flops, bytes_accessed=16 * 2**20, transcendentals=0),
+    )(chosen, *args, *fetched)
+
+
+def outer_call(split_left, outs, widths, flops, chosen, first, second):
+    there = pl.BlockSpec(memory_space=pl.ANY)
+    args = [array for side in (first, second) for factor in side for array in factor]
+    return pl.pallas_call(
+        partial(outer_sum, split_left),
+        out_shape=tuple(jax.ShapeDtypeStruct(shape, F32) for shape in outs),
+        in_specs=[pl.BlockSpec(memory_space=pltpu.SMEM)] + [there] * len(args),
+        out_specs=tuple(there for _ in outs),
+        scratch_shapes=[pltpu.VMEM(shape, F32) for shape in outs]
+        + [pltpu.VMEM((sum(CHUNKS), w), F32) for w in widths]
+        + [
+            pltpu.SemaphoreType.DMA((len(widths) * len(CHUNKS),)),
+            pltpu.SemaphoreType.DMA((len(outs),)),
+        ],
+        compiler_params=pltpu.CompilerParams(vmem_limit_bytes=60 * 2**20),
+        cost_estimate=pl.CostEstimate(flops=flops, bytes_accessed=16 * 2**20, transcendentals=0),
+    )(chosen, *args)
+
+
+def other_core(value):
+    return lax.ppermute(value, "mp", [(0, 1), (1, 0)])
+
+
+def gather_blocks(value):
+    count = lax.axis_size("edge")
+    if count & (count - 1) or count > 8:
+        return lax.all_gather(value, "edge", axis=0)
+    index = lax.axis_index("edge")
+    out = value[None]
+    step = 1
+    while step < count:
+        got = lax.ppermute(out, "edge", [(i, i ^ step) for i in range(count)])
+        low = (index // step) % 2 == 0
+        out = jnp.where(low, jnp.concatenate([out, got]), jnp.concatenate([got, out]))
+        step *= 2
+    return out
+
+
+def prefix_in_rows(flags):
+    rows, length = flags.shape
+    pieces = flags.reshape(rows, length // LANES, LANES)
+    upper = (jnp.arange(LANES)[:, None] <= jnp.arange(LANES)[None, :]).astype(F32)
+    inner = jnp.einsum("rkl,lm->rkm", pieces, upper, precision=HIGHEST)
+    totals = inner[:, :, -1]
+    count = length // LANES
+    before = (jnp.arange(count)[:, None] < jnp.arange(count)[None, :]).astype(F32)
+    offsets = jnp.dot(totals, before, precision=HIGHEST)
+    return (inner + offsets[:, :, None]).reshape(rows, length)
+
+
+def plan_edges(edge_vectors, edge_species, centres, edge_mask, structures):
+    batch_count, _, edge_count = edge_vectors.shape
+    blocks = lax.axis_size("edge")
+    block = lax.axis_index("edge")
+    core = lax.axis_index("mp")
+    atoms = blocks * ATOM_DEV
+    per_block = batch_count * edge_count
+    vectors = edge_vectors.transpose(1, 0, 2).reshape(3, per_block)
+    squares = jnp.maximum(jnp.sum(vectors * vectors, axis=0), 0.25)
+    live = ((jnp.sqrt(squares) / CUTOFF) < 1.0) & (edge_mask.reshape(-1) > 0)
+    batch_of = jnp.arange(per_block) // edge_count
+    raw = jnp.concatenate(
+        [
+            vectors,
+            edge_species.transpose(1, 0, 2).reshape(2, per_block).astype(F32),
+            (centres.reshape(-1) + batch_of * atoms).astype(F32)[None],
+            live.astype(F32)[None],
+            (structures.reshape(-1) + batch_of * STRUCTS).astype(F32)[None],
+        ]
+    )
+    gathered = gather_blocks(raw)
+    keys = gathered[:, 5].reshape(blocks, batch_count, edge_count)
+    alive = gathered[:, 6].reshape(blocks, batch_count, edge_count)
+    local = keys - (jnp.arange(batch_count) * atoms)[None, :, None].astype(F32)
+    degree = jnp.sum(
+        jnp.where(
+            local.transpose(1, 0, 2).reshape(batch_count, 1, -1)
+            == jnp.arange(atoms, dtype=F32)[None, :, None],
+            alive.transpose(1, 0, 2).reshape(batch_count, 1, -1),
+            0.0,
+        ),
+        axis=2,
+    )
+    spans = batch_count * ATOM_DEV
+    degree = degree.reshape(batch_count, blocks, ATOM_DEV).transpose(1, 0, 2).reshape(blocks, spans)
+    upper = (jnp.arange(spans)[:, None] <= jnp.arange(spans)[None, :]).astype(F32)
+    upto = jnp.dot(degree, upper, precision=HIGHEST)
+    start = jnp.zeros((blocks, 1), F32)
+    starts = [start]
+    for size in CHUNKS:
+        for _ in range(2):
+            start = jnp.max(jnp.where(upto <= start + size, jnp.maximum(upto, start), start), axis=1, keepdims=True)
+            starts.append(start)
+    fits = jnp.all(starts[-1] >= upto[:, -1:])
+    starts = jnp.concatenate(starts[:-1], axis=1)
+    own_before = (upto - degree)[block]
+    bin_of = jnp.sum((own_before[:, None] >= starts[block][None, 1:]).astype(F32), axis=1)
+    padded = jnp.concatenate([jnp.zeros_like(gathered[:1]), gathered, jnp.zeros_like(gathered[:1])])
+    window = lax.dynamic_slice_in_dim(padded, block, 3, 0)
+    flat = window.transpose(1, 0, 2).reshape(8, 3 * per_block)
+    position = jnp.arange(3 * per_block)
+    batch_flat = (position % per_block) // edge_count
+    spot = flat[5] - (batch_flat * atoms + block * ATOM_DEV).astype(F32)
+    mine = (spot >= 0) & (spot < ATOM_DEV) & (flat[6] > 0.5)
+    slot = jnp.where(mine, spot + (batch_flat * ATOM_DEV).astype(F32), -1.0)
+    chosen = jnp.sum(
+        jnp.where(jnp.arange(spans, dtype=F32)[:, None] == slot[None, :], bin_of[:, None], 0.0), axis=0
+    )
+    wanted = 2 * jnp.arange(len(CHUNKS)) + core
+    picked = (chosen[None, :] == wanted[:, None].astype(F32)) & mine[None, :]
+    rank = prefix_in_rows(picked.astype(F32)) - 1.0
+    offsets = [sum(CHUNKS[:k]) for k in range(len(CHUNKS))]
+    place = jnp.sum(
+        jnp.where(picked, rank + jnp.array(offsets, F32)[:, None], 0.0), axis=0
+    ) - (1.0 - jnp.sum(picked.astype(F32), axis=0))
+    total = sum(CHUNKS)
+    hot = (place[None, :] == jnp.arange(total, dtype=F32)[:, None]).astype(F32)
+    edges = lax.dot_general(hot, flat, (((1,), (1,)), ((), ())), precision=HIGHEST)
+    return fits, edges, place
+
+
+def tied(first, *others):
+    return lax.optimization_barrier((first, others))[0]
+
+
+def hop(value, distance):
+    return lax.ppermute(value, "edge", [(i, i ^ distance) for i in range(8)])
+
+
+def halves(value, second):
+    half = value.shape[0] // 2
+    kept = lax.dynamic_slice_in_dim(value, second * half, half, 0)
+    return kept, lax.dynamic_slice_in_dim(value, (1 - second) * half, half, 0)
+
+
+def joined(kept, got, second):
+    return jnp.where(second == 0, jnp.concatenate([kept, got]), jnp.concatenate([got, kept]))
+
+
+def sum_piece(value, outer_hop, inner_hop):
+    index = lax.axis_index("edge")
+    seconds = {1: index % 2, 2: ((index // 2) ^ (index // 4)) % 2}
+    kept, given = halves(value, seconds[outer_hop])
+    kept, given = halves(kept + hop(given, outer_hop), seconds[inner_hop])
+    part = kept + hop(given, inner_hop)
+    part = part + hop(part, 6)
+    part = joined(part, hop(part, inner_hop), seconds[inner_hop])
+    half = part.shape[0]
+    return [(part, seconds[outer_hop] * half), (hop(part, outer_hop), (1 - seconds[outer_hop]) * half)]
+
+
+def sum_blocks(matrices, plan):
+    if lax.axis_size("edge") != 8:
+        return [lax.psum(value, "edge") for value in matrices]
+    sums = [jnp.zeros_like(value) for value in matrices]
+    for which, first, rows, outer_hop, inner_hop in plan:
+        piece = lax.slice_in_dim(matrices[which], first, first + rows, axis=0)
+        for part, start in sum_piece(piece, outer_hop, inner_hop):
+            sums[which] = lax.dynamic_update_slice_in_dim(sums[which], part, first + start, 0)
+    return sums
+
+
+def fast_device(edges, place, others, args):
+    (
+        edge_vectors, edge_species, centres, edge_mask, structures, energy_cot, embed_in,
+        section_head, env_weight, mix_weight, w_in, w_out, read_weight,
+    ) = args
+    is_first = lax.axis_index("section") == 0
+    core = lax.axis_index("mp")
+    width = section_head.shape[1]
+    half = section_head.shape[2]
+    batch_count, _, edge_count = edge_vectors.shape
+    chan_count = mix_weight.shape[1]
+    gap = LANES - chan_count
+    read_left, read_right = read_weight[:half], read_weight[half:]
+    read_line = jnp.where(
+        core == 0,
+        jnp.concatenate([read_left, read_right]),
+        jnp.concatenate([read_right, read_left]),
+    )[None]
+    cot_row = jnp.pad(energy_cot.reshape(1, -1), ((0, 0), (0, LANES - energy_cot.size)))
+    lead_flag = jnp.full((8, LANES), 1.0, F32) * (core == 0).astype(F32)
+    mix = jnp.pad(mix_weight, ((0, 0), (0, gap), (0, gap)))
+    env_w = jnp.pad(env_weight[0], ((0, 0), (0, gap)))
+    env_wt = env_w.T
+    heads, ins, outs_w = (section_head[0], others[0]), (w_in[0], others[1]), (w_out[0], others[2])
+    count = len(CHUNKS)
+    offsets = [sum(CHUNKS[:k]) for k in range(count)]
+    rows = [edges[o : o + m, 5].reshape(1, -1) for o, m in zip(offsets, CHUNKS)]
+    layer_width = width + 2 * LANES
+
+    first_flag = jnp.full((1,), 1, jnp.int32) * is_first.astype(jnp.int32)
+    second_flag = 1 - first_flag
+    saved, moved = [], []
+    for k, m in enumerate(CHUNKS):
+        outs = [(m, width + LANES), (m, width), (m, layer_width), (m, width), (m, width)]
+        work = 12 * m * width * (3 * width + 384)
+        result = on_core(
+            partial(first_forward, offsets[k]), outs, work,
+            (edges, rows[k], lead_flag, embed_in), (*heads, env_w, *ins, *outs_w), first_flag,
+        )
+        moved.append(shifted(result[0], "section", 1))
+        saved.append(result[1:])
+    seconds, returned, firsts = [], [], []
+    for k, m in enumerate(CHUNKS):
+        outs = [
+            (m, width + LANES), (m, layer_width), (m, width), (m, width), (m, width),
+            (m, width), (m, width), (m, LANES), (8, width), (3, LANES, LANES), (8, LANES),
+        ]
+        work = 18 * m * width * (3 * width + 384)
+        seconds.append(
+            on_core(
+                partial(second_both, offsets[k]), outs, work,
+                (edges, rows[k], mix, read_line, cot_row),
+                (moved[k], env_w, *ins, *outs_w, *heads, env_wt), second_flag,
+            )
+        )
+    outer_work = 6 * sum(CHUNKS) * width * width
+    for k, m in enumerate(CHUNKS):
+        back = seconds[k][0] if k == 0 else tied(seconds[k][0], firsts[k - 1][0])
+        returned.append(shifted(back, "section", -1))
+        arrived = returned[k]
+        if k == count - 1:
+            out_own, out_other = outer_call(
+                True, [(half, width)] * 2, (width, width), outer_work, second_flag,
+                ([s[3] for s in saved], returned),
+                ([s[3] for s in seconds], [s[4] for s in seconds]),
+            )
+            arrived = tied(arrived, out_other)
+        outs = [(m, LANES), (m, width), (m, width), (m, LANES), (16, width)]
+        work = 9 * m * width * (3 * width + 384)
+        firsts.append(
+            on_core(
+                partial(first_backward, offsets[k]), outs, work,
+                (edges, rows[k], lead_flag, embed_in),
+                (saved[k][1], env_w, arrived, *outs_w, saved[k][2], *ins, env_wt, *heads), first_flag,
+            )
+        )
+    grad_out = out_own + other_core(out_other)
+    in_own, in_other, grad_env = outer_call(
+        False, [(layer_width, half)] * 2 + [(width, LANES)], (layer_width, width, LANES), outer_work,
+        second_flag,
+        ([s[1] for s in saved], [f[2] for f in firsts], [f[3] for f in firsts]),
+        ([s[1] for s in seconds], [s[2] for s in seconds], [s[7] for s in seconds]),
+    )
+    grad_in = in_own + other_core(in_other)
+    head_own, head_other = outer_call(
+        False, [(width, half)] * 2, (width, width), outer_work, tied(second_flag, in_other),
+        ([s[0] for s in saved], [f[1] for f in firsts]),
+        ([s[5] for s in seconds], [s[6] for s in seconds]),
+    )
+    none = jnp.zeros((), F32)
+    read_sum = sum(s[8][0] for s in seconds)
+    read_sum = jnp.where(
+        core == 0, read_sum, jnp.concatenate([read_sum[half:], read_sum[:half]])
+    )
+    mix_sum = sum(s[9] for s in seconds)[:, :chan_count, :chan_count].reshape(-1, width)
+    energy_sum = sum(s[10][0] for s in seconds)
+    embed_sum = sum(f[4] for f in firsts)
+    small_second = jnp.concatenate(
+        [read_sum[None], jnp.pad(energy_sum, (0, width - LANES))[None], mix_sum]
+    )
+    small_second = jnp.pad(small_second, ((0, 16 - small_second.shape[0]), (0, 0)))
+    small = jnp.concatenate(
+        [jnp.where(is_first, embed_sum, none), jnp.where(is_first, none, small_second)]
+    )
+    small = small + lax.ppermute(small, "section", [(0, 1), (1, 0)])
+    small = jnp.concatenate([small, grad_env[:, :chan_count].reshape(-1, width)]).reshape(-1, half)
+    head_own = jnp.concatenate([head_own, small])
+    grad_head = head_own + other_core(jnp.concatenate([head_other, small]))
+    grad_out, grad_in, grad_head = sum_blocks(
+        [grad_out, grad_in, grad_head],
+        [
+            (0, 0, 512, 2, 1), (1, 0, 640, 1, 2), (1, 640, 640, 1, 2), (2, 0, 608, 2, 1),
+            (2, 608, 608, 1, 2),
+        ],
+    )
+    small = grad_head[width:].reshape(-1, width)
+    grad_head = grad_head[:width]
+    grad_embed, grad_read = small[:16], small[16]
+    energies = small[17, : energy_cot.size].reshape(energy_cot.shape)
+    grad_mix = small[18 : 18 + mix_sum.shape[0]].reshape(mix_weight.shape)
+    grad_env = small[32:].reshape(width, chan_count)
+
+    d_vectors = jnp.concatenate([f[0][:, :8] for f in firsts])
+    total = sum(CHUNKS)
+    hot = (place[None, :] == jnp.arange(total, dtype=F32)[:, None]).astype(F32)
+    spread = lax.dot_general(d_vectors, hot, (((0,), (0,)), ((), ())), precision=HIGHEST)[:3]
+    spread = jnp.where(is_first, spread, none)
+    spread = spread + other_core(spread)
+    per_block = batch_count * edge_count
+    to_left, kept, to_right = (spread[:, i * per_block : (i + 1) * per_block] for i in range(3))
+    forces = kept + shifted(to_right, "edge", 1) + shifted(to_left, "edge", -1)
+    forces = jnp.where(is_first, forces, shifted(forces, "section", 1))
+    forces = -forces.reshape(3, batch_count, edge_count).transpose(1, 0, 2)
+    return (
+        energies, forces, grad_embed, grad_head[None], grad_env[None], grad_mix,
+        grad_in[None, : w_in.shape[1]], grad_out[None], grad_read,
+    )
+
+
+def per_device(*args):
+    section_head, w_in, w_out = args[7], args[10], args[11]
+    others = tuple(other_core(m[0]) for m in (section_head, w_in, w_out))
+    fits, edges, place = plan_edges(*args[:5])
+    return lax.cond(
+        fits,
+        lambda: fast_device(edges, place, others, args),
+        lambda: general_device(*args),
+    )
+
+
 def solution(mesh):
     placed = (
         P(None, None, "edge"),

time: 1500 us -> 484 us (0.32)
  the two profiles are of different devices: /device:TPU:0 before, /device:TPU:10 now
where the time goes in v1:
time: 484 us; the launch traced here: 475 us
  waiting for transfers between devices  196 us (40%)
  Pallas kernels  116 us (24%)
  starting transfers between devices  73.4 us (15%)
  local copies, waits for them, and re-layouts  37.9 us (8%)
  other arithmetic  22.1 us (5%)
  between operations  15.5 us (3%)
  loops' own time  8.19 us (2%)
  matrix products  6.11 us (1%)
    ppermute x25, waiting for transfers between devices, hop(): return lax.ppermute(value, 'edge', [(i, i ^ distance) for i in range(8)])  142 us
    pallas_call x9, Pallas kernels, on_core(): pl.pallas_call(guarded, out_shape=tuple((jax.ShapeDtypeStruct(shape, F32)...  92.7 us
    ppermute x9, waiting for transfers between devices, shifted(): lax.ppermute(value, axis, [(source, source + steps) for source in range(f...  39.4 us
    ppermute x25, starting transfers between devices, hop(): return lax.ppermute(value, 'edge', [(i, i ^ distance) for i in range(8)])  31 us
    pallas_call x3, Pallas kernels, outer_call(): pl.pallas_call(partial(outer_sum, split_left), out_shape=tuple((jax.Shape...  23.1 us
    ppermute x9, starting transfers between devices, shifted(): lax.ppermute(value, axis, [(source, source + steps) for source in range(f...  20.7 us
    ppermute x1, starting transfers between devices, fast_device(): small = small + lax.ppermute(small, 'section', [(0, 1), (1, 0)])  15.3 us
    unnamed x35, local copies, waits for them, and re-layouts  10.7 us
  transfers between devices with their start and end apart: 45, of which 19 were waited for; matrix products, arithmetic and copies ran while one was open for 8% of the time, Pallas kernels for 20%

profile of v1, /device:TPU:10, one launch (start us, length us, event | category | flops | bytes accessed | tf_op | source)
XLA Modules:
  0.0 474.9 jit_solution(8238066944187573809)
XLA Ops:
  36.8 421.4 %conditional.9 = (f32[3,16]{1,0:T(4,128)S(1)}, f32[3,3,384]{2,1,0:T(4,128)S(1)}, f32[16,1024]{1,0:T(8,128)}, f32[1,1024,512]{2,1,0:T(8,128)}, f32[1,1024,64]{1,2...) conditional(s32[]{:T(128)} %convert_element_type.315, ...), branch_computations={%region_13.120_spmd, %region_120.121_spmd} | conditional | flops 166489915392 | bytes 1579873792 | solution.py:1177
  61.8 30.7 %collective-permute-done.refs_5_ = f32[160,1152]{1,0:T(8,128)} collective-permute-done((f32[160,1152]{1,0:T(8,128)}, f32[160,1152]{1,0:T(8,128)}, u32[]{:S(2)}, u32[]{:S(2)}) %collective-permute-start) | collective-permute-done | bytes 737312 | tf_op jit(solution)/shard_map/cond/branch_1_fun/ppermute | solution.py:40
  92.6 27.9 %branch_1_fun.15 = (f32[160,1152]{1,0:T(8,128)}, f32[160,1280]{1,0:T(8,128)}, f32[160,1024]{1,0:T(8,128)}, f32[160,1024]{1,0:T(8,128)}, f32[160,1024]{1,0:T(8,12...) custom-call(s32[1]{0:T(128)S(6)} %sub.469.flag.chosen, ...), custom_call_target="tpu_custom_call" | custom-call | flops 10192158720 | bytes 16777216 | tf_op jit(solution)/shard_map/cond/branch_1_fun/pallas_call | solution.py:861
  121.8 26.2 %branch_1_fun.17 = (f32[160,1152]{1,0:T(8,128)}, f32[160,1280]{1,0:T(8,128)}, f32[160,1024]{1,0:T(8,128)}, f32[160,1024]{1,0:T(8,128)}, f32[160,1024]{1,0:T(8,12...) custom-call(s32[1]{0:T(128)S(6)} %sub.469.flag.chosen, ...), custom_call_target="tpu_custom_call" | custom-call | flops 10192158720 | bytes 16777216 | tf_op jit(solution)/shard_map/cond/branch_1_fun/pallas_call | solution.py:861
  153.6 27.8 %branch_1_fun.19 = (f32[160,1152]{1,0:T(8,128)}, f32[160,1280]{1,0:T(8,128)}, f32[160,1024]{1,0:T(8,128)}, f32[160,1024]{1,0:T(8,128)}, f32[160,1024]{1,0:T(8,12...) custom-call(s32[1]{0:T(128)S(6)} %sub.469.flag.chosen, ...), custom_call_target="tpu_custom_call" | custom-call | flops 10192158720 | bytes 16777216 | tf_op jit(solution)/shard_map/cond/branch_1_fun/pallas_call | solution.py:861
  190.4 8.6 %collective-permute-done.5.refs_5_.refs_6_ = f32[160,1152]{1,0:T(8,128)} collective-permute-done((f32[160,1152]{1,0:T(8,128)}, f32[160,1152]{1,0:T(8,128)}, u32[]{:S(2)}, u32[]{:S(2)}) %collective-permute-start.5) | collective-permute-done | bytes 737312 | tf_op jit(solution)/shard_map/cond/branch_1_fun/ppermute | solution.py:40
  199.0 6.9 %branch_1_fun.20 = (f32[512,1024]{1,0:T(8,128)}, f32[512,1024]{1,0:T(8,128)}) custom-call(s32[1]{0:T(128)S(6)} %sub.469.flag.chosen, f32[160,1024]{1,0:T(8,128)} %get-tuple-element.421.refs_0_, f32[160,1024]{1,0:T(8,128)} %get-tuple-element.422.refs_1_, f32[160,1024]{1,0:T(8,128)} %get-tuple-element.423.refs_2_, f32[160,1152]{1,0:T(8,128)} %copy-done.455, ...), custom_call_target="tpu_custom_call" | custom-call | flops 3019898880 | bytes 16777216 | tf_op jit(solution)/shard_map/cond/branch_1_fun/pallas_call | solution.py:875
  207.3 9.2 %branch_1_fun.22 = (f32[1280,512]{1,0:T(8,128)}, f32[1280,512]{1,0:T(8,128)}, f32[1024,128]{1,0:T(8,128)}) custom-call(s32[1]{0:T(128)S(6)} %sub.469.flag.chosen, f32[160,1280]{1,0:T(8,128)} %get-tuple-element.401.refs_4_.refs_0_, f32[160,1280]{1,0:T(8,128)} %get-tuple-element.402.refs_4_.refs_1_, f32[160,1280]{1,0:T(8,128)} %get-tuple-element.403.refs_4_.refs_2_, ...), custom_call_target="tpu_custom_call" | custom-call | flops 3019898880 | bytes 16777216 | tf_op jit(solution)/shard_map/cond/branch_1_fun/pallas_call | solution.py:875
  216.6 15.3 %collective-permute-start.6 = (f32[32,1024]{1,0:T(8,128)S(1)}, f32[32,1024]{1,0:T(8,128)S(1)}, u32[]{:S(2)}, u32[]{:S(2)}) collective-permute-start(f32[32,1024]{1,0:T(8,128)S(1)} %pad_maximum_fusion.30), channel_id=1, source_target_pairs={{0,16},{16,0},{1,17},{17,1},{2,18},{18,2},{3,19},{19,3},{4,20},{20... | collective-permute-start | bytes 393224 | tf_op jit(solution)/shard_map/cond/branch_1_fun/ppermute | solution.py:1138
  231.9 7.0 %branch_1_fun.23 = (f32[1024,512]{1,0:T(8,128)}, f32[1024,512]{1,0:T(8,128)}) custom-call(s32[1]{0:T(128)S(6)} %sub.469.flag.chosen, f32[160,1024]{1,0:T(8,128)} %get-tuple-element.448.refs_0_, f32[160,1024]{1,0:T(8,128)} %get-tuple-element.449.refs_1_, f32[160,1024]{1,0:T(8,128)} %get-tuple-element.450.refs_2_, f32[160,1024]{1,0:T(8,128)} %get-tuple-element.451.refs_3_, ...), custom_call_target="tpu_custom_call" | custom-call | flops 3019898880 | bytes 16777216 | tf_op jit(solution)/shard_map/cond/branch_1_fun/pallas_call | solution.py:875
  256.1 5.6 %collective-permute-start.34 = (f32[256,1024]{1,0:T(8,128)S(1)}, f32[256,1024]{1,0:T(8,128)S(1)}, u32[]{:S(2)}, u32[]{:S(2)}) collective-permute-start(f32[256,1024]{1,0:T(8,128)S(1)} %constant_dynamic-slice_fusion.91), channel_id=1, source_target_pairs={{0,4},{2,6},{4,0},{6,2},{8,12},{10,14},{12,8},{14,10},{1,5},{3,7},... | collective-permute-start | bytes 3145736 | tf_op jit(solution)/shard_map/cond/branch_1_fun/ppermute | solution.py:998
  271.6 14.0 %collective-permute-done.34 = f32[256,1024]{1,0:T(8,128)S(1)} collective-permute-done((f32[256,1024]{1,0:T(8,128)S(1)}, f32[256,1024]{1,0:T(8,128)S(1)}, u32[]{:S(2)}, u32[]{:S(2)}) %collective-permute-start.34) | collective-permute-done | bytes 1048608 | tf_op jit(solution)/shard_map/cond/branch_1_fun/ppermute | solution.py:998
  285.8 12.7 %collective-permute-done.8 = f32[304,512]{1,0:T(8,128)S(1)} collective-permute-done((f32[304,512]{1,0:T(8,128)S(1)}, f32[304,512]{1,0:T(8,128)S(1)}, u32[]{:S(2)}, u32[]{:S(2)}) %collective-permute-start.8) | collective-permute-done | bytes 622624 | tf_op jit(solution)/shard_map/cond/branch_1_fun/ppermute | solution.py:998
  302.8 8.9 %collective-permute-done.28 = f32[320,512]{1,0:T(8,128)S(1)} collective-permute-done((f32[320,512]{1,0:T(8,128)S(1)}, f32[320,512]{1,0:T(8,128)S(1)}, u32[]{:S(2)}, u32[]{:S(2)}) %collective-permute-start.28) | collective-permute-done | bytes 655392 | tf_op jit(solution)/shard_map/cond/branch_1_fun/ppermute | solution.py:998
  313.1 15.4 %collective-permute-done.9 = f32[152,512]{1,0:T(8,128)S(1)} collective-permute-done((f32[152,512]{1,0:T(8,128)S(1)}, f32[152,512]{1,0:T(8,128)S(1)}, u32[]{:S(2)}, u32[]{:S(2)}) %collective-permute-start.9) | collective-permute-done | bytes 311328 | tf_op jit(solution)/shard_map/cond/branch_1_fun/ppermute | solution.py:998
  331.3 19.5 %collective-permute-done.10 = f32[152,512]{1,0:T(8,128)S(1)} collective-permute-done((f32[152,512]{1,0:T(8,128)S(1)}, f32[152,512]{1,0:T(8,128)S(1)}, u32[]{:S(2)}, u32[]{:S(2)}) %collective-permute-start.10) | collective-permute-done | bytes 311328 | tf_op jit(solution)/shard_map/cond/branch_1_fun/ppermute | solution.py:998
  351.8 8.2 %collective-permute-done.25 = f32[160,512]{1,0:T(8,128)S(1)} collective-permute-done((f32[160,512]{1,0:T(8,128)S(1)}, f32[160,512]{1,0:T(8,128)S(1)}, u32[]{:S(2)}, u32[]{:S(2)}) %collective-permute-start.25) | collective-permute-done | bytes 327712 | tf_op jit(solution)/shard_map/cond/branch_1_fun/ppermute | solution.py:998
  364.7 20.9 %collective-permute-done.15 = f32[152,512]{1,0:T(8,128)S(1)} collective-permute-done((f32[152,512]{1,0:T(8,128)S(1)}, f32[152,512]{1,0:T(8,128)S(1)}, u32[]{:S(2)}, u32[]{:S(2)}) %collective-permute-start.15) | collective-permute-done | bytes 311328 | tf_op jit(solution)/shard_map/cond/branch_1_fun/ppermute | solution.py:998
  387.2 8.1 %collective-permute-done.36 = f32[128,1024]{1,0:T(8,128)S(1)} collective-permute-done((f32[128,1024]{1,0:T(8,128)S(1)}, f32[128,1024]{1,0:T(8,128)S(1)}, u32[]{:S(2)}, u32[]{:S(2)}) %collective-permute-start.36) | collective-permute-done | bytes 524320 | tf_op jit(solution)/shard_map/cond/branch_1_fun/ppermute | solution.py:998
  402.2 5.2 %collective-permute-done.16 = f32[152,512]{1,0:T(8,128)S(1)} collective-permute-done((f32[152,512]{1,0:T(8,128)S(1)}, f32[152,512]{1,0:T(8,128)S(1)}, u32[]{:S(2)}, u32[]{:S(2)}) %collective-permute-start.16) | collective-permute-done | bytes 311328 | tf_op jit(solution)/shard_map/cond/branch_1_fun/ppermute | solution.py:998
  409.0 5.5 %collective-permute-start.31 = (f32[160,512]{1,0:T(8,128)S(1)}, f32[160,512]{1,0:T(8,128)S(1)}, u32[]{:S(2)}, u32[]{:S(2)}) collective-permute-start(f32[160,512]{1,0:T(8,128)S(1)} %add.1111), channel_id=1, source_target_pairs={{0,4},{2,6},{4,0},{6,2},{8,12},{10,14},{12,8},{14,10},{1,5},{3,7},... | collective-permute-start | bytes 983048 | tf_op jit(solution)/shard_map/cond/branch_1_fun/ppermute | solution.py:998
  416.1 10.3 %collective-permute-done.27 = f32[320,512]{1,0:T(8,128)S(1)} collective-permute-done((f32[320,512]{1,0:T(8,128)S(1)}, f32[320,512]{1,0:T(8,128)S(1)}, u32[]{:S(2)}, u32[]{:S(2)}) %collective-permute-start.27) | collective-permute-done | bytes 655392 | tf_op jit(solution)/shard_map/cond/branch_1_fun/ppermute | solution.py:998
  428.3 11.3 %collective-permute-done.17 = f32[304,512]{1,0:T(8,128)S(1)} collective-permute-done((f32[304,512]{1,0:T(8,128)S(1)}, f32[304,512]{1,0:T(8,128)S(1)}, u32[]{:S(2)}, u32[]{:S(2)}) %collective-permute-start.17) | collective-permute-done | bytes 622624 | tf_op jit(solution)/shard_map/cond/branch_1_fun/ppermute | solution.py:998
  445.6 6.0 %collective-permute-done.32 = f32[320,512]{1,0:T(8,128)} collective-permute-done((f32[320,512]{1,0:T(8,128)}, f32[320,512]{1,0:T(8,128)}, u32[]{:S(2)}, u32[]{:S(2)}) %collective-permute-start.32) | collective-permute-done | bytes 655392 | tf_op jit(solution)/shard_map/cond/branch_1_fun/ppermute | solution.py:998
  (316 shorter events, 139.9 us)
Async XLA Ops:
  48.8 104.9 %collective-permute-start.4 = (f32[160,1152]{1,0:T(8,128)}, f32[160,1152]{1,0:T(8,128)}, u32[]{:S(2)}, u32[]{:S(2)}) collective-permute-start(f32[160,1152]{1,0:T(8,128)} %get-tuple-element.417), channel_id=1, source_target_pairs={{0,16},{1,17},{2,18},{3,19},{4,20},{5,21},{6,22},{7,23},{8,24},{9,... | collective-permute-start | bytes 2211848 | tf_op jit(solution)/shard_map/cond/branch_1_fun/ppermute | solution.py:40
  51.3 41.3 %collective-permute-start = (f32[160,1152]{1,0:T(8,128)}, f32[160,1152]{1,0:T(8,128)}, u32[]{:S(2)}, u32[]{:S(2)}) collective-permute-start(f32[160,1152]{1,0:T(8,128)} %get-tuple-element.407), channel_id=1, source_target_pairs={{0,16},{1,17},{2,18},{3,19},{4,20},{5,21},{6,22},{7,23},{8,24},{9,... | collective-permute-start | bytes 2211848 | tf_op jit(solution)/shard_map/cond/branch_1_fun/ppermute | solution.py:40
  57.7 64.1 %collective-permute-start.2 = (f32[160,1152]{1,0:T(8,128)}, f32[160,1152]{1,0:T(8,128)}, u32[]{:S(2)}, u32[]{:S(2)}) collective-permute-start(f32[160,1152]{1,0:T(8,128)} %get-tuple-element.411), channel_id=1, source_target_pairs={{0,16},{1,17},{2,18},{3,19},{4,20},{5,21},{6,22},{7,23},{8,24},{9,... | collective-permute-start | bytes 2211848 | tf_op jit(solution)/shard_map/cond/branch_1_fun/ppermute | solution.py:40
  120.5 27.5 %collective-permute-start.1 = (f32[160,1152]{1,0:T(8,128)}, f32[160,1152]{1,0:T(8,128)S(1)}, u32[]{:S(2)}, u32[]{:S(2)}) collective-permute-start(f32[160,1152]{1,0:T(8,128)} %get-tuple-element.408), channel_id=1, source_target_pairs={{16,0},{17,1},{18,2},{19,3},{20,4},{21,5},{22,6},{23,7},{24,8},{25... | collective-permute-start | bytes 2211848 | tf_op jit(solution)/shard_map/cond/branch_1_fun/ppermute | solution.py:40
  150.0 33.1 %collective-permute-start.3 = (f32[160,1152]{1,0:T(8,128)}, f32[160,1152]{1,0:T(8,128)S(1)}, u32[]{:S(2)}, u32[]{:S(2)}) collective-permute-start(f32[160,1152]{1,0:T(8,128)} %get-tuple-element.414), channel_id=1, source_target_pairs={{16,0},{17,1},{18,2},{19,3},{20,4},{21,5},{22,6},{23,7},{24,8},{25... | collective-permute-start | bytes 2211848 | tf_op jit(solution)/shard_map/cond/branch_1_fun/ppermute | solution.py:40
  249.7 113.0 %collective-permute-start.19 = (f32[3,1152]{1,0:T(4,128)S(1)}, f32[3,1152]{1,0:T(4,128)S(1)}, u32[]{:S(2)}, u32[]{:S(2)}) collective-permute-start(f32[3,1152]{1,0:T(4,128)S(1)} %get-tuple-element.1174), channel_id=1, source_target_pairs={{0,2},{2,4},{4,6},{6,8},{8,10},{10,12},{12,14},{1,3},{3,5},{5,7},{... | collective-permute-start | bytes 41480 | tf_op jit(solution)/shard_map/cond/branch_1_fun/ppermute | solution.py:40
  256.1 29.5 %collective-permute-start.34 = (f32[256,1024]{1,0:T(8,128)S(1)}, f32[256,1024]{1,0:T(8,128)S(1)}, u32[]{:S(2)}, u32[]{:S(2)}) collective-permute-start(f32[256,1024]{1,0:T(8,128)S(1)} %constant_dynamic-slice_fusion.91), channel_id=1, source_target_pairs={{0,4},{2,6},{4,0},{6,2},{8,12},{10,14},{12,8},{14,10},{1,5},{3,7},... | collective-permute-start | bytes 3145736 | tf_op jit(solution)/shard_map/cond/branch_1_fun/ppermute | solution.py:998
  265.7 32.7 %collective-permute-start.8 = (f32[304,512]{1,0:T(8,128)S(1)}, f32[304,512]{1,0:T(8,128)S(1)}, u32[]{:S(2)}, u32[]{:S(2)}) collective-permute-start(f32[304,512]{1,0:T(8,128)S(1)} %constant_dynamic-slice_fusion.99), channel_id=1, source_target_pairs={{0,4},{2,6},{4,0},{6,2},{8,12},{10,14},{12,8},{14,10},{1,5},{3,7},... | collective-permute-start | bytes 1867784 | tf_op jit(solution)/shard_map/cond/branch_1_fun/ppermute | solution.py:998
  266.7 31.9 %collective-permute-start.13 = (f32[304,512]{1,0:T(8,128)S(1)}, f32[304,512]{1,0:T(8,128)S(1)}, u32[]{:S(2)}, u32[]{:S(2)}) collective-permute-start(f32[304,512]{1,0:T(8,128)S(1)} %constant_dynamic-slice_fusion.97), channel_id=1, source_target_pairs={{0,2},{2,0},{4,6},{6,4},{8,10},{10,8},{12,14},{14,12},{1,3},{3,1},... | collective-permute-start | bytes 1867784 | tf_op jit(solution)/shard_map/cond/branch_1_fun/ppermute | solution.py:998
  269.9 31.0 %collective-permute-start.23 = (f32[320,512]{1,0:T(8,128)S(1)}, f32[320,512]{1,0:T(8,128)S(1)}, u32[]{:S(2)}, u32[]{:S(2)}) collective-permute-start(f32[320,512]{1,0:T(8,128)S(1)} %constant_dynamic-slice_fusion.95), channel_id=1, source_target_pairs={{0,2},{2,0},{4,6},{6,4},{8,10},{10,8},{12,14},{14,12},{1,3},{3,1},... | collective-permute-start | bytes 1966088 | tf_op jit(solution)/shard_map/cond/branch_1_fun/ppermute | solution.py:998
  285.6 26.1 %collective-permute-start.28 = (f32[320,512]{1,0:T(8,128)S(1)}, f32[320,512]{1,0:T(8,128)S(1)}, u32[]{:S(2)}, u32[]{:S(2)}) collective-permute-start(f32[320,512]{1,0:T(8,128)S(1)} %constant_dynamic-slice_fusion.93), channel_id=1, source_target_pairs={{0,2},{2,0},{4,6},{6,4},{8,10},{10,8},{12,14},{14,12},{1,3},{3,1},... | collective-permute-start | bytes 1966088 | tf_op jit(solution)/shard_map/cond/branch_1_fun/ppermute | solution.py:998
  298.5 53.2 %collective-permute-start.35 = (f32[128,1024]{1,0:T(8,128)S(1)}, f32[128,1024]{1,0:T(8,128)S(1)}, u32[]{:S(2)}, u32[]{:S(2)}) collective-permute-start(f32[128,1024]{1,0:T(8,128)S(1)} %constant_dynamic-slice_fusion.90), channel_id=1, source_target_pairs={{0,2},{2,0},{4,6},{6,4},{8,10},{10,8},{12,14},{14,12},{1,3},{3,1},... | collective-permute-start | bytes 1572872 | tf_op jit(solution)/shard_map/cond/branch_1_fun/ppermute | solution.py:998
  298.6 29.9 %collective-permute-start.9 = (f32[152,512]{1,0:T(8,128)S(1)}, f32[152,512]{1,0:T(8,128)S(1)}, u32[]{:S(2)}, u32[]{:S(2)}) collective-permute-start(f32[152,512]{1,0:T(8,128)S(1)} %constant_dynamic-slice_fusion.98), channel_id=1, source_target_pairs={{0,2},{2,0},{4,6},{6,4},{8,10},{10,8},{12,14},{14,12},{1,3},{3,1},... | collective-permute-start | bytes 933896 | tf_op jit(solution)/shard_map/cond/branch_1_fun/ppermute | solution.py:998
  300.9 50.1 %collective-permute-start.14 = (f32[152,512]{1,0:T(8,128)S(1)}, f32[152,512]{1,0:T(8,128)S(1)}, u32[]{:S(2)}, u32[]{:S(2)}) collective-permute-start(f32[152,512]{1,0:T(8,128)S(1)} %constant_dynamic-slice_fusion.96), channel_id=1, source_target_pairs={{0,4},{2,6},{4,0},{6,2},{8,12},{10,14},{12,8},{14,10},{1,5},{3,7},... | collective-permute-start | bytes 933896 | tf_op jit(solution)/shard_map/cond/branch_1_fun/ppermute | solution.py:998
  328.7 34.0 %collective-permute-start.20 = (f32[3,1152]{1,0:T(4,128)S(1)}, f32[3,1152]{1,0:T(4,128)S(1)}, u32[]{:S(2)}, u32[]{:S(2)}) collective-permute-start(f32[3,1152]{1,0:T(4,128)S(1)} %get-tuple-element.1175), channel_id=1, source_target_pairs={{2,0},{4,2},{6,4},{8,6},{10,8},{12,10},{14,12},{3,1},{5,3},{7,5},{... | collective-permute-start | bytes 41480 | tf_op jit(solution)/shard_map/cond/branch_1_fun/ppermute | solution.py:40
  351.7 35.3 %collective-permute-start.29 = (f32[160,512]{1,0:T(8,128)S(1)}, f32[160,512]{1,0:T(8,128)S(1)}, u32[]{:S(2)}, u32[]{:S(2)}) collective-permute-start(f32[160,512]{1,0:T(8,128)S(1)} %constant_dynamic-slice_fusion.92), channel_id=1, source_target_pairs={{0,4},{2,6},{4,0},{6,2},{8,12},{10,14},{12,8},{14,10},{1,5},{3,7},... | collective-permute-start | bytes 983048 | tf_op jit(solution)/shard_map/cond/branch_1_fun/ppermute | solution.py:998
  360.0 25.6 %collective-permute-start.15 = (f32[152,512]{1,0:T(8,128)S(1)}, f32[152,512]{1,0:T(8,128)S(1)}, u32[]{:S(2)}, u32[]{:S(2)}) collective-permute-start(f32[152,512]{1,0:T(8,128)S(1)} %dynamic-slice_add_fusion.8), channel_id=1, source_target_pairs={{0,12},{2,14},{4,8},{6,10},{8,4},{10,6},{12,0},{14,2},{1,13},{3,15... | collective-permute-start | bytes 933896 | tf_op jit(solution)/shard_map/cond/branch_1_fun/ppermute | solution.py:998
  360.6 34.7 %collective-permute-start.36 = (f32[128,1024]{1,0:T(8,128)S(1)}, f32[128,1024]{1,0:T(8,128)S(1)}, u32[]{:S(2)}, u32[]{:S(2)}) collective-permute-start(f32[128,1024]{1,0:T(8,128)S(1)} %dynamic-slice_add_fusion.5), channel_id=1, source_target_pairs={{0,12},{2,14},{4,8},{6,10},{8,4},{10,6},{12,0},{14,2},{1,13},{3,15... | collective-permute-start | bytes 1572872 | tf_op jit(solution)/shard_map/cond/branch_1_fun/ppermute | solution.py:998
  362.6 34.7 %collective-permute-start.26 = (f32[160,512]{1,0:T(8,128)S(1)}, f32[160,512]{1,0:T(8,128)S(1)}, u32[]{:S(2)}, u32[]{:S(2)}) collective-permute-start(f32[160,512]{1,0:T(8,128)S(1)} %add.1106), channel_id=1, source_target_pairs={{0,4},{2,6},{4,0},{6,2},{8,12},{10,14},{12,8},{14,10},{1,5},{3,7},... | collective-permute-start | bytes 983048 | tf_op jit(solution)/shard_map/cond/branch_1_fun/ppermute | solution.py:998
  362.7 38.0 %collective-permute-start.12 = (f32[304,512]{1,0:T(8,128)S(1)}, f32[304,512]{1,0:T(8,128)S(1)}, u32[]{:S(2)}, u32[]{:S(2)}) collective-permute-start(f32[304,512]{1,0:T(8,128)S(1)} %get-tuple-element.890), channel_id=1, source_target_pairs={{0,4},{2,6},{4,0},{6,2},{8,12},{10,14},{12,8},{14,10},{1,5},{3,7},... | collective-permute-start | bytes 1867784 | tf_op jit(solution)/shard_map/cond/branch_1_fun/ppermute | solution.py:998
  400.7 25.6 %collective-permute-start.27 = (f32[320,512]{1,0:T(8,128)S(1)}, f32[320,512]{1,0:T(8,128)S(1)}, u32[]{:S(2)}, u32[]{:S(2)}) collective-permute-start(f32[320,512]{1,0:T(8,128)S(1)} %get-tuple-element.886), channel_id=1, source_target_pairs={{0,2},{2,0},{4,6},{6,4},{8,10},{10,8},{12,14},{14,12},{1,3},{3,1},... | collective-permute-start | bytes 1966088 | tf_op jit(solution)/shard_map/cond/branch_1_fun/ppermute | solution.py:998
  407.5 32.2 %collective-permute-start.17 = (f32[304,512]{1,0:T(8,128)S(1)}, f32[304,512]{1,0:T(8,128)S(1)}, u32[]{:S(2)}, u32[]{:S(2)}) collective-permute-start(f32[304,512]{1,0:T(8,128)S(1)} %get-tuple-element.888), channel_id=1, source_target_pairs={{0,2},{2,0},{4,6},{6,4},{8,10},{10,8},{12,14},{14,12},{1,3},{3,1},... | collective-permute-start | bytes 1867784 | tf_op jit(solution)/shard_map/cond/branch_1_fun/ppermute | solution.py:998
  415.7 38.8 %collective-permute-start.38 = (f32[256,1024]{1,0:T(8,128)}, f32[256,1024]{1,0:T(8,128)}, u32[]{:S(2)}, u32[]{:S(2)}) collective-permute-start(f32[256,1024]{1,0:T(8,128)} %maximum_select_fusion.1), channel_id=1, source_target_pairs={{0,4},{2,6},{4,0},{6,2},{8,12},{10,14},{12,8},{14,10},{1,5},{3,7},... | collective-permute-start | bytes 3145736 | tf_op jit(solution)/shard_map/cond/branch_1_fun/ppermute | solution.py:998
  427.3 24.3 %collective-permute-start.32 = (f32[320,512]{1,0:T(8,128)}, f32[320,512]{1,0:T(8,128)}, u32[]{:S(2)}, u32[]{:S(2)}) collective-permute-start(f32[320,512]{1,0:T(8,128)} %get-tuple-element.884), channel_id=1, source_target_pairs={{0,2},{2,0},{4,6},{6,4},{8,10},{10,8},{12,14},{14,12},{1,3},{3,1},... | collective-permute-start | bytes 1966088 | tf_op jit(solution)/shard_map/cond/branch_1_fun/ppermute | solution.py:998
  (60 other events, 599.5 us)

commit v2 on v1

--- a/solution.py
+++ b/solution.py
@@ -38,6 +38,23 @@
     count = lax.axis_size(axis)
     first, last = (max(0, -steps), min(count, count - steps))
     return lax.ppermute(value, axis, [(source, source + steps) for source in range(first, last)])
+
+
+def other_core(value):
+    return lax.ppermute(value, "mp", [(0, 1), (1, 0)])
+
+
+def ring_sum(values):
+    count = lax.axis_size("edge")
+
+    def step(_, state):
+        moving, total = state
+        moving = tuple(
+            lax.ppermute(v, "edge", [(i, (i + 1) % count) for i in range(count)]) for v in moving
+        )
+        return moving, tuple(t + v for t, v in zip(total, moving))
+
+    return lax.fori_loop(0, count - 1, step, (tuple(values), tuple(values)))[1]
 
 
 def matmul(left, right):
@@ -170,7 +187,17 @@
         return extended(totals, (("edge", 0),), atoms_dev)
 
     def collect(partial_rows):
-        return lax.psum_scatter(partial_rows, "mp", scatter_dimension=1, tiled=True)
+        width = partial_rows.shape[1] // 2
+        own = lax.dynamic_slice_in_dim(partial_rows, core_index * width, width, 1)
+        return own + other_core(lax.dynamic_slice_in_dim(partial_rows, (1 - core_index) * width, width, 1))
+
+    def both_halves(half):
+        other = other_core(half)
+        return jnp.where(
+            core_index == 0,
+            jnp.concatenate([half, other], axis=1),
+            jnp.concatenate([other, half], axis=1),
+        )
 
     def batch_data(batch_index):
         vectors = lax.dynamic_index_in_dim(edge_vectors, batch_index, 0, keepdims=False)
@@ -208,8 +235,8 @@
             lambda: recv_latent,
         )
         latent_full, tensor_full = (
-            lax.all_gather(latent_half, "mp", axis=1, tiled=True),
-            lax.all_gather(recv_tensor, "mp", axis=1, tiled=True),
+            both_halves(latent_half),
+            both_halves(recv_tensor),
         )
         weight, part_sums = contribute(latent_full, harmonics, envelope, env_local, centre_hot)
         env_window = window_rows(reduce_rims(part_sums))
@@ -217,11 +244,11 @@
             tensor_full, env_window, weight, harmonics, mix_weight, centre_hot, is_first
         )
         branch_out = perceptron(latent_full, scalars, in_local, out_local)
-        summed = lax.psum_scatter(branch_out, "mp", scatter_dimension=1, tiled=True)
+        summed = collect(branch_out)
         tensor_own = lax.dynamic_slice_in_dim(updated, core_index * tensor_half, tensor_half, 1)
         next_half = latent_half + summed
         recv_latent, recv_tensor = shifted((next_half, tensor_own), "section", 1)
-        next_full = lax.all_gather(next_half, "mp", axis=1, tiled=True)
+        next_full = both_halves(next_half)
         edge_energy = readout(next_full, envelope, head_local, read_half)
         batch_slot = (batch_range == batch_index).astype(jnp.float32) * is_valid * last_flag
         energies = (
@@ -262,8 +289,8 @@
         d_next_read, d_env_read, g_head_read, g_read = read_pull(energy_rows)
         d_next_half = jnp.where(is_first, recv_grad, collect(d_next_read))
         d_out_full, d_updated = (
-            lax.all_gather(d_next_half, "mp", axis=1, tiled=True),
-            lax.all_gather(recv_tgrad, "mp", axis=1, tiled=True),
+            both_halves(d_next_half),
+            both_halves(recv_tgrad),
         )
         (weight, part_sums), contribute_pull = jax.vjp(
             partial(contribute, centre_hot=centre_hot), latent_full, harmonics, envelope, env_local
@@ -278,7 +305,7 @@
         )
         _, perceptron_pull = jax.vjp(perceptron, latent_full, scalars, in_local, out_local)
         d_latent_mlp, d_scalar_part, g_in, g_out = perceptron_pull(d_out_full)
-        d_scalars = lax.psum(d_scalar_part, "mp")
+        d_scalars = d_scalar_part + other_core(d_scalar_part)
         d_tensor, d_window, d_weight, d_harm_tensor, g_mix = tensor_pull((d_scalars, d_updated))
         d_parts = window_rows(reduce_rims(d_window))
         d_latent_env, d_harm_env, d_envelope_env, g_env = contribute_pull((d_weight, d_parts))
@@ -319,16 +346,15 @@
         grad_mix = grad_mix + is_valid * g_mix
         grad_embed = grad_embed + is_valid * g_embed
         grad_read = grad_read + is_valid * g_read
-    grad_head, grad_env, grad_in, grad_out = lax.psum(
-        (grad_head, grad_env, grad_in, grad_out), "edge"
-    )
+    grad_head, grad_env, grad_in, grad_out = ring_sum((grad_head, grad_env, grad_in, grad_out))
     read_full = lax.dynamic_update_slice_in_dim(
         jnp.zeros_like(read_weight), grad_read, core_index * shard_width, 0
     )
-    energies, grad_embed, grad_mix, read_full = lax.psum(
-        (energies, grad_embed, core_lead * grad_mix, read_full), ("section", "edge", "mp")
-    )
-    forces = lax.psum(forces, ("section", "mp"))
+    chip_sums = [v + other_core(v) for v in (energies, grad_embed, core_lead * grad_mix, read_full, forces)]
+    energies, grad_embed, grad_mix, read_full, forces = (
+        v + lax.ppermute(v, "section", [(0, 1), (1, 0)]) for v in chip_sums
+    )
+    energies, grad_embed, grad_mix, read_full = ring_sum((energies, grad_embed, grad_mix, read_full))
     return (
         energies,
         -forces,
@@ -888,10 +914,6 @@
     )(chosen, *args)
 
 
-def other_core(value):
-    return lax.ppermute(value, "mp", [(0, 1), (1, 0)])
-
-
 def gather_blocks(value):
     count = lax.axis_size("edge")
     if count & (count - 1) or count > 8:
@@ -919,6 +941,20 @@
     return (inner + offsets[:, :, None]).reshape(rows, length)
 
 
+def pack_edges(atoms, vectors, species, centres, mask, structures, out):
+    count = centres.shape[1]
+    for b in range(centres.shape[0]):
+        span = slice(b * count, (b + 1) * count)
+        vector = vectors[b]
+        out[0:3, span] = vector
+        out[3:5, span] = species[b].astype(F32)
+        out[5:6, span] = (centres[b : b + 1, :] + b * atoms).astype(F32)
+        squares = jnp.maximum(jnp.sum(vector * vector, axis=0, keepdims=True), 0.25)
+        near = jnp.where(jnp.sqrt(squares) / CUTOFF < 1.0, 1.0, 0.0)
+        out[6:7, span] = jnp.where(mask[b : b + 1, :] > 0, near, 0.0)
+        out[7:8, span] = (structures[b : b + 1, :] + b * STRUCTS).astype(F32)
+
+
 def plan_edges(edge_vectors, edge_species, centres, edge_mask, structures):
     batch_count, _, edge_count = edge_vectors.shape
     blocks = lax.axis_size("edge")
@@ -926,19 +962,9 @@
     core = lax.axis_index("mp")
     atoms = blocks * ATOM_DEV
     per_block = batch_count * edge_count
-    vectors = edge_vectors.transpose(1, 0, 2).reshape(3, per_block)
-    squares = jnp.maximum(jnp.sum(vectors * vectors, axis=0), 0.25)
-    live = ((jnp.sqrt(squares) / CUTOFF) < 1.0) & (edge_mask.reshape(-1) > 0)
-    batch_of = jnp.arange(per_block) // edge_count
-    raw = jnp.concatenate(
-        [
-            vectors,
-            edge_species.transpose(1, 0, 2).reshape(2, per_block).astype(F32),
-            (centres.reshape(-1) + batch_of * atoms).astype(F32)[None],
-            live.astype(F32)[None],
-            (structures.reshape(-1) + batch_of * STRUCTS).astype(F32)[None],
-        ]
-    )
+    raw = pl.pallas_call(
+        partial(pack_edges, atoms), out_shape=jax.ShapeDtypeStruct((8, per_block), F32)
+    )(edge_vectors, edge_species, centres, edge_mask, structures)
     gathered = gather_blocks(raw)
     keys = gathered[:, 5].reshape(blocks, batch_count, edge_count)
     alive = gathered[:, 6].reshape(blocks, batch_count, edge_count)
@@ -1174,11 +1200,15 @@
     section_head, w_in, w_out = args[7], args[10], args[11]
     others = tuple(other_core(m[0]) for m in (section_head, w_in, w_out))
     fits, edges, place = plan_edges(*args[:5])
-    return lax.cond(
-        fits,
-        lambda: fast_device(edges, place, others, args),
-        lambda: general_device(*args),
-    )
+    results = fast_device(edges, place, others, args)
+
+    def again(state):
+        rest, _ = state
+        held, rest = lax.optimization_barrier((args, rest))
+        return rest - 1, general_device(*held)
+
+    overflow = 1 - fits.astype(jnp.int32)
+    return lax.while_loop(lambda state: state[0] > 0, again, (overflow, results))[1]
 
 
 def solution(mesh):

time: 484 us -> 434 us (0.90)
  waiting for transfers between devices: 196 us -> 169 us
  Pallas kernels: 116 us -> 129 us
  between operations: 15.5 us -> 2.58 us
  starting transfers between devices: 73.4 us -> 63.8 us
  loops' own time: 8.19 us -> 1.1 us
  local copies, waits for them, and re-layouts: 37.9 us -> 32.4 us
    pallas_call x9, Pallas kernels: 92.7 us -> 105 us  [on_core(): pl.pallas_call(guarded, out_shape=tuple((jax.ShapeDtypeStruct(shape, F32)...]
    ppermute x9, waiting for transfers between devices: 39.4 us -> 29.6 us  [shifted(): lax.ppermute(value, axis, [(source, source + steps) for source in range(f...]
    ppermute x25, waiting for transfers between devices: 142 us -> 133 us  [hop(): return lax.ppermute(value, 'edge', [(i, i ^ distance) for i in range(8)])]
    cond x58 -> x0, local copies, waits for them, and re-layouts: 8.8 us -> none
    ppermute x1, starting transfers between devices: 15.3 us -> 6.94 us  [fast_device(): small = small + lax.ppermute(small, 'section', [(0, 1), (1, 0)])]
    another operation x1, loops' own time: 8.19 us -> 1.1 us  [per_device(): lax.while_loop(lambda state: state[0] > 0, again, (overflow, results))[1]]
    ppermute x3, waiting for transfers between devices: 9.94 us -> 3.97 us  [gather_blocks(): got = lax.ppermute(out, 'edge', [(i, i ^ step) for i in range(count)])]
    unnamed x35 -> x46, local copies, waits for them, and re-layouts: 10.7 us -> 6.94 us
  transfers between devices with their start and end apart: 45 -> 45, of which waited for: 19 -> 22; matrix products, arithmetic and copies ran while one was open for 8% -> 12% of each run, Pallas kernels for 20% -> 23%
where the time goes in v2:
time: 434 us; the launch traced here: 428 us
  waiting for transfers between devices  169 us (39%)
  Pallas kernels  129 us (30%)
  starting transfers between devices  63.8 us (15%)
  local copies, waits for them, and re-layouts  32.4 us (7%)
  other arithmetic  24.4 us (6%)
  matrix products  5.48 us (1%)
    ppermute x25, waiting for transfers between devices, hop(): return lax.ppermute(value, 'edge', [(i, i ^ distance) for i in range(8)])  133 us
    pallas_call x9, Pallas kernels, on_core(): pl.pallas_call(guarded, out_shape=tuple((jax.ShapeDtypeStruct(shape, F32)...  105 us
    ppermute x25, starting transfers between devices, hop(): return lax.ppermute(value, 'edge', [(i, i ^ distance) for i in range(8)])  32.9 us
    ppermute x9, waiting for transfers between devices, shifted(): lax.ppermute(value, axis, [(source, source + steps) for source in range(f...  29.6 us
    pallas_call x3, Pallas kernels, outer_call(): pl.pallas_call(partial(outer_sum, split_left), out_shape=tuple((jax.Shape...  23.1 us
    ppermute x9, starting transfers between devices, shifted(): lax.ppermute(value, axis, [(source, source + steps) for source in range(f...  17.7 us
  transfers between devices with their start and end apart: 45, of which 22 were waited for; matrix products, arithmetic and copies ran while one was open for 12% of the time, Pallas kernels for 23%

profile of v2, /device:TPU:10, one launch (start us, length us, event | category | flops | bytes accessed | tf_op | source)
XLA Modules:
  0.0 427.8 jit_solution(7308887851376065712)
XLA Ops:
  32.3 5.4 %shard_map.208 = (f32[160,1152]{1,0:T(8,128)}, f32[160,1024]{1,0:T(8,128)}, f32[160,1280]{1,0:T(8,128)}, f32[160,1024]{1,0:T(8,128)}, f32[160,1024]{1,0:T(8,128)}) custom-call(s32[1]{0:T(128)} %bitcast.282.flag, f32[480,8]{1,0:T(8,128)} %copy.605.refs_0_, f32[1,160]{1,0:T(1,128)} %get-tuple-element.1886.refs_1_, f32[8,128]{1,0:T(8,128)} %mul.9346.refs_2_, ...), custom_call_target="tpu_custom_call" | custom-call | flops 6794772480 | bytes 16777216 | tf_op jit(solution)/shard_map/pallas_call | solution.py:887
  39.0 5.0 %shard_map.207 = (f32[160,1152]{1,0:T(8,128)}, f32[160,1024]{1,0:T(8,128)}, f32[160,1280]{1,0:T(8,128)}, f32[160,1024]{1,0:T(8,128)}, f32[160,1024]{1,0:T(8,128)}) custom-call(s32[1]{0:T(128)} %bitcast.282.flag, f32[480,8]{1,0:T(8,128)} %copy.605.refs_0_, f32[1,160]{1,0:T(1,128)} %get-tuple-element.1887.refs_1_, f32[8,128]{1,0:T(8,128)} %mul.9346.refs_2_, ...), custom_call_target="tpu_custom_call" | custom-call | flops 6794772480 | bytes 16777216 | tf_op jit(solution)/shard_map/pallas_call | solution.py:887
  45.3 15.5 %collective-permute-done.103.refs_5_ = f32[160,1152]{1,0:T(8,128)S(1)} collective-permute-done((f32[160,1152]{1,0:T(8,128)}, f32[160,1152]{1,0:T(8,128)S(1)}, u32[]{:S(2)}, u32[]{:S(2)}) %collective-permute-start.103) | collective-permute-done | bytes 737312 | tf_op jit(solution)/shard_map/ppermute | solution.py:40
  61.8 28.0 %shard_map.209 = (f32[160,1152]{1,0:T(8,128)}, f32[160,1280]{1,0:T(8,128)}, f32[160,1024]{1,0:T(8,128)}, f32[160,1024]{1,0:T(8,128)}, f32[160,1024]{1,0:T(8,128)...) custom-call(s32[1]{0:T(128)S(6)} %sub.748.flag.chosen, ...), custom_call_target="tpu_custom_call" | custom-call | flops 10192158720 | bytes 16777216 | tf_op jit(solution)/shard_map/pallas_call | solution.py:887
  92.0 25.9 %shard_map.211 = (f32[160,1152]{1,0:T(8,128)}, f32[160,1280]{1,0:T(8,128)}, f32[160,1024]{1,0:T(8,128)}, f32[160,1024]{1,0:T(8,128)}, f32[160,1024]{1,0:T(8,128)...) custom-call(s32[1]{0:T(128)S(6)} %sub.748.flag.chosen, ...), custom_call_target="tpu_custom_call" | custom-call | flops 10192158720 | bytes 16777216 | tf_op jit(solution)/shard_map/pallas_call | solution.py:887
  120.0 4.8 %collective-permute-start.106 = (f32[160,1152]{1,0:T(8,128)}, f32[160,1152]{1,0:T(8,128)}, u32[]{:S(2)}, u32[]{:S(2)}) collective-permute-start(f32[160,1152]{1,0:T(8,128)} %get-tuple-element.982), channel_id=1, source_target_pairs={{16,0},{17,1},{18,2},{19,3},{20,4},{21,5},{22,6},{23,7},{24,8},{25... | collective-permute-start | bytes 2211848 | tf_op jit(solution)/shard_map/ppermute | solution.py:40
  124.8 26.5 %shard_map.213 = (f32[160,1152]{1,0:T(8,128)}, f32[160,1280]{1,0:T(8,128)}, f32[160,1024]{1,0:T(8,128)}, f32[160,1024]{1,0:T(8,128)}, f32[160,1024]{1,0:T(8,128)...) custom-call(s32[1]{0:T(128)S(6)} %sub.748.flag.chosen, ...), custom_call_target="tpu_custom_call" | custom-call | flops 10192158720 | bytes 16777216 | tf_op jit(solution)/shard_map/pallas_call | solution.py:887
  157.3 13.2 %collective-permute-done.108.refs_5_.refs_6_ = f32[160,1152]{1,0:T(8,128)} collective-permute-done((f32[160,1152]{1,0:T(8,128)}, f32[160,1152]{1,0:T(8,128)}, u32[]{:S(2)}, u32[]{:S(2)}) %collective-permute-start.108) | collective-permute-done | bytes 737312 | tf_op jit(solution)/shard_map/ppermute | solution.py:40
  170.5 7.0 %shard_map.214 = (f32[512,1024]{1,0:T(8,128)}, f32[512,1024]{1,0:T(8,128)}) custom-call(s32[1]{0:T(128)S(6)} %sub.748.flag.chosen, f32[160,1024]{1,0:T(8,128)} %get-tuple-element.989.refs_0_, f32[160,1024]{1,0:T(8,128)} %get-tuple-element.990.refs_1_, f32[160,1024]{1,0:T(8,128)} %get-tuple-element.991.refs_2_, f32[160,1152]{1,0:T(8,128)} %copy-done.342, ...), custom_call_target="tpu_custom_call" | custom-call | flops 3019898880 | bytes 16777216 | tf_op jit(solution)/shard_map/pallas_call | solution.py:901
  177.5 10.1 %shard_map.215 = (f32[160,128]{1,0:T(8,128)}, f32[160,1024]{1,0:T(8,128)}, f32[160,1024]{1,0:T(8,128)}, f32[160,128]{1,0:T(8,128)}, f32[16,1024]{1,0:T(8,128)}) custom-call(s32[1]{0:T(128)} %bitcast.282.flag, f32[480,8]{1,0:T(8,128)} %copy.605.refs_0_, f32[1,160]{1,0:T(1,128)} %get-tuple-element.1886.refs_1_, f32[8,128]{1,0:T(8,128)} %mul.9346.refs_2_, ...), custom_call_target="tpu_custom_call" | custom-call | flops 5096079360 | bytes 16777216 | tf_op jit(solution)/shard_map/pallas_call | solution.py:887
  187.6 9.2 %shard_map.216 = (f32[1280,512]{1,0:T(8,128)}, f32[1280,512]{1,0:T(8,128)}, f32[1024,128]{1,0:T(8,128)}) custom-call(s32[1]{0:T(128)S(6)} %sub.748.flag.chosen, f32[160,1280]{1,0:T(8,128)} %get-tuple-element.972.refs_4_.refs_0_, f32[160,1280]{1,0:T(8,128)} %get-tuple-element.973.refs_4_.refs_1_, f32[160,1280]{1,0:T(8,128)} %get-tuple-element.974.refs_4_.refs_2_, ...), custom_call_target="tpu_custom_call" | custom-call | flops 3019898880 | bytes 16777216 | tf_op jit(solution)/shard_map/pallas_call | solution.py:901
  196.9 6.9 %collective-permute-start.109 = (f32[32,1024]{1,0:T(8,128)S(1)}, f32[32,1024]{1,0:T(8,128)S(1)}, u32[]{:S(2)}, u32[]{:S(2)}) collective-permute-start(f32[32,1024]{1,0:T(8,128)S(1)} %pad_maximum_fusion.30), channel_id=1, source_target_pairs={{0,16},{16,0},{1,17},{17,1},{2,18},{18,2},{3,19},{19,3},{4,20},{20... | collective-permute-start | bytes 393224 | tf_op jit(solution)/shard_map/ppermute | solution.py:1164
  203.8 6.9 %shard_map.217 = (f32[1024,512]{1,0:T(8,128)}, f32[1024,512]{1,0:T(8,128)}) custom-call(s32[1]{0:T(128)S(6)} %sub.748.flag.chosen, f32[160,1024]{1,0:T(8,128)} %get-tuple-element.1016.refs_0_, f32[160,1024]{1,0:T(8,128)} %get-tuple-element.1017.refs_1_, f32[160,1024]{1,0:T(8,128)} %get-tuple-element.1018.refs_2_, f32[160,1024]{1,0:T(8,128)} %get-tuple-element.1019.refs_3_, ...), custom_call_target="tpu_custom_call" | custom-call | flops 3019898880 | bytes 16777216 | tf_op jit(solution)/shard_map/pallas_call | solution.py:901
  237.3 15.0 %collective-permute-done.137 = f32[256,1024]{1,0:T(8,128)S(1)} collective-permute-done((f32[256,1024]{1,0:T(8,128)S(1)}, f32[256,1024]{1,0:T(8,128)S(1)}, u32[]{:S(2)}, u32[]{:S(2)}) %collective-permute-start.137) | collective-permute-done | bytes 1048608 | tf_op jit(solution)/shard_map/ppermute | solution.py:1024
  252.6 12.3 %collective-permute-done.111 = f32[304,512]{1,0:T(8,128)S(1)} collective-permute-done((f32[304,512]{1,0:T(8,128)S(1)}, f32[304,512]{1,0:T(8,128)S(1)}, u32[]{:S(2)}, u32[]{:S(2)}) %collective-permute-start.111) | collective-permute-done | bytes 622624 | tf_op jit(solution)/shard_map/ppermute | solution.py:1024
  267.6 9.9 %collective-permute-done.131 = f32[320,512]{1,0:T(8,128)S(1)} collective-permute-done((f32[320,512]{1,0:T(8,128)S(1)}, f32[320,512]{1,0:T(8,128)S(1)}, u32[]{:S(2)}, u32[]{:S(2)}) %collective-permute-start.131) | collective-permute-done | bytes 655392 | tf_op jit(solution)/shard_map/ppermute | solution.py:1024
  277.5 16.7 %collective-permute-done.112 = f32[152,512]{1,0:T(8,128)S(1)} collective-permute-done((f32[152,512]{1,0:T(8,128)S(1)}, f32[152,512]{1,0:T(8,128)S(1)}, u32[]{:S(2)}, u32[]{:S(2)}) %collective-permute-start.112) | collective-permute-done | bytes 311328 | tf_op jit(solution)/shard_map/ppermute | solution.py:1024
  299.8 17.6 %collective-permute-done.113 = f32[152,512]{1,0:T(8,128)S(1)} collective-permute-done((f32[152,512]{1,0:T(8,128)S(1)}, f32[152,512]{1,0:T(8,128)S(1)}, u32[]{:S(2)}, u32[]{:S(2)}) %collective-permute-start.113) | collective-permute-done | bytes 311328 | tf_op jit(solution)/shard_map/ppermute | solution.py:1024
  331.1 21.5 %collective-permute-done.118 = f32[152,512]{1,0:T(8,128)S(1)} collective-permute-done((f32[152,512]{1,0:T(8,128)S(1)}, f32[152,512]{1,0:T(8,128)S(1)}, u32[]{:S(2)}, u32[]{:S(2)}) %collective-permute-start.118) | collective-permute-done | bytes 311328 | tf_op jit(solution)/shard_map/ppermute | solution.py:1024
  354.1 8.6 %collective-permute-done.139 = f32[128,1024]{1,0:T(8,128)S(1)} collective-permute-done((f32[128,1024]{1,0:T(8,128)S(1)}, f32[128,1024]{1,0:T(8,128)S(1)}, u32[]{:S(2)}, u32[]{:S(2)}) %collective-permute-start.139) | collective-permute-done | bytes 524320 | tf_op jit(solution)/shard_map/ppermute | solution.py:1024
  371.3 4.5 %collective-permute-done.119 = f32[152,512]{1,0:T(8,128)S(1)} collective-permute-done((f32[152,512]{1,0:T(8,128)S(1)}, f32[152,512]{1,0:T(8,128)S(1)}, u32[]{:S(2)}, u32[]{:S(2)}) %collective-permute-start.119) | collective-permute-done | bytes 311328 | tf_op jit(solution)/shard_map/ppermute | solution.py:1024
  378.8 6.9 %collective-permute-start.134 = (f32[160,512]{1,0:T(8,128)S(1)}, f32[160,512]{1,0:T(8,128)S(1)}, u32[]{:S(2)}, u32[]{:S(2)}) collective-permute-start(f32[160,512]{1,0:T(8,128)S(1)} %add.1916), channel_id=1, source_target_pairs={{0,4},{2,6},{4,0},{6,2},{8,12},{10,14},{12,8},{14,10},{1,5},{3,7},... | collective-permute-start | bytes 983048 | tf_op jit(solution)/shard_map/ppermute | solution.py:1024
  389.4 4.7 %collective-permute-done.130 = f32[320,512]{1,0:T(8,128)S(1)} collective-permute-done((f32[320,512]{1,0:T(8,128)S(1)}, f32[320,512]{1,0:T(8,128)S(1)}, u32[]{:S(2)}, u32[]{:S(2)}) %collective-permute-start.130) | collective-permute-done | bytes 655392 | tf_op jit(solution)/shard_map/ppermute | solution.py:1024
  396.1 11.3 %collective-permute-done.120 = f32[304,512]{1,0:T(8,128)S(1)} collective-permute-done((f32[304,512]{1,0:T(8,128)S(1)}, f32[304,512]{1,0:T(8,128)S(1)}, u32[]{:S(2)}, u32[]{:S(2)}) %collective-permute-start.120) | collective-permute-done | bytes 622624 | tf_op jit(solution)/shard_map/ppermute | solution.py:1024
  (268 shorter events, 131.8 us)
Async XLA Ops:
  3.6 25.4 %collective-permute-start.100 = (f32[1024,512]{1,0:T(8,128)}, f32[1024,512]{1,0:T(8,128)}, u32[]{:S(2)}, u32[]{:S(2)}) collective-permute-start(f32[1024,512]{1,0:T(8,128)} %bitcast.1902), channel_id=1, source_target_pairs={{0,1},{1,0},{2,3},{3,2},{4,5},{5,4},{6,7},{7,6},{8,9},{9,8},{10,11... | collective-permute-start | bytes 6291464 | tf_op jit(solution)/shard_map/ppermute | solution.py:44
  3.6 25.4 %collective-permute-start.102 = (f32[512,1024]{1,0:T(8,128)}, f32[512,1024]{1,0:T(8,128)}, u32[]{:S(2)}, u32[]{:S(2)}) collective-permute-start(f32[512,1024]{1,0:T(8,128)} %bitcast.2047), channel_id=1, source_target_pairs={{0,1},{1,0},{2,3},{3,2},{4,5},{5,4},{6,7},{7,6},{8,9},{9,8},{10,11... | collective-permute-start | bytes 6291464 | tf_op jit(solution)/shard_map/ppermute | solution.py:44
  31.0 29.8 %collective-permute-start.103 = (f32[160,1152]{1,0:T(8,128)}, f32[160,1152]{1,0:T(8,128)S(1)}, u32[]{:S(2)}, u32[]{:S(2)}) collective-permute-start(f32[160,1152]{1,0:T(8,128)} %get-tuple-element.975), channel_id=1, source_target_pairs={{0,16},{1,17},{2,18},{3,19},{4,20},{5,21},{6,22},{7,23},{8,24},{9,... | collective-permute-start | bytes 2211848 | tf_op jit(solution)/shard_map/ppermute | solution.py:40
  37.7 87.1 %collective-permute-start.107 = (f32[160,1152]{1,0:T(8,128)}, f32[160,1152]{1,0:T(8,128)}, u32[]{:S(2)}, u32[]{:S(2)}) collective-permute-start(f32[160,1152]{1,0:T(8,128)} %get-tuple-element.985), channel_id=1, source_target_pairs={{0,16},{1,17},{2,18},{3,19},{4,20},{5,21},{6,22},{7,23},{8,24},{9,... | collective-permute-start | bytes 2211848 | tf_op jit(solution)/shard_map/ppermute | solution.py:40
  44.0 48.0 %collective-permute-start.105 = (f32[160,1152]{1,0:T(8,128)}, f32[160,1152]{1,0:T(8,128)}, u32[]{:S(2)}, u32[]{:S(2)}) collective-permute-start(f32[160,1152]{1,0:T(8,128)} %get-tuple-element.979), channel_id=1, source_target_pairs={{0,16},{1,17},{2,18},{3,19},{4,20},{5,21},{6,22},{7,23},{8,24},{9,... | collective-permute-start | bytes 2211848 | tf_op jit(solution)/shard_map/ppermute | solution.py:40
  89.7 28.2 %collective-permute-start.104 = (f32[160,1152]{1,0:T(8,128)}, f32[160,1152]{1,0:T(8,128)S(1)}, u32[]{:S(2)}, u32[]{:S(2)}) collective-permute-start(f32[160,1152]{1,0:T(8,128)} %get-tuple-element.976), channel_id=1, source_target_pairs={{16,0},{17,1},{18,2},{19,3},{20,4},{21,5},{22,6},{23,7},{24,8},{25... | collective-permute-start | bytes 2211848 | tf_op jit(solution)/shard_map/ppermute | solution.py:40
  120.0 33.1 %collective-permute-start.106 = (f32[160,1152]{1,0:T(8,128)}, f32[160,1152]{1,0:T(8,128)}, u32[]{:S(2)}, u32[]{:S(2)}) collective-permute-start(f32[160,1152]{1,0:T(8,128)} %get-tuple-element.982), channel_id=1, source_target_pairs={{16,0},{17,1},{18,2},{19,3},{20,4},{21,5},{22,6},{23,7},{24,8},{25... | collective-permute-start | bytes 2211848 | tf_op jit(solution)/shard_map/ppermute | solution.py:40
  226.2 26.1 %collective-permute-start.137 = (f32[256,1024]{1,0:T(8,128)S(1)}, f32[256,1024]{1,0:T(8,128)S(1)}, u32[]{:S(2)}, u32[]{:S(2)}) collective-permute-start(f32[256,1024]{1,0:T(8,128)S(1)} %constant_dynamic-slice_fusion.103), channel_id=1, source_target_pairs={{0,4},{2,6},{4,0},{6,2},{8,12},{10,14},{12,8},{14,10},{1,5},{3,7},... | collective-permute-start | bytes 3145736 | tf_op jit(solution)/shard_map/ppermute | solution.py:1024
  230.7 34.2 %collective-permute-start.111 = (f32[304,512]{1,0:T(8,128)S(1)}, f32[304,512]{1,0:T(8,128)S(1)}, u32[]{:S(2)}, u32[]{:S(2)}) collective-permute-start(f32[304,512]{1,0:T(8,128)S(1)} %constant_dynamic-slice_fusion.111), channel_id=1, source_target_pairs={{0,4},{2,6},{4,0},{6,2},{8,12},{10,14},{12,8},{14,10},{1,5},{3,7},... | collective-permute-start | bytes 1867784 | tf_op jit(solution)/shard_map/ppermute | solution.py:1024
  232.2 32.9 %collective-permute-start.116 = (f32[304,512]{1,0:T(8,128)S(1)}, f32[304,512]{1,0:T(8,128)S(1)}, u32[]{:S(2)}, u32[]{:S(2)}) collective-permute-start(f32[304,512]{1,0:T(8,128)S(1)} %constant_dynamic-slice_fusion.109), channel_id=1, source_target_pairs={{0,2},{2,0},{4,6},{6,4},{8,10},{10,8},{12,14},{14,12},{1,3},{3,1},... | collective-permute-start | bytes 1867784 | tf_op jit(solution)/shard_map/ppermute | solution.py:1024
  235.1 31.9 %collective-permute-start.126 = (f32[320,512]{1,0:T(8,128)S(1)}, f32[320,512]{1,0:T(8,128)S(1)}, u32[]{:S(2)}, u32[]{:S(2)}) collective-permute-start(f32[320,512]{1,0:T(8,128)S(1)} %constant_dynamic-slice_fusion.107), channel_id=1, source_target_pairs={{0,2},{2,0},{4,6},{6,4},{8,10},{10,8},{12,14},{14,12},{1,3},{3,1},... | collective-permute-start | bytes 1966088 | tf_op jit(solution)/shard_map/ppermute | solution.py:1024
  237.2 40.2 %collective-permute-start.131 = (f32[320,512]{1,0:T(8,128)S(1)}, f32[320,512]{1,0:T(8,128)S(1)}, u32[]{:S(2)}, u32[]{:S(2)}) collective-permute-start(f32[320,512]{1,0:T(8,128)S(1)} %constant_dynamic-slice_fusion.105), channel_id=1, source_target_pairs={{0,2},{2,0},{4,6},{6,4},{8,10},{10,8},{12,14},{14,12},{1,3},{3,1},... | collective-permute-start | bytes 1966088 | tf_op jit(solution)/shard_map/ppermute | solution.py:1024
  252.5 67.6 %collective-permute-start.138 = (f32[128,1024]{1,0:T(8,128)S(1)}, f32[128,1024]{1,0:T(8,128)S(1)}, u32[]{:S(2)}, u32[]{:S(2)}) collective-permute-start(f32[128,1024]{1,0:T(8,128)S(1)} %constant_dynamic-slice_fusion.102), channel_id=1, source_target_pairs={{0,2},{2,0},{4,6},{6,4},{8,10},{10,8},{12,14},{14,12},{1,3},{3,1},... | collective-permute-start | bytes 1572872 | tf_op jit(solution)/shard_map/ppermute | solution.py:1024
  265.0 29.2 %collective-permute-start.112 = (f32[152,512]{1,0:T(8,128)S(1)}, f32[152,512]{1,0:T(8,128)S(1)}, u32[]{:S(2)}, u32[]{:S(2)}) collective-permute-start(f32[152,512]{1,0:T(8,128)S(1)} %constant_dynamic-slice_fusion.110), channel_id=1, source_target_pairs={{0,2},{2,0},{4,6},{6,4},{8,10},{10,8},{12,14},{14,12},{1,3},{3,1},... | collective-permute-start | bytes 933896 | tf_op jit(solution)/shard_map/ppermute | solution.py:1024
  265.2 52.9 %collective-permute-start.117 = (f32[152,512]{1,0:T(8,128)S(1)}, f32[152,512]{1,0:T(8,128)S(1)}, u32[]{:S(2)}, u32[]{:S(2)}) collective-permute-start(f32[152,512]{1,0:T(8,128)S(1)} %constant_dynamic-slice_fusion.108), channel_id=1, source_target_pairs={{0,4},{2,6},{4,0},{6,2},{8,12},{10,14},{12,8},{14,10},{1,5},{3,7},... | collective-permute-start | bytes 933896 | tf_op jit(solution)/shard_map/ppermute | solution.py:1024
  267.2 32.4 %collective-permute-start.127 = (f32[160,512]{1,0:T(8,128)S(1)}, f32[160,512]{1,0:T(8,128)S(1)}, u32[]{:S(2)}, u32[]{:S(2)}) collective-permute-start(f32[160,512]{1,0:T(8,128)S(1)} %constant_dynamic-slice_fusion.106), channel_id=1, source_target_pairs={{0,4},{2,6},{4,0},{6,2},{8,12},{10,14},{12,8},{14,10},{1,5},{3,7},... | collective-permute-start | bytes 983048 | tf_op jit(solution)/shard_map/ppermute | solution.py:1024
  297.4 31.6 %collective-permute-start.122 = (f32[3,1152]{1,0:T(4,128)S(1)}, f32[3,1152]{1,0:T(4,128)S(1)}, u32[]{:S(2)}, u32[]{:S(2)}) collective-permute-start(f32[3,1152]{1,0:T(4,128)S(1)} %get-tuple-element.1884), channel_id=1, source_target_pairs={{0,2},{2,4},{4,6},{6,8},{8,10},{10,12},{12,14},{1,3},{3,5},{5,7},{... | collective-permute-start | bytes 41480 | tf_op jit(solution)/shard_map/ppermute | solution.py:40
  320.2 32.5 %collective-permute-start.132 = (f32[160,512]{1,0:T(8,128)S(1)}, f32[160,512]{1,0:T(8,128)S(1)}, u32[]{:S(2)}, u32[]{:S(2)}) collective-permute-start(f32[160,512]{1,0:T(8,128)S(1)} %constant_dynamic-slice_fusion.104), channel_id=1, source_target_pairs={{0,4},{2,6},{4,0},{6,2},{8,12},{10,14},{12,8},{14,10},{1,5},{3,7},... | collective-permute-start | bytes 983048 | tf_op jit(solution)/shard_map/ppermute | solution.py:1024
  324.2 28.4 %collective-permute-start.118 = (f32[152,512]{1,0:T(8,128)S(1)}, f32[152,512]{1,0:T(8,128)S(1)}, u32[]{:S(2)}, u32[]{:S(2)}) collective-permute-start(f32[152,512]{1,0:T(8,128)S(1)} %dynamic-slice_add_fusion.8), channel_id=1, source_target_pairs={{0,12},{2,14},{4,8},{6,10},{8,4},{10,6},{12,0},{14,2},{1,13},{3,15... | collective-permute-start | bytes 933896 | tf_op jit(solution)/shard_map/ppermute | solution.py:1024
  327.1 35.6 %collective-permute-start.139 = (f32[128,1024]{1,0:T(8,128)S(1)}, f32[128,1024]{1,0:T(8,128)S(1)}, u32[]{:S(2)}, u32[]{:S(2)}) collective-permute-start(f32[128,1024]{1,0:T(8,128)S(1)} %dynamic-slice_add_fusion.5), channel_id=1, source_target_pairs={{0,12},{2,14},{4,8},{6,10},{8,4},{10,6},{12,0},{14,2},{1,13},{3,15... | collective-permute-start | bytes 1572872 | tf_op jit(solution)/shard_map/ppermute | solution.py:1024
  329.0 35.6 %collective-permute-start.129 = (f32[160,512]{1,0:T(8,128)S(1)}, f32[160,512]{1,0:T(8,128)S(1)}, u32[]{:S(2)}, u32[]{:S(2)}) collective-permute-start(f32[160,512]{1,0:T(8,128)S(1)} %add.1911), channel_id=1, source_target_pairs={{0,4},{2,6},{4,0},{6,2},{8,12},{10,14},{12,8},{14,10},{1,5},{3,7},... | collective-permute-start | bytes 983048 | tf_op jit(solution)/shard_map/ppermute | solution.py:1024
  329.0 40.2 %collective-permute-start.115 = (f32[304,512]{1,0:T(8,128)S(1)}, f32[304,512]{1,0:T(8,128)S(1)}, u32[]{:S(2)}, u32[]{:S(2)}) collective-permute-start(f32[304,512]{1,0:T(8,128)S(1)} %get-tuple-element.1607), channel_id=1, source_target_pairs={{0,4},{2,6},{4,0},{6,2},{8,12},{10,14},{12,8},{14,10},{1,5},{3,7},... | collective-permute-start | bytes 1867784 | tf_op jit(solution)/shard_map/ppermute | solution.py:1024
  376.0 31.4 %collective-permute-start.120 = (f32[304,512]{1,0:T(8,128)S(1)}, f32[304,512]{1,0:T(8,128)S(1)}, u32[]{:S(2)}, u32[]{:S(2)}) collective-permute-start(f32[304,512]{1,0:T(8,128)S(1)} %get-tuple-element.1605), channel_id=1, source_target_pairs={{0,2},{2,0},{4,6},{6,4},{8,10},{10,8},{12,14},{14,12},{1,3},{3,1},... | collective-permute-start | bytes 1867784 | tf_op jit(solution)/shard_map/ppermute | solution.py:1024
  386.7 35.5 %collective-permute-start.141 = (f32[256,1024]{1,0:T(8,128)}, f32[256,1024]{1,0:T(8,128)}, u32[]{:S(2)}, u32[]{:S(2)}) collective-permute-start(f32[256,1024]{1,0:T(8,128)} %maximum_select_fusion.50), channel_id=1, source_target_pairs={{0,4},{2,6},{4,0},{6,2},{8,12},{10,14},{12,8},{14,10},{1,5},{3,7},... | collective-permute-start | bytes 3145736 | tf_op jit(solution)/shard_map/ppermute | solution.py:1024
  (42 other events, 510.1 us)

commit v3 on v2

--- a/solution.py
+++ b/solution.py
@@ -368,7 +368,15 @@
     )
 
 
-CHUNKS = (160, 160, 160)
+CHUNKS = (128, 192, 160)
+PLAN = (
+    (0, 0, 256, 2, 1), (0, 256, 256, 1, 2), (1, 0, 640, 1, 2), (1, 640, 640, 1, 2), (2, 0, 608, 2, 1),
+    (2, 608, 608, 1, 2),
+)
+EARLY = (0, 1)
+ORDER = (
+    0, 2, 4, 5, 2, 1, 2, 4, 3, 1, 5, 0, 4, 3, 2, 5, 1, 3, 4, 2, 5, 3, 0, 5, 3, 4, 2, 1, 5, 0, 3, 4,
+)
 LANES = 128
 F32 = jnp.float32
 BF16 = jnp.bfloat16
@@ -1034,27 +1042,50 @@
     return jnp.where(second == 0, jnp.concatenate([kept, got]), jnp.concatenate([got, kept]))
 
 
-def sum_piece(value, outer_hop, inner_hop):
+def sum_steps(value, outer_hop, inner_hop, wait):
     index = lax.axis_index("edge")
     seconds = {1: index % 2, 2: ((index // 2) ^ (index // 4)) % 2}
     kept, given = halves(value, seconds[outer_hop])
-    kept, given = halves(kept + hop(given, outer_hop), seconds[inner_hop])
-    part = kept + hop(given, inner_hop)
-    part = part + hop(part, 6)
-    part = joined(part, hop(part, inner_hop), seconds[inner_hop])
+    given = wait(given)
+    got = hop(given, outer_hop)
+    yield given
+    kept, given = halves(kept + wait(got), seconds[inner_hop])
+    got = hop(given, inner_hop)
+    yield given
+    part = kept + wait(got)
+    got = hop(part, 6)
+    yield part
+    part = part + wait(got)
+    got = hop(part, inner_hop)
+    yield part
+    part = joined(part, wait(got), seconds[inner_hop])
     half = part.shape[0]
-    return [(part, seconds[outer_hop] * half), (hop(part, outer_hop), (1 - seconds[outer_hop]) * half)]
-
-
-def sum_blocks(matrices, plan):
-    if lax.axis_size("edge") != 8:
-        return [lax.psum(value, "edge") for value in matrices]
-    sums = [jnp.zeros_like(value) for value in matrices]
-    for which, first, rows, outer_hop, inner_hop in plan:
-        piece = lax.slice_in_dim(matrices[which], first, first + rows, axis=0)
-        for part, start in sum_piece(piece, outer_hop, inner_hop):
-            sums[which] = lax.dynamic_update_slice_in_dim(sums[which], part, first + start, 0)
-    return sums
+    got = hop(part, outer_hop)
+    yield part
+    yield [(part, seconds[outer_hop] * half), (wait(got), (1 - seconds[outer_hop]) * half)]
+
+
+class BlockSums:
+    def __init__(self, plan):
+        self.plan, self.steps, self.sums, self.moment = plan, {}, {}, None
+
+    def wait(self, value):
+        return value if self.moment is None else tied(value, self.moment)
+
+    def advance(self, matrices, order):
+        for piece in order:
+            which, first, rows, outer_hop, inner_hop = self.plan[piece]
+            if piece not in self.steps:
+                value = lax.slice_in_dim(matrices[which], first, first + rows, axis=0)
+                self.steps[piece] = sum_steps(value, outer_hop, inner_hop, self.wait)
+            given = next(self.steps[piece])
+            if isinstance(given, list):
+                total = self.sums.get(which, jnp.zeros_like(matrices[which]))
+                for part, start in given:
+                    total = lax.dynamic_update_slice_in_dim(total, part, first + start, 0)
+                self.sums[which] = total
+                given = given[1][0]
+            self.moment = given
 
 
 def fast_device(edges, place, others, args):
@@ -1113,6 +1144,8 @@
             )
         )
     outer_work = 6 * sum(CHUNKS) * width * width
+    by_hand = lax.axis_size("edge") == 8
+    sums = BlockSums(PLAN)
     for k, m in enumerate(CHUNKS):
         back = seconds[k][0] if k == 0 else tied(seconds[k][0], firsts[k - 1][0])
         returned.append(shifted(back, "section", -1))
@@ -1124,6 +1157,9 @@
                 ([s[3] for s in seconds], [s[4] for s in seconds]),
             )
             arrived = tied(arrived, out_other)
+            grad_out = out_own + other_core(out_other)
+            if by_hand:
+                sums.advance([grad_out], EARLY)
         outs = [(m, LANES), (m, width), (m, width), (m, LANES), (16, width)]
         work = 9 * m * width * (3 * width + 384)
         firsts.append(
@@ -1133,16 +1169,18 @@
                 (saved[k][1], env_w, arrived, *outs_w, saved[k][2], *ins, env_wt, *heads), first_flag,
             )
         )
-    grad_out = out_own + other_core(out_other)
     in_own, in_other, grad_env = outer_call(
         False, [(layer_width, half)] * 2 + [(width, LANES)], (layer_width, width, LANES), outer_work,
-        second_flag,
+        sums.wait(second_flag),
         ([s[1] for s in saved], [f[2] for f in firsts], [f[3] for f in firsts]),
         ([s[1] for s in seconds], [s[2] for s in seconds], [s[7] for s in seconds]),
     )
     grad_in = in_own + other_core(in_other)
+    if by_hand:
+        sums.moment = (sums.moment, in_other)
+        sums.advance([grad_out], EARLY)
     head_own, head_other = outer_call(
-        False, [(width, half)] * 2, (width, width), outer_work, tied(second_flag, in_other),
+        False, [(width, half)] * 2, (width, width), outer_work, tied(second_flag, in_other, sums.moment),
         ([s[0] for s in saved], [f[1] for f in firsts]),
         ([s[5] for s in seconds], [s[6] for s in seconds]),
     )
@@ -1165,13 +1203,27 @@
     small = jnp.concatenate([small, grad_env[:, :chan_count].reshape(-1, width)]).reshape(-1, half)
     head_own = jnp.concatenate([head_own, small])
     grad_head = head_own + other_core(jnp.concatenate([head_other, small]))
-    grad_out, grad_in, grad_head = sum_blocks(
-        [grad_out, grad_in, grad_head],
-        [
-            (0, 0, 512, 2, 1), (1, 0, 640, 1, 2), (1, 640, 640, 1, 2), (2, 0, 608, 2, 1),
-            (2, 608, 608, 1, 2),
-        ],
-    )
+    total = sum(CHUNKS)
+    hot = (place[None, :] == jnp.arange(total, dtype=F32)[:, None]).astype(F32)
+    d_vectors = jnp.concatenate([f[0][:, :8] for f in firsts])
+    spread = lax.dot_general(d_vectors, hot, (((0,), (0,)), ((), ())), precision=HIGHEST)[:3]
+    spread = jnp.where(is_first, spread, none)
+    if by_hand:
+        matrices = [grad_out, grad_in, grad_head]
+        sums.moment = (sums.moment, head_other, grad_in, grad_head)
+        sums.advance(matrices, ORDER[:8])
+        spread = sums.wait(spread)
+        spread = spread + other_core(spread)
+        sums.advance(matrices, ORDER[8:16])
+        spread = sums.wait(spread)
+        sums.advance(matrices, ORDER[16:])
+        grad_out, grad_in, grad_head = (sums.sums[i] for i in range(3))
+    else:
+        spread = spread + other_core(spread)
+        grad_out, grad_in, grad_head = lax.psum((grad_out, grad_in, grad_head), "edge")
+    per_block = batch_count * edge_count
+    to_left, kept, to_right = (spread[:, i * per_block : (i + 1) * per_block] for i in range(3))
+    forces = kept + shifted(to_right, "edge", 1) + shifted(to_left, "edge", -1)
     small = grad_head[width:].reshape(-1, width)
     grad_head = grad_head[:width]
     grad_embed, grad_read = small[:16], small[16]
@@ -1179,15 +1231,6 @@
     grad_mix = small[18 : 18 + mix_sum.shape[0]].reshape(mix_weight.shape)
     grad_env = small[32:].reshape(width, chan_count)
 
-    d_vectors = jnp.concatenate([f[0][:, :8] for f in firsts])
-    total = sum(CHUNKS)
-    hot = (place[None, :] == jnp.arange(total, dtype=F32)[:, None]).astype(F32)
-    spread = lax.dot_general(d_vectors, hot, (((0,), (0,)), ((), ())), precision=HIGHEST)[:3]
-    spread = jnp.where(is_first, spread, none)
-    spread = spread + other_core(spread)
-    per_block = batch_count * edge_count
-    to_left, kept, to_right = (spread[:, i * per_block : (i + 1) * per_block] for i in range(3))
-    forces = kept + shifted(to_right, "edge", 1) + shifted(to_left, "edge", -1)
     forces = jnp.where(is_first, forces, shifted(forces, "section", 1))
     forces = -forces.reshape(3, batch_count, edge_count).transpose(1, 0, 2)
     return (

time: 434 us -> 429 us (0.988)
  the two profiles are of different devices: /device:TPU:10 before, /device:TPU:0 now
where the time goes in v3:
time: 429 us; the launch traced here: 423 us
  waiting for transfers between devices  142 us (33%)
  Pallas kernels  127 us (30%)
  starting transfers between devices  76.3 us (18%)
  local copies, waits for them, and re-layouts  39.9 us (9%)
  other arithmetic  28.6 us (7%)
  matrix products  5.46 us (1%)
    pallas_call x9, Pallas kernels, on_core(): pl.pallas_call(guarded, out_shape=tuple((jax.ShapeDtypeStruct(shape, F32)...  103 us
    ppermute x30, waiting for transfers between devices, hop(): return lax.ppermute(value, 'edge', [(i, i ^ distance) for i in range(8)])  96.1 us
    ppermute x30, starting transfers between devices, hop(): return lax.ppermute(value, 'edge', [(i, i ^ distance) for i in range(8)])  47.6 us
    ppermute x9, waiting for transfers between devices, shifted(): lax.ppermute(value, axis, [(source, source + steps) for source in range(f...  37 us
    pallas_call x3, Pallas kernels, outer_call(): pl.pallas_call(partial(outer_sum, split_left), out_shape=tuple((jax.Shape...  22.9 us
    ppermute x9, starting transfers between devices, shifted(): lax.ppermute(value, axis, [(source, source + steps) for source in range(f...  20.5 us
  transfers between devices with their start and end apart: 50, of which 19 were waited for; matrix products, arithmetic and copies ran while one was open for 13% of the time, Pallas kernels for 22%

profile of v3, /device:TPU:0, one launch (start us, length us, event | category | flops | bytes accessed | tf_op | source)
XLA Modules:
  0.0 423.1 jit_solution(10602308830545736190)
XLA Ops:
  32.2 11.6 %shard_map.206 = (f32[128,1152]{1,0:T(8,128)}, f32[128,1024]{1,0:T(8,128)}, f32[128,1280]{1,0:T(8,128)}, f32[128,1024]{1,0:T(8,128)}, f32[128,1024]{1,0:T(8,128)}) custom-call(s32[1]{0:T(128)} %bitcast.282.flag, f32[480,8]{1,0:T(8,128)} %copy.605.refs_0_, f32[1,128]{1,0:T(1,128)} %slice_bitcast_fusion.57.refs_1_, f32[8,128]{1,0:T(8,128)} %mul.9360.refs_2_, ...), custom_call_target="tpu_custom_call" | custom-call | flops 5435817984 | bytes 16777216 | tf_op jit(solution)/shard_map/pallas_call | solution.py:895
  45.2 15.8 %shard_map.207 = (f32[192,1152]{1,0:T(8,128)}, f32[192,1024]{1,0:T(8,128)}, f32[192,1280]{1,0:T(8,128)}, f32[192,1024]{1,0:T(8,128)}, f32[192,1024]{1,0:T(8,128)}) custom-call(s32[1]{0:T(128)} %bitcast.282.flag, f32[480,8]{1,0:T(8,128)} %copy.605.refs_0_, f32[1,192]{1,0:T(1,128)} %slice_bitcast_fusion.56.refs_1_, f32[8,128]{1,0:T(8,128)} %mul.9360.refs_2_, ...), custom_call_target="tpu_custom_call" | custom-call | flops 8153726976 | bytes 16777216 | tf_op jit(solution)/shard_map/pallas_call | solution.py:895
  63.3 13.4 %shard_map.208 = (f32[160,1152]{1,0:T(8,128)}, f32[160,1024]{1,0:T(8,128)}, f32[160,1280]{1,0:T(8,128)}, f32[160,1024]{1,0:T(8,128)}, f32[160,1024]{1,0:T(8,128)}) custom-call(s32[1]{0:T(128)} %bitcast.282.flag, f32[480,8]{1,0:T(8,128)} %copy.605.refs_0_, f32[1,160]{1,0:T(1,128)} %slice_bitcast_fusion.55.refs_1_, f32[8,128]{1,0:T(8,128)} %mul.9360.refs_2_, ...), custom_call_target="tpu_custom_call" | custom-call | flops 6794772480 | bytes 16777216 | tf_op jit(solution)/shard_map/pallas_call | solution.py:895
  82.7 9.1 %shard_map.210 = (f32[192,1152]{1,0:T(8,128)}, f32[192,1280]{1,0:T(8,128)}, f32[192,1024]{1,0:T(8,128)}, f32[192,1024]{1,0:T(8,128)}, f32[192,1024]{1,0:T(8,128)...) custom-call(s32[1]{0:T(128)S(6)} %sub.753.flag.chosen, ...), custom_call_target="tpu_custom_call" | custom-call | flops 12230590464 | bytes 16777216 | tf_op jit(solution)/shard_map/pallas_call | solution.py:895
  98.5 12.2 %shard_map.211 = (f32[128,128]{1,0:T(8,128)}, f32[128,1024]{1,0:T(8,128)}, f32[128,1024]{1,0:T(8,128)}, f32[128,128]{1,0:T(8,128)}, f32[16,1024]{1,0:T(8,128)}) custom-call(s32[1]{0:T(128)} %bitcast.282.flag, f32[480,8]{1,0:T(8,128)} %copy.605.refs_0_, f32[1,128]{1,0:T(1,128)} %slice_bitcast_fusion.57.refs_1_, f32[8,128]{1,0:T(8,128)} %mul.9360.refs_2_, ...), custom_call_target="tpu_custom_call" | custom-call | flops 4076863488 | bytes 16777216 | tf_op jit(solution)/shard_map/pallas_call | solution.py:895
  112.0 9.3 %shard_map.212 = (f32[160,1152]{1,0:T(8,128)}, f32[160,1280]{1,0:T(8,128)}, f32[160,1024]{1,0:T(8,128)}, f32[160,1024]{1,0:T(8,128)}, f32[160,1024]{1,0:T(8,128)...) custom-call(s32[1]{0:T(128)S(6)} %sub.753.flag.chosen, ...), custom_call_target="tpu_custom_call" | custom-call | flops 10192158720 | bytes 16777216 | tf_op jit(solution)/shard_map/pallas_call | solution.py:895
  121.3 14.2 %collective-permute-done.106.refs_6_.refs_4_ = f32[192,1152]{1,0:T(8,128)S(1)} collective-permute-done((f32[192,1152]{1,0:T(8,128)}, f32[192,1152]{1,0:T(8,128)S(1)}, u32[]{:S(2)}, u32[]{:S(2)}) %collective-permute-start.106) | collective-permute-done | bytes 884768 | tf_op jit(solution)/shard_map/ppermute | solution.py:40
  136.5 15.6 %shard_map.213 = (f32[192,128]{1,0:T(8,128)}, f32[192,1024]{1,0:T(8,128)}, f32[192,1024]{1,0:T(8,128)}, f32[192,128]{1,0:T(8,128)}, f32[16,1024]{1,0:T(8,128)}) custom-call(s32[1]{0:T(128)} %bitcast.282.flag, f32[480,8]{1,0:T(8,128)} %copy.605.refs_0_, f32[1,192]{1,0:T(1,128)} %slice_bitcast_fusion.56.refs_1_, f32[8,128]{1,0:T(8,128)} %mul.9360.refs_2_, ...), custom_call_target="tpu_custom_call" | custom-call | flops 6115295232 | bytes 16777216 | tf_op jit(solution)/shard_map/pallas_call | solution.py:895
  153.8 16.9 %collective-permute-done.108.refs_5_.refs_6_ = f32[160,1152]{1,0:T(8,128)} collective-permute-done((f32[160,1152]{1,0:T(8,128)}, f32[160,1152]{1,0:T(8,128)}, u32[]{:S(2)}, u32[]{:S(2)}) %collective-permute-start.108) | collective-permute-done | bytes 737312 | tf_op jit(solution)/shard_map/ppermute | solution.py:40
  170.7 6.9 %shard_map.214 = (f32[512,1024]{1,0:T(8,128)}, f32[512,1024]{1,0:T(8,128)}) custom-call(s32[1]{0:T(128)S(6)} %sub.753.flag.chosen, f32[128,1024]{1,0:T(8,128)} %get-tuple-element.1010.refs_0_, f32[192,1024]{1,0:T(8,128)} %get-tuple-element.1011.refs_1_, f32[160,1024]{1,0:T(8,128)} %get-tuple-element.1012.refs_2_, f32[128,1152]{1,0:T(8,128)} %copy-done.272, ...), custom_call_target="tpu_custom_call" | custom-call | flops 3019898880 | bytes 16777216 | tf_op jit(solution)/shard_map/pallas_call | solution.py:909
  179.3 14.3 %shard_map.215 = (f32[160,128]{1,0:T(8,128)}, f32[160,1024]{1,0:T(8,128)}, f32[160,1024]{1,0:T(8,128)}, f32[160,128]{1,0:T(8,128)}, f32[16,1024]{1,0:T(8,128)}) custom-call(s32[1]{0:T(128)} %bitcast.282.flag, f32[480,8]{1,0:T(8,128)} %copy.605.refs_0_, f32[1,160]{1,0:T(1,128)} %slice_bitcast_fusion.55.refs_1_, f32[8,128]{1,0:T(8,128)} %mul.9360.refs_2_, ...), custom_call_target="tpu_custom_call" | custom-call | flops 5096079360 | bytes 16777216 | tf_op jit(solution)/shard_map/pallas_call | solution.py:895
  205.5 9.1 %shard_map.216 = (f32[1280,512]{1,0:T(8,128)}, f32[1280,512]{1,0:T(8,128)}, f32[1024,128]{1,0:T(8,128)}) custom-call(s32[1]{0:T(128)S(6)} %sub.753.flag.chosen, f32[128,1280]{1,0:T(8,128)} %get-tuple-element.1017.refs_4_.refs_0_, f32[192,1280]{1,0:T(8,128)} %get-tuple-element.1023.refs_4_.refs_1_, f32[160,1280]{1,0:T(8,128)} %get-tuple-element.1037.refs_4_.refs_2_, ...), custom_call_target="tpu_custom_call" | custom-call | flops 3019898880 | bytes 16777216 | tf_op jit(solution)/shard_map/pallas_call | solution.py:909
  222.3 6.9 %shard_map.217 = (f32[1024,512]{1,0:T(8,128)}, f32[1024,512]{1,0:T(8,128)}) custom-call(s32[1]{0:T(128)S(6)} %sub.753.flag.chosen, f32[128,1024]{1,0:T(8,128)} %get-tuple-element.1059.refs_0_, f32[192,1024]{1,0:T(8,128)} %get-tuple-element.1060.refs_1_, f32[160,1024]{1,0:T(8,128)} %get-tuple-element.1061.refs_2_, f32[128,1024]{1,0:T(8,128)} %get-tuple-element.1062.refs_3_, ...), custom_call_target="tpu_custom_call" | custom-call | flops 3019898880 | bytes 16777216 | tf_op jit(solution)/shard_map/pallas_call | solution.py:909
  253.4 7.7 %collective-permute-done.118 = f32[320,512]{1,0:T(8,128)} collective-permute-done((f32[320,512]{1,0:T(8,128)}, f32[320,512]{1,0:T(8,128)}, u32[]{:S(2)}, u32[]{:S(2)}) %collective-permute-start.118) | collective-permute-done | bytes 655392 | tf_op jit(solution)/shard_map/ppermute | solution.py:1032
  268.9 8.9 %collective-permute-done.121 = f32[160,512]{1,0:T(8,128)S(1)} collective-permute-done((f32[160,512]{1,0:T(8,128)S(1)}, f32[160,512]{1,0:T(8,128)S(1)}, u32[]{:S(2)}, u32[]{:S(2)}) %collective-permute-start.121) | collective-permute-done | bytes 327712 | tf_op jit(solution)/shard_map/ppermute | solution.py:1032
  280.8 9.2 %collective-permute-start.126 = (f32[64,1024]{1,0:T(8,128)S(1)}, f32[64,1024]{1,0:T(8,128)S(1)}, u32[]{:S(2)}, u32[]{:S(2)}) collective-permute-start(f32[64,1024]{1,0:T(8,128)S(1)} %dynamic-slice_add_fusion.11), channel_id=1, source_target_pairs={{0,12},{2,14},{4,8},{6,10},{8,4},{10,6},{12,0},{14,2},{1,13},{3,15... | collective-permute-start | bytes 786440 | tf_op jit(solution)/shard_map/ppermute | solution.py:1032
  302.9 7.2 %collective-permute-start.129 = (f32[152,512]{1,0:T(8,128)S(1)}, f32[152,512]{1,0:T(8,128)S(1)}, u32[]{:S(2)}, u32[]{:S(2)}) collective-permute-start(f32[152,512]{1,0:T(8,128)S(1)} %dynamic-slice_add_fusion.8), channel_id=1, source_target_pairs={{0,12},{2,14},{4,8},{6,10},{8,4},{10,6},{12,0},{14,2},{1,13},{3,15... | collective-permute-start | bytes 933896 | tf_op jit(solution)/shard_map/ppermute | solution.py:1032
  310.4 7.7 %collective-permute-done.123 = f32[160,512]{1,0:T(8,128)S(1)} collective-permute-done((f32[160,512]{1,0:T(8,128)S(1)}, f32[160,512]{1,0:T(8,128)S(1)}, u32[]{:S(2)}, u32[]{:S(2)}) %collective-permute-start.123) | collective-permute-done | bytes 327712 | tf_op jit(solution)/shard_map/ppermute | solution.py:1032
  320.1 6.9 %collective-permute-start.144 = (f32[3,1152]{1,0:T(4,128)S(1)}, f32[3,1152]{1,0:T(4,128)S(1)}, u32[]{:S(2)}, u32[]{:S(2)}) collective-permute-start(f32[3,1152]{1,0:T(4,128)S(1)} %get-tuple-element.1958), channel_id=1, source_target_pairs={{0,2},{2,4},{4,6},{6,8},{8,10},{10,12},{12,14},{1,3},{3,5},{5,7},{... | collective-permute-start | bytes 41480 | tf_op jit(solution)/shard_map/ppermute | solution.py:40
  341.2 10.7 %collective-permute-done.128 = f32[160,512]{1,0:T(8,128)S(1)} collective-permute-done((f32[160,512]{1,0:T(8,128)S(1)}, f32[160,512]{1,0:T(8,128)S(1)}, u32[]{:S(2)}, u32[]{:S(2)}) %collective-permute-start.128) | collective-permute-done | bytes 327712 | tf_op jit(solution)/shard_map/ppermute | solution.py:1032
  363.1 6.5 %collective-permute-done.139 = f32[160,512]{1,0:T(8,128)S(1)} collective-permute-done((f32[160,512]{1,0:T(8,128)S(1)}, f32[160,512]{1,0:T(8,128)S(1)}, u32[]{:S(2)}, u32[]{:S(2)}) %collective-permute-start.139) | collective-permute-done | bytes 327712 | tf_op jit(solution)/shard_map/ppermute | solution.py:1032
  377.1 10.9 %collective-permute-done.136 = f32[128,1024]{1,0:T(8,128)S(1)} collective-permute-done((f32[128,1024]{1,0:T(8,128)S(1)}, f32[128,1024]{1,0:T(8,128)S(1)}, u32[]{:S(2)}, u32[]{:S(2)}) %collective-permute-start.136) | collective-permute-done | bytes 524320 | tf_op jit(solution)/shard_map/ppermute | solution.py:1032
  389.8 11.6 %collective-permute-done.135 = f32[304,512]{1,0:T(8,128)S(1)} collective-permute-done((f32[304,512]{1,0:T(8,128)S(1)}, f32[304,512]{1,0:T(8,128)S(1)}, u32[]{:S(2)}, u32[]{:S(2)}) %collective-permute-start.135) | collective-permute-done | bytes 622624 | tf_op jit(solution)/shard_map/ppermute | solution.py:1032
  402.3 10.4 %collective-permute-done.141 = f32[320,512]{1,0:T(8,128)S(1)} collective-permute-done((f32[320,512]{1,0:T(8,128)S(1)}, f32[320,512]{1,0:T(8,128)S(1)}, u32[]{:S(2)}, u32[]{:S(2)}) %collective-permute-start.141) | collective-permute-done | bytes 655392 | tf_op jit(solution)/shard_map/ppermute | solution.py:1032
  (300 shorter events, 167.1 us)
Async XLA Ops:
  5.1 26.5 %collective-permute-start.100 = (f32[1024,512]{1,0:T(8,128)}, f32[1024,512]{1,0:T(8,128)}, u32[]{:S(2)}, u32[]{:S(2)}) collective-permute-start(f32[1024,512]{1,0:T(8,128)} %bitcast.1906), channel_id=1, source_target_pairs={{0,1},{1,0},{2,3},{3,2},{4,5},{5,4},{6,7},{7,6},{8,9},{9,8},{10,11... | collective-permute-start | bytes 6291464 | tf_op jit(solution)/shard_map/ppermute | solution.py:44
  5.1 26.5 %collective-permute-start.102 = (f32[512,1024]{1,0:T(8,128)}, f32[512,1024]{1,0:T(8,128)}, u32[]{:S(2)}, u32[]{:S(2)}) collective-permute-start(f32[512,1024]{1,0:T(8,128)} %bitcast.2016), channel_id=1, source_target_pairs={{0,1},{1,0},{2,3},{3,2},{4,5},{5,4},{6,7},{7,6},{8,9},{9,8},{10,11... | collective-permute-start | bytes 6291464 | tf_op jit(solution)/shard_map/ppermute | solution.py:44
  5.6 26.0 %collective-permute-start.101 = (f32[1216,512]{1,0:T(8,128)}, f32[1216,512]{1,0:T(8,128)}, u32[]{:S(2)}, u32[]{:S(2)}) collective-permute-start(f32[1216,512]{1,0:T(8,128)} %bitcast.1896), channel_id=1, source_target_pairs={{0,1},{1,0},{2,3},{3,2},{4,5},{5,4},{6,7},{7,6},{8,9},{9,8},{10,11... | collective-permute-start | bytes 7471112 | tf_op jit(solution)/shard_map/ppermute | solution.py:44
  43.8 35.1 %collective-permute-start.103 = (f32[128,1152]{1,0:T(8,128)}, f32[128,1152]{1,0:T(8,128)S(1)}, u32[]{:S(2)}, u32[]{:S(2)}) collective-permute-start(f32[128,1152]{1,0:T(8,128)} %get-tuple-element.1013), channel_id=1, source_target_pairs={{0,16},{1,17},{2,18},{3,19},{4,20},{5,21},{6,22},{7,23},{8,24},{9,... | collective-permute-start | bytes 1769480 | tf_op jit(solution)/shard_map/ppermute | solution.py:40
  61.0 21.7 %collective-permute-start.105 = (f32[192,1152]{1,0:T(8,128)}, f32[192,1152]{1,0:T(8,128)}, u32[]{:S(2)}, u32[]{:S(2)}) collective-permute-start(f32[192,1152]{1,0:T(8,128)} %get-tuple-element.1015), channel_id=1, source_target_pairs={{0,16},{1,17},{2,18},{3,19},{4,20},{5,21},{6,22},{7,23},{8,24},{9,... | collective-permute-start | bytes 2654216 | tf_op jit(solution)/shard_map/ppermute | solution.py:40
  76.7 35.3 %collective-permute-start.107 = (f32[160,1152]{1,0:T(8,128)}, f32[160,1152]{1,0:T(8,128)}, u32[]{:S(2)}, u32[]{:S(2)}) collective-permute-start(f32[160,1152]{1,0:T(8,128)} %get-tuple-element.1021), channel_id=1, source_target_pairs={{0,16},{1,17},{2,18},{3,19},{4,20},{5,21},{6,22},{7,23},{8,24},{9,... | collective-permute-start | bytes 2211848 | tf_op jit(solution)/shard_map/ppermute | solution.py:40
  110.7 24.9 %collective-permute-start.106 = (f32[192,1152]{1,0:T(8,128)}, f32[192,1152]{1,0:T(8,128)S(1)}, u32[]{:S(2)}, u32[]{:S(2)}) collective-permute-start(f32[192,1152]{1,0:T(8,128)} %get-tuple-element.1020), channel_id=1, source_target_pairs={{16,0},{17,1},{18,2},{19,3},{20,4},{21,5},{22,6},{23,7},{24,8},{25... | collective-permute-start | bytes 2654216 | tf_op jit(solution)/shard_map/ppermute | solution.py:40
  177.6 22.9 %collective-permute-start.109 = (f32[512,1024]{1,0:T(8,128)}, f32[512,1024]{1,0:T(8,128)}, u32[]{:S(2)}, u32[]{:S(2)}) collective-permute-start(f32[512,1024]{1,0:T(8,128)} %get-tuple-element.1034), channel_id=1, source_target_pairs={{0,1},{1,0},{2,3},{3,2},{4,5},{5,4},{6,7},{7,6},{8,9},{9,8},{10,11... | collective-permute-start | bytes 6291464 | tf_op jit(solution)/shard_map/ppermute | solution.py:44
  251.7 26.2 %collective-permute-start.120 = (f32[304,512]{1,0:T(8,128)S(1)}, f32[304,512]{1,0:T(8,128)S(1)}, u32[]{:S(2)}, u32[]{:S(2)}) collective-permute-start(f32[304,512]{1,0:T(8,128)S(1)} %get-tuple-element.1089), channel_id=1, source_target_pairs={{0,4},{2,6},{4,0},{6,2},{8,12},{10,14},{12,8},{14,10},{1,5},{3,7},... | collective-permute-start | bytes 1867784 | tf_op jit(solution)/shard_map/ppermute | solution.py:1032
  264.0 27.7 %collective-permute-start.116 = (f32[304,512]{1,0:T(8,128)S(1)}, f32[304,512]{1,0:T(8,128)S(1)}, u32[]{:S(2)}, u32[]{:S(2)}) collective-permute-start(f32[304,512]{1,0:T(8,128)S(1)} %get-tuple-element.1090), channel_id=1, source_target_pairs={{0,2},{2,0},{4,6},{6,4},{8,10},{10,8},{12,14},{14,12},{1,3},{3,1},... | collective-permute-start | bytes 1867784 | tf_op jit(solution)/shard_map/ppermute | solution.py:1032
  264.9 26.8 %collective-permute-start.119 = (f32[64,1024]{1,0:T(8,128)S(1)}, f32[64,1024]{1,0:T(8,128)S(1)}, u32[]{:S(2)}, u32[]{:S(2)}) collective-permute-start(f32[64,1024]{1,0:T(8,128)S(1)} %dynamic-slice_add_fusion.10), channel_id=1, source_target_pairs={{0,12},{2,14},{4,8},{6,10},{8,4},{10,6},{12,0},{14,2},{1,13},{3,15... | collective-permute-start | bytes 786440 | tf_op jit(solution)/shard_map/ppermute | solution.py:1032
  278.0 32.1 %collective-permute-start.124 = (f32[320,512]{1,0:T(8,128)S(1)}, f32[320,512]{1,0:T(8,128)S(1)}, u32[]{:S(2)}, u32[]{:S(2)}) collective-permute-start(f32[320,512]{1,0:T(8,128)S(1)} %constant_dynamic-slice_fusion.105), channel_id=1, source_target_pairs={{0,2},{2,0},{4,6},{6,4},{8,10},{10,8},{12,14},{14,12},{1,3},{3,1},... | collective-permute-start | bytes 1966088 | tf_op jit(solution)/shard_map/ppermute | solution.py:1032
  292.0 28.1 %collective-permute-start.131 = (f32[64,1024]{1,0:T(8,128)S(1)}, f32[64,1024]{1,0:T(8,128)S(1)}, u32[]{:S(2)}, u32[]{:S(2)}) collective-permute-start(f32[64,1024]{1,0:T(8,128)S(1)} %add.1948), channel_id=1, source_target_pairs={{0,4},{2,6},{4,0},{6,2},{8,12},{10,14},{12,8},{14,10},{1,5},{3,7},... | collective-permute-start | bytes 786440 | tf_op jit(solution)/shard_map/ppermute | solution.py:1032
  297.1 22.8 %collective-permute-start.122 = (f32[152,512]{1,0:T(8,128)S(1)}, f32[152,512]{1,0:T(8,128)S(1)}, u32[]{:S(2)}, u32[]{:S(2)}) collective-permute-start(f32[152,512]{1,0:T(8,128)S(1)} %constant_dynamic-slice_fusion.103), channel_id=1, source_target_pairs={{0,4},{2,6},{4,0},{6,2},{8,12},{10,14},{12,8},{14,10},{1,5},{3,7},... | collective-permute-start | bytes 933896 | tf_op jit(solution)/shard_map/ppermute | solution.py:1032
  302.9 35.9 %collective-permute-start.129 = (f32[152,512]{1,0:T(8,128)S(1)}, f32[152,512]{1,0:T(8,128)S(1)}, u32[]{:S(2)}, u32[]{:S(2)}) collective-permute-start(f32[152,512]{1,0:T(8,128)S(1)} %dynamic-slice_add_fusion.8), channel_id=1, source_target_pairs={{0,12},{2,14},{4,8},{6,10},{8,4},{10,6},{12,0},{14,2},{1,13},{3,15... | collective-permute-start | bytes 933896 | tf_op jit(solution)/shard_map/ppermute | solution.py:1032
  310.3 25.6 %collective-permute-start.130 = (f32[160,512]{1,0:T(8,128)S(1)}, f32[160,512]{1,0:T(8,128)S(1)}, u32[]{:S(2)}, u32[]{:S(2)}) collective-permute-start(f32[160,512]{1,0:T(8,128)S(1)} %constant_dynamic-slice_fusion.102), channel_id=1, source_target_pairs={{0,4},{2,6},{4,0},{6,2},{8,12},{10,14},{12,8},{14,10},{1,5},{3,7},... | collective-permute-start | bytes 983048 | tf_op jit(solution)/shard_map/ppermute | solution.py:1032
  320.0 32.5 %collective-permute-start.127 = (f32[152,512]{1,0:T(8,128)S(1)}, f32[152,512]{1,0:T(8,128)S(1)}, u32[]{:S(2)}, u32[]{:S(2)}) collective-permute-start(f32[152,512]{1,0:T(8,128)S(1)} %dynamic-slice_add_fusion.9), channel_id=1, source_target_pairs={{0,12},{2,14},{4,8},{6,10},{8,4},{10,6},{12,0},{14,2},{1,13},{3,15... | collective-permute-start | bytes 933896 | tf_op jit(solution)/shard_map/ppermute | solution.py:1032
  352.4 24.6 %collective-permute-start.137 = (f32[320,512]{1,0:T(8,128)S(1)}, f32[320,512]{1,0:T(8,128)S(1)}, u32[]{:S(2)}, u32[]{:S(2)}) collective-permute-start(f32[320,512]{1,0:T(8,128)S(1)} %get-tuple-element.1677), channel_id=1, source_target_pairs={{0,2},{2,0},{4,6},{6,4},{8,10},{10,8},{12,14},{14,12},{1,3},{3,1},... | collective-permute-start | bytes 1966088 | tf_op jit(solution)/shard_map/ppermute | solution.py:1032
  357.6 19.2 %collective-permute-start.138 = (f32[152,512]{1,0:T(8,128)S(1)}, f32[152,512]{1,0:T(8,128)S(1)}, u32[]{:S(2)}, u32[]{:S(2)}) collective-permute-start(f32[152,512]{1,0:T(8,128)S(1)} %add.1959), channel_id=1, source_target_pairs={{0,2},{2,0},{4,6},{6,4},{8,10},{10,8},{12,14},{14,12},{1,3},{3,1},... | collective-permute-start | bytes 933896 | tf_op jit(solution)/shard_map/ppermute | solution.py:1032
  357.7 30.3 %collective-permute-start.136 = (f32[128,1024]{1,0:T(8,128)S(1)}, f32[128,1024]{1,0:T(8,128)S(1)}, u32[]{:S(2)}, u32[]{:S(2)}) collective-permute-start(f32[128,1024]{1,0:T(8,128)S(1)} %maximum_select_fusion.53), channel_id=1, source_target_pairs={{0,2},{2,0},{4,6},{6,4},{8,10},{10,8},{12,14},{14,12},{1,3},{3,1},... | collective-permute-start | bytes 1572872 | tf_op jit(solution)/shard_map/ppermute | solution.py:1032
  363.0 38.4 %collective-permute-start.142 = (f32[128,1024]{1,0:T(8,128)S(1)}, f32[128,1024]{1,0:T(8,128)S(1)}, u32[]{:S(2)}, u32[]{:S(2)}) collective-permute-start(f32[128,1024]{1,0:T(8,128)S(1)} %maximum_select_fusion.54), channel_id=1, source_target_pairs={{0,4},{2,6},{4,0},{6,2},{8,12},{10,14},{12,8},{14,10},{1,5},{3,7},... | collective-permute-start | bytes 1572872 | tf_op jit(solution)/shard_map/ppermute | solution.py:1032
  369.6 31.8 %collective-permute-start.135 = (f32[304,512]{1,0:T(8,128)S(1)}, f32[304,512]{1,0:T(8,128)S(1)}, u32[]{:S(2)}, u32[]{:S(2)}) collective-permute-start(f32[304,512]{1,0:T(8,128)S(1)} %get-tuple-element.1679), channel_id=1, source_target_pairs={{0,2},{2,0},{4,6},{6,4},{8,10},{10,8},{12,14},{14,12},{1,3},{3,1},... | collective-permute-start | bytes 1867784 | tf_op jit(solution)/shard_map/ppermute | solution.py:1032
  376.9 35.8 %collective-permute-start.140 = (f32[304,512]{1,0:T(8,128)S(1)}, f32[304,512]{1,0:T(8,128)S(1)}, u32[]{:S(2)}, u32[]{:S(2)}) collective-permute-start(f32[304,512]{1,0:T(8,128)S(1)} %maximum_select_fusion.52), channel_id=1, source_target_pairs={{0,4},{2,6},{4,0},{6,2},{8,12},{10,14},{12,8},{14,10},{1,5},{3,7},... | collective-permute-start | bytes 1867784 | tf_op jit(solution)/shard_map/ppermute | solution.py:1032
  377.0 35.7 %collective-permute-start.141 = (f32[320,512]{1,0:T(8,128)S(1)}, f32[320,512]{1,0:T(8,128)S(1)}, u32[]{:S(2)}, u32[]{:S(2)}) collective-permute-start(f32[320,512]{1,0:T(8,128)S(1)} %maximum_select_fusion.50), channel_id=1, source_target_pairs={{0,2},{2,0},{4,6},{6,4},{8,10},{10,8},{12,14},{14,12},{1,3},{3,1},... | collective-permute-start | bytes 1966088 | tf_op jit(solution)/shard_map/ppermute | solution.py:1032
  (52 other events, 558.5 us)

commit v4 on v3

--- a/solution.py
+++ b/solution.py
@@ -1147,9 +1147,10 @@
     by_hand = lax.axis_size("edge") == 8
     sums = BlockSums(PLAN)
     for k, m in enumerate(CHUNKS):
-        back = seconds[k][0] if k == 0 else tied(seconds[k][0], firsts[k - 1][0])
-        returned.append(shifted(back, "section", -1))
-        arrived = returned[k]
+        arrived = shifted(seconds[k][0], "section", -1)
+        if k > 0:
+            arrived = tied(arrived, firsts[k - 1][0])
+        returned.append(arrived)
         if k == count - 1:
             out_own, out_other = outer_call(
                 True, [(half, width)] * 2, (width, width), outer_work, second_flag,
@@ -1210,7 +1211,7 @@
     spread = jnp.where(is_first, spread, none)
     if by_hand:
         matrices = [grad_out, grad_in, grad_head]
-        sums.moment = (sums.moment, head_other, grad_in, grad_head)
+        sums.moment = (sums.moment, head_other, grad_in)
         sums.advance(matrices, ORDER[:8])
         spread = sums.wait(spread)
         spread = spread + other_core(spread)

time: 429 us -> 408 us (0.951)
  waiting for transfers between devices: 142 us -> 126 us
  local copies, waits for them, and re-layouts: 39.9 us -> 35.5 us
    ppermute x9, waiting for transfers between devices: 37 us -> 23.7 us  [shifted(): lax.ppermute(value, axis, [(source, source + steps) for source in range(f...]
    ppermute x9, starting transfers between devices: 20.5 us -> 13.7 us  [shifted(): lax.ppermute(value, axis, [(source, source + steps) for source in range(f...]
    ppermute x30, starting transfers between devices: 47.6 us -> 52.7 us  [hop(): return lax.ppermute(value, 'edge', [(i, i ^ distance) for i in range(8)])]
  transfers between devices with their start and end apart: 50 -> 50, of which waited for: 19 -> 18; matrix products, arithmetic and copies ran while one was open for 13% -> 13% of each run, Pallas kernels for 22% -> 27%
where the time goes in v4:
time: 408 us; the launch traced here: 401 us
  Pallas kernels  128 us (31%)
  waiting for transfers between devices  126 us (31%)
  starting transfers between devices  74.6 us (18%)
  local copies, waits for them, and re-layouts  35.5 us (9%)
  other arithmetic  27.8 us (7%)
  matrix products  5.46 us (1%)
    pallas_call x9, Pallas kernels, on_core(): pl.pallas_call(guarded, out_shape=tuple((jax.ShapeDtypeStruct(shape, F32)...  104 us
    ppermute x30, waiting for transfers between devices, hop(): return lax.ppermute(value, 'edge', [(i, i ^ distance) for i in range(8)])  93.7 us
    ppermute x30, starting transfers between devices, hop(): return lax.ppermute(value, 'edge', [(i, i ^ distance) for i in range(8)])  52.7 us
    ppermute x9, waiting for transfers between devices, shifted(): lax.ppermute(value, axis, [(source, source + steps) for source in range(f...  23.7 us
    pallas_call x3, Pallas kernels, outer_call(): pl.pallas_call(partial(outer_sum, split_left), out_shape=tuple((jax.Shape...  22.9 us
    ppermute x9, starting transfers between devices, shifted(): lax.ppermute(value, axis, [(source, source + steps) for source in range(f...  13.7 us
  transfers between devices with their start and end apart: 50, of which 18 were waited for; matrix products, arithmetic and copies ran while one was open for 13% of the time, Pallas kernels for 27%

profile of v4, /device:TPU:0, one launch (start us, length us, event | category | flops | bytes accessed | tf_op | source)
XLA Modules:
  0.0 401.4 jit_solution(16496592533747938118)
XLA Ops:
  32.2 11.5 %shard_map.206 = (f32[128,1152]{1,0:T(8,128)}, f32[128,1024]{1,0:T(8,128)}, f32[128,1280]{1,0:T(8,128)}, f32[128,1024]{1,0:T(8,128)}, f32[128,1024]{1,0:T(8,128)}) custom-call(s32[1]{0:T(128)} %bitcast.282.flag, f32[480,8]{1,0:T(8,128)} %copy.605.refs_0_, f32[1,128]{1,0:T(1,128)} %slice_bitcast_fusion.57.refs_1_, f32[8,128]{1,0:T(8,128)} %mul.9360.refs_2_, ...), custom_call_target="tpu_custom_call" | custom-call | flops 5435817984 | bytes 16777216 | tf_op jit(solution)/shard_map/pallas_call | solution.py:895
  45.0 15.6 %shard_map.207 = (f32[192,1152]{1,0:T(8,128)}, f32[192,1024]{1,0:T(8,128)}, f32[192,1280]{1,0:T(8,128)}, f32[192,1024]{1,0:T(8,128)}, f32[192,1024]{1,0:T(8,128)}) custom-call(s32[1]{0:T(128)} %bitcast.282.flag, f32[480,8]{1,0:T(8,128)} %copy.605.refs_0_, f32[1,192]{1,0:T(1,128)} %slice_bitcast_fusion.56.refs_1_, f32[8,128]{1,0:T(8,128)} %mul.9360.refs_2_, ...), custom_call_target="tpu_custom_call" | custom-call | flops 8153726976 | bytes 16777216 | tf_op jit(solution)/shard_map/pallas_call | solution.py:895
  62.9 13.4 %shard_map.208 = (f32[160,1152]{1,0:T(8,128)}, f32[160,1024]{1,0:T(8,128)}, f32[160,1280]{1,0:T(8,128)}, f32[160,1024]{1,0:T(8,128)}, f32[160,1024]{1,0:T(8,128)}) custom-call(s32[1]{0:T(128)} %bitcast.282.flag, f32[480,8]{1,0:T(8,128)} %copy.605.refs_0_, f32[1,160]{1,0:T(1,128)} %slice_bitcast_fusion.55.refs_1_, f32[8,128]{1,0:T(8,128)} %mul.9360.refs_2_, ...), custom_call_target="tpu_custom_call" | custom-call | flops 6794772480 | bytes 16777216 | tf_op jit(solution)/shard_map/pallas_call | solution.py:895
  82.3 11.7 %shard_map.210 = (f32[192,1152]{1,0:T(8,128)}, f32[192,1280]{1,0:T(8,128)}, f32[192,1024]{1,0:T(8,128)}, f32[192,1024]{1,0:T(8,128)}, f32[192,1024]{1,0:T(8,128)...) custom-call(s32[1]{0:T(128)S(6)} %sub.753.flag.chosen, ...), custom_call_target="tpu_custom_call" | custom-call | flops 12230590464 | bytes 16777216 | tf_op jit(solution)/shard_map/pallas_call | solution.py:895
  96.2 7.7 %shard_map.212 = (f32[160,1152]{1,0:T(8,128)}, f32[160,1280]{1,0:T(8,128)}, f32[160,1024]{1,0:T(8,128)}, f32[160,1024]{1,0:T(8,128)}, f32[160,1024]{1,0:T(8,128)...) custom-call(s32[1]{0:T(128)S(6)} %sub.753.flag.chosen, ...), custom_call_target="tpu_custom_call" | custom-call | flops 10192158720 | bytes 16777216 | tf_op jit(solution)/shard_map/pallas_call | solution.py:895
  107.1 12.2 %shard_map.211 = (f32[128,128]{1,0:T(8,128)}, f32[128,1024]{1,0:T(8,128)}, f32[128,1024]{1,0:T(8,128)}, f32[128,128]{1,0:T(8,128)}, f32[16,1024]{1,0:T(8,128)}) custom-call(s32[1]{0:T(128)} %bitcast.282.flag, f32[480,8]{1,0:T(8,128)} %copy.605.refs_0_, f32[1,128]{1,0:T(1,128)} %slice_bitcast_fusion.57.refs_1_, f32[8,128]{1,0:T(8,128)} %mul.9360.refs_2_, ...), custom_call_target="tpu_custom_call" | custom-call | flops 4076863488 | bytes 16777216 | tf_op jit(solution)/shard_map/pallas_call | solution.py:895
  119.3 14.1 %collective-permute-done.106.refs_6_.refs_4_ = f32[192,1152]{1,0:T(8,128)} collective-permute-done((f32[192,1152]{1,0:T(8,128)}, f32[192,1152]{1,0:T(8,128)}, u32[]{:S(2)}, u32[]{:S(2)}) %collective-permute-start.106) | collective-permute-done | bytes 884768 | tf_op jit(solution)/shard_map/ppermute | solution.py:40
  133.4 15.8 %shard_map.213 = (f32[192,128]{1,0:T(8,128)}, f32[192,1024]{1,0:T(8,128)}, f32[192,1024]{1,0:T(8,128)}, f32[192,128]{1,0:T(8,128)}, f32[16,1024]{1,0:T(8,128)}) custom-call(s32[1]{0:T(128)} %bitcast.282.flag, f32[480,8]{1,0:T(8,128)} %copy.605.refs_0_, f32[1,192]{1,0:T(1,128)} %slice_bitcast_fusion.56.refs_1_, f32[8,128]{1,0:T(8,128)} %mul.9360.refs_2_, ...), custom_call_target="tpu_custom_call" | custom-call | flops 6115295232 | bytes 16777216 | tf_op jit(solution)/shard_map/pallas_call | solution.py:895
  149.2 8.8 %collective-permute-done.108.refs_5_.refs_6_ = f32[160,1152]{1,0:T(8,128)} collective-permute-done((f32[160,1152]{1,0:T(8,128)}, f32[160,1152]{1,0:T(8,128)}, u32[]{:S(2)}, u32[]{:S(2)}) %collective-permute-start.108) | collective-permute-done | bytes 737312 | tf_op jit(solution)/shard_map/ppermute | solution.py:40
  158.0 6.9 %shard_map.214 = (f32[512,1024]{1,0:T(8,128)}, f32[512,1024]{1,0:T(8,128)}) custom-call(s32[1]{0:T(128)S(6)} %sub.753.flag.chosen, f32[128,1024]{1,0:T(8,128)} %get-tuple-element.1010.refs_0_, f32[192,1024]{1,0:T(8,128)} %get-tuple-element.1011.refs_1_, f32[160,1024]{1,0:T(8,128)} %get-tuple-element.1012.refs_2_, f32[128,1152]{1,0:T(8,128)} %copy-done.269, ...), custom_call_target="tpu_custom_call" | custom-call | flops 3019898880 | bytes 16777216 | tf_op jit(solution)/shard_map/pallas_call | solution.py:909
  166.6 14.3 %shard_map.215 = (f32[160,128]{1,0:T(8,128)}, f32[160,1024]{1,0:T(8,128)}, f32[160,1024]{1,0:T(8,128)}, f32[160,128]{1,0:T(8,128)}, f32[16,1024]{1,0:T(8,128)}) custom-call(s32[1]{0:T(128)} %bitcast.282.flag, f32[480,8]{1,0:T(8,128)} %copy.605.refs_0_, f32[1,160]{1,0:T(1,128)} %slice_bitcast_fusion.55.refs_1_, f32[8,128]{1,0:T(8,128)} %mul.9360.refs_2_, ...), custom_call_target="tpu_custom_call" | custom-call | flops 5096079360 | bytes 16777216 | tf_op jit(solution)/shard_map/pallas_call | solution.py:895
  182.0 5.8 %collective-permute-done.112 = f32[32,1024]{1,0:T(8,128)S(1)} collective-permute-done((f32[32,1024]{1,0:T(8,128)S(1)}, f32[32,1024]{1,0:T(8,128)S(1)}, u32[]{:S(2)}, u32[]{:S(2)}) %collective-permute-start.112) | collective-permute-done | bytes 131104 | tf_op jit(solution)/shard_map/ppermute | solution.py:1203
  193.9 9.1 %shard_map.216 = (f32[1280,512]{1,0:T(8,128)}, f32[1280,512]{1,0:T(8,128)}, f32[1024,128]{1,0:T(8,128)}) custom-call(s32[1]{0:T(128)S(6)} %sub.753.flag.chosen, f32[128,1280]{1,0:T(8,128)} %get-tuple-element.1017.refs_4_.refs_0_, f32[192,1280]{1,0:T(8,128)} %get-tuple-element.1023.refs_4_.refs_1_, f32[160,1280]{1,0:T(8,128)} %get-tuple-element.1037.refs_4_.refs_2_, ...), custom_call_target="tpu_custom_call" | custom-call | flops 3019898880 | bytes 16777216 | tf_op jit(solution)/shard_map/pallas_call | solution.py:909
  209.6 6.9 %shard_map.217 = (f32[1024,512]{1,0:T(8,128)}, f32[1024,512]{1,0:T(8,128)}) custom-call(s32[1]{0:T(128)S(6)} %sub.753.flag.chosen, f32[128,1024]{1,0:T(8,128)} %get-tuple-element.1059.refs_0_, f32[192,1024]{1,0:T(8,128)} %get-tuple-element.1060.refs_1_, f32[160,1024]{1,0:T(8,128)} %get-tuple-element.1061.refs_2_, f32[128,1024]{1,0:T(8,128)} %get-tuple-element.1062.refs_3_, ...), custom_call_target="tpu_custom_call" | custom-call | flops 3019898880 | bytes 16777216 | tf_op jit(solution)/shard_map/pallas_call | solution.py:909
  237.1 11.4 %collective-permute-done.118 = f32[320,512]{1,0:T(8,128)S(1)} collective-permute-done((f32[320,512]{1,0:T(8,128)S(1)}, f32[320,512]{1,0:T(8,128)S(1)}, u32[]{:S(2)}, u32[]{:S(2)}) %collective-permute-start.118) | collective-permute-done | bytes 655392 | tf_op jit(solution)/shard_map/ppermute | solution.py:1032
  261.7 9.3 %collective-permute-start.126 = (f32[64,1024]{1,0:T(8,128)S(1)}, f32[64,1024]{1,0:T(8,128)S(1)}, u32[]{:S(2)}, u32[]{:S(2)}) collective-permute-start(f32[64,1024]{1,0:T(8,128)S(1)} %dynamic-slice_add_fusion.11), channel_id=1, source_target_pairs={{0,12},{2,14},{4,8},{6,10},{8,4},{10,6},{12,0},{14,2},{1,13},{3,15... | collective-permute-start | bytes 786440 | tf_op jit(solution)/shard_map/ppermute | solution.py:1032
  276.8 10.0 %collective-permute-start.131 = (f32[64,1024]{1,0:T(8,128)S(1)}, f32[64,1024]{1,0:T(8,128)S(1)}, u32[]{:S(2)}, u32[]{:S(2)}) collective-permute-start(f32[64,1024]{1,0:T(8,128)S(1)} %add.1948), channel_id=1, source_target_pairs={{0,4},{2,6},{4,0},{6,2},{8,12},{10,14},{12,8},{14,10},{1,5},{3,7},... | collective-permute-start | bytes 786440 | tf_op jit(solution)/shard_map/ppermute | solution.py:1032
  290.3 20.2 %collective-permute-done.122 = f32[152,512]{1,0:T(8,128)S(1)} collective-permute-done((f32[152,512]{1,0:T(8,128)S(1)}, f32[152,512]{1,0:T(8,128)S(1)}, u32[]{:S(2)}, u32[]{:S(2)}) %collective-permute-start.122) | collective-permute-done | bytes 311328 | tf_op jit(solution)/shard_map/ppermute | solution.py:1032
  319.1 4.8 %collective-permute-start.134 = (f32[160,512]{1,0:T(8,128)S(1)}, f32[160,512]{1,0:T(8,128)S(1)}, u32[]{:S(2)}, u32[]{:S(2)}) collective-permute-start(f32[160,512]{1,0:T(8,128)S(1)} %dynamic-slice_add_fusion.6), channel_id=1, source_target_pairs={{0,12},{2,14},{4,8},{6,10},{8,4},{10,6},{12,0},{14,2},{1,13},{3,15... | collective-permute-start | bytes 983048 | tf_op jit(solution)/shard_map/ppermute | solution.py:1032
  344.4 5.0 %collective-permute-done.139 = f32[160,512]{1,0:T(8,128)S(1)} collective-permute-done((f32[160,512]{1,0:T(8,128)S(1)}, f32[160,512]{1,0:T(8,128)S(1)}, u32[]{:S(2)}, u32[]{:S(2)}) %collective-permute-start.139) | collective-permute-done | bytes 327712 | tf_op jit(solution)/shard_map/ppermute | solution.py:1032
  351.2 4.7 %collective-permute-done.138 = f32[152,512]{1,0:T(8,128)S(1)} collective-permute-done((f32[152,512]{1,0:T(8,128)S(1)}, f32[152,512]{1,0:T(8,128)S(1)}, u32[]{:S(2)}, u32[]{:S(2)}) %collective-permute-start.138) | collective-permute-done | bytes 311328 | tf_op jit(solution)/shard_map/ppermute | solution.py:1032
  356.2 10.9 %collective-permute-done.136 = f32[128,1024]{1,0:T(8,128)S(1)} collective-permute-done((f32[128,1024]{1,0:T(8,128)S(1)}, f32[128,1024]{1,0:T(8,128)S(1)}, u32[]{:S(2)}, u32[]{:S(2)}) %collective-permute-start.136) | collective-permute-done | bytes 524320 | tf_op jit(solution)/shard_map/ppermute | solution.py:1032
  368.9 11.6 %collective-permute-done.135 = f32[304,512]{1,0:T(8,128)S(1)} collective-permute-done((f32[304,512]{1,0:T(8,128)S(1)}, f32[304,512]{1,0:T(8,128)S(1)}, u32[]{:S(2)}, u32[]{:S(2)}) %collective-permute-start.135) | collective-permute-done | bytes 622624 | tf_op jit(solution)/shard_map/ppermute | solution.py:1032
  381.5 9.5 %collective-permute-done.141 = f32[320,512]{1,0:T(8,128)S(1)} collective-permute-done((f32[320,512]{1,0:T(8,128)S(1)}, f32[320,512]{1,0:T(8,128)S(1)}, u32[]{:S(2)}, u32[]{:S(2)}) %collective-permute-start.141) | collective-permute-done | bytes 655392 | tf_op jit(solution)/shard_map/ppermute | solution.py:1032
  (288 shorter events, 147.3 us)
Async XLA Ops:
  5.1 26.5 %collective-permute-start.100 = (f32[1024,512]{1,0:T(8,128)}, f32[1024,512]{1,0:T(8,128)}, u32[]{:S(2)}, u32[]{:S(2)}) collective-permute-start(f32[1024,512]{1,0:T(8,128)} %bitcast.1906), channel_id=1, source_target_pairs={{0,1},{1,0},{2,3},{3,2},{4,5},{5,4},{6,7},{7,6},{8,9},{9,8},{10,11... | collective-permute-start | bytes 6291464 | tf_op jit(solution)/shard_map/ppermute | solution.py:44
  5.1 26.5 %collective-permute-start.102 = (f32[512,1024]{1,0:T(8,128)}, f32[512,1024]{1,0:T(8,128)}, u32[]{:S(2)}, u32[]{:S(2)}) collective-permute-start(f32[512,1024]{1,0:T(8,128)} %bitcast.2016), channel_id=1, source_target_pairs={{0,1},{1,0},{2,3},{3,2},{4,5},{5,4},{6,7},{7,6},{8,9},{9,8},{10,11... | collective-permute-start | bytes 6291464 | tf_op jit(solution)/shard_map/ppermute | solution.py:44
  5.6 26.0 %collective-permute-start.101 = (f32[1216,512]{1,0:T(8,128)}, f32[1216,512]{1,0:T(8,128)}, u32[]{:S(2)}, u32[]{:S(2)}) collective-permute-start(f32[1216,512]{1,0:T(8,128)} %bitcast.1896), channel_id=1, source_target_pairs={{0,1},{1,0},{2,3},{3,2},{4,5},{5,4},{6,7},{7,6},{8,9},{9,8},{10,11... | collective-permute-start | bytes 7471112 | tf_op jit(solution)/shard_map/ppermute | solution.py:44
  43.7 34.9 %collective-permute-start.103 = (f32[128,1152]{1,0:T(8,128)}, f32[128,1152]{1,0:T(8,128)S(1)}, u32[]{:S(2)}, u32[]{:S(2)}) collective-permute-start(f32[128,1152]{1,0:T(8,128)} %get-tuple-element.1013), channel_id=1, source_target_pairs={{0,16},{1,17},{2,18},{3,19},{4,20},{5,21},{6,22},{7,23},{8,24},{9,... | collective-permute-start | bytes 1769480 | tf_op jit(solution)/shard_map/ppermute | solution.py:40
  60.6 21.7 %collective-permute-start.105 = (f32[192,1152]{1,0:T(8,128)}, f32[192,1152]{1,0:T(8,128)}, u32[]{:S(2)}, u32[]{:S(2)}) collective-permute-start(f32[192,1152]{1,0:T(8,128)} %get-tuple-element.1015), channel_id=1, source_target_pairs={{0,16},{1,17},{2,18},{3,19},{4,20},{5,21},{6,22},{7,23},{8,24},{9,... | collective-permute-start | bytes 2654216 | tf_op jit(solution)/shard_map/ppermute | solution.py:40
  81.0 25.3 %collective-permute-start.104 = (f32[128,1152]{1,0:T(8,128)}, f32[128,1152]{1,0:T(8,128)S(1)}, u32[]{:S(2)}, u32[]{:S(2)}) collective-permute-start(f32[128,1152]{1,0:T(8,128)} %get-tuple-element.1014), channel_id=1, source_target_pairs={{16,0},{17,1},{18,2},{19,3},{20,4},{21,5},{22,6},{23,7},{24,8},{25... | collective-permute-start | bytes 1769480 | tf_op jit(solution)/shard_map/ppermute | solution.py:40
  94.0 39.4 %collective-permute-start.106 = (f32[192,1152]{1,0:T(8,128)}, f32[192,1152]{1,0:T(8,128)}, u32[]{:S(2)}, u32[]{:S(2)}) collective-permute-start(f32[192,1152]{1,0:T(8,128)} %get-tuple-element.1016), channel_id=1, source_target_pairs={{16,0},{17,1},{18,2},{19,3},{20,4},{21,5},{22,6},{23,7},{24,8},{25... | collective-permute-start | bytes 2654216 | tf_op jit(solution)/shard_map/ppermute | solution.py:40
  104.0 54.1 %collective-permute-start.108 = (f32[160,1152]{1,0:T(8,128)}, f32[160,1152]{1,0:T(8,128)}, u32[]{:S(2)}, u32[]{:S(2)}) collective-permute-start(f32[160,1152]{1,0:T(8,128)} %get-tuple-element.1022), channel_id=1, source_target_pairs={{16,0},{17,1},{18,2},{19,3},{20,4},{21,5},{22,6},{23,7},{24,8},{25... | collective-permute-start | bytes 2211848 | tf_op jit(solution)/shard_map/ppermute | solution.py:40
  165.0 22.9 %collective-permute-start.109 = (f32[512,1024]{1,0:T(8,128)}, f32[512,1024]{1,0:T(8,128)}, u32[]{:S(2)}, u32[]{:S(2)}) collective-permute-start(f32[512,1024]{1,0:T(8,128)} %get-tuple-element.1034), channel_id=1, source_target_pairs={{0,1},{1,0},{2,3},{3,2},{4,5},{5,4},{6,7},{7,6},{8,9},{9,8},{10,11... | collective-permute-start | bytes 6291464 | tf_op jit(solution)/shard_map/ppermute | solution.py:44
  204.3 22.8 %collective-permute-start.114 = (f32[1280,512]{1,0:T(8,128)}, f32[1280,512]{1,0:T(8,128)}, u32[]{:S(2)}, u32[]{:S(2)}) collective-permute-start(f32[1280,512]{1,0:T(8,128)} %get-tuple-element.1055), channel_id=1, source_target_pairs={{0,1},{1,0},{2,3},{3,2},{4,5},{5,4},{6,7},{7,6},{8,9},{9,8},{10,11... | collective-permute-start | bytes 7864328 | tf_op jit(solution)/shard_map/ppermute | solution.py:44
  226.0 25.5 %collective-permute-start.117 = (f32[64,1024]{1,0:T(8,128)S(1)}, f32[64,1024]{1,0:T(8,128)S(1)}, u32[]{:S(2)}, u32[]{:S(2)}) collective-permute-start(f32[64,1024]{1,0:T(8,128)S(1)} %constant_dynamic-slice_fusion.110), channel_id=1, source_target_pairs={{0,4},{2,6},{4,0},{6,2},{8,12},{10,14},{12,8},{14,10},{1,5},{3,7},... | collective-permute-start | bytes 786440 | tf_op jit(solution)/shard_map/ppermute | solution.py:1032
  236.0 22.8 %collective-permute-start.120 = (f32[304,512]{1,0:T(8,128)S(1)}, f32[304,512]{1,0:T(8,128)S(1)}, u32[]{:S(2)}, u32[]{:S(2)}) collective-permute-start(f32[304,512]{1,0:T(8,128)S(1)} %get-tuple-element.1089), channel_id=1, source_target_pairs={{0,4},{2,6},{4,0},{6,2},{8,12},{10,14},{12,8},{14,10},{1,5},{3,7},... | collective-permute-start | bytes 1867784 | tf_op jit(solution)/shard_map/ppermute | solution.py:1032
  249.7 22.2 %collective-permute-start.116 = (f32[304,512]{1,0:T(8,128)S(1)}, f32[304,512]{1,0:T(8,128)S(1)}, u32[]{:S(2)}, u32[]{:S(2)}) collective-permute-start(f32[304,512]{1,0:T(8,128)S(1)} %get-tuple-element.1090), channel_id=1, source_target_pairs={{0,2},{2,0},{4,6},{6,4},{8,10},{10,8},{12,14},{14,12},{1,3},{3,1},... | collective-permute-start | bytes 1867784 | tf_op jit(solution)/shard_map/ppermute | solution.py:1032
  258.9 30.3 %collective-permute-start.124 = (f32[320,512]{1,0:T(8,128)S(1)}, f32[320,512]{1,0:T(8,128)S(1)}, u32[]{:S(2)}, u32[]{:S(2)}) collective-permute-start(f32[320,512]{1,0:T(8,128)S(1)} %constant_dynamic-slice_fusion.105), channel_id=1, source_target_pairs={{0,2},{2,0},{4,6},{6,4},{8,10},{10,8},{12,14},{14,12},{1,3},{3,1},... | collective-permute-start | bytes 1966088 | tf_op jit(solution)/shard_map/ppermute | solution.py:1032
  276.8 33.9 %collective-permute-start.131 = (f32[64,1024]{1,0:T(8,128)S(1)}, f32[64,1024]{1,0:T(8,128)S(1)}, u32[]{:S(2)}, u32[]{:S(2)}) collective-permute-start(f32[64,1024]{1,0:T(8,128)S(1)} %add.1948), channel_id=1, source_target_pairs={{0,4},{2,6},{4,0},{6,2},{8,12},{10,14},{12,8},{14,10},{1,5},{3,7},... | collective-permute-start | bytes 786440 | tf_op jit(solution)/shard_map/ppermute | solution.py:1032
  286.8 23.7 %collective-permute-start.122 = (f32[152,512]{1,0:T(8,128)S(1)}, f32[152,512]{1,0:T(8,128)S(1)}, u32[]{:S(2)}, u32[]{:S(2)}) collective-permute-start(f32[152,512]{1,0:T(8,128)S(1)} %constant_dynamic-slice_fusion.103), channel_id=1, source_target_pairs={{0,4},{2,6},{4,0},{6,2},{8,12},{10,14},{12,8},{14,10},{1,5},{3,7},... | collective-permute-start | bytes 933896 | tf_op jit(solution)/shard_map/ppermute | solution.py:1032
  287.0 39.2 %collective-permute-start.129 = (f32[152,512]{1,0:T(8,128)S(1)}, f32[152,512]{1,0:T(8,128)S(1)}, u32[]{:S(2)}, u32[]{:S(2)}) collective-permute-start(f32[152,512]{1,0:T(8,128)S(1)} %dynamic-slice_add_fusion.8), channel_id=1, source_target_pairs={{0,12},{2,14},{4,8},{6,10},{8,4},{10,6},{12,0},{14,2},{1,13},{3,15... | collective-permute-start | bytes 933896 | tf_op jit(solution)/shard_map/ppermute | solution.py:1032
  289.3 26.4 %collective-permute-start.130 = (f32[160,512]{1,0:T(8,128)S(1)}, f32[160,512]{1,0:T(8,128)S(1)}, u32[]{:S(2)}, u32[]{:S(2)}) collective-permute-start(f32[160,512]{1,0:T(8,128)S(1)} %constant_dynamic-slice_fusion.102), channel_id=1, source_target_pairs={{0,4},{2,6},{4,0},{6,2},{8,12},{10,14},{12,8},{14,10},{1,5},{3,7},... | collective-permute-start | bytes 983048 | tf_op jit(solution)/shard_map/ppermute | solution.py:1032
  331.5 24.6 %collective-permute-start.137 = (f32[320,512]{1,0:T(8,128)S(1)}, f32[320,512]{1,0:T(8,128)S(1)}, u32[]{:S(2)}, u32[]{:S(2)}) collective-permute-start(f32[320,512]{1,0:T(8,128)S(1)} %get-tuple-element.1677), channel_id=1, source_target_pairs={{0,2},{2,0},{4,6},{6,4},{8,10},{10,8},{12,14},{14,12},{1,3},{3,1},... | collective-permute-start | bytes 1966088 | tf_op jit(solution)/shard_map/ppermute | solution.py:1032
  337.6 29.5 %collective-permute-start.136 = (f32[128,1024]{1,0:T(8,128)S(1)}, f32[128,1024]{1,0:T(8,128)S(1)}, u32[]{:S(2)}, u32[]{:S(2)}) collective-permute-start(f32[128,1024]{1,0:T(8,128)S(1)} %maximum_select_fusion.53), channel_id=1, source_target_pairs={{0,2},{2,0},{4,6},{6,4},{8,10},{10,8},{12,14},{14,12},{1,3},{3,1},... | collective-permute-start | bytes 1572872 | tf_op jit(solution)/shard_map/ppermute | solution.py:1032
  342.8 37.7 %collective-permute-start.142 = (f32[128,1024]{1,0:T(8,128)S(1)}, f32[128,1024]{1,0:T(8,128)S(1)}, u32[]{:S(2)}, u32[]{:S(2)}) collective-permute-start(f32[128,1024]{1,0:T(8,128)S(1)} %maximum_select_fusion.54), channel_id=1, source_target_pairs={{0,4},{2,6},{4,0},{6,2},{8,12},{10,14},{12,8},{14,10},{1,5},{3,7},... | collective-permute-start | bytes 1572872 | tf_op jit(solution)/shard_map/ppermute | solution.py:1032
  349.5 31.0 %collective-permute-start.135 = (f32[304,512]{1,0:T(8,128)S(1)}, f32[304,512]{1,0:T(8,128)S(1)}, u32[]{:S(2)}, u32[]{:S(2)}) collective-permute-start(f32[304,512]{1,0:T(8,128)S(1)} %get-tuple-element.1679), channel_id=1, source_target_pairs={{0,2},{2,0},{4,6},{6,4},{8,10},{10,8},{12,14},{14,12},{1,3},{3,1},... | collective-permute-start | bytes 1867784 | tf_op jit(solution)/shard_map/ppermute | solution.py:1032
  356.0 35.0 %collective-permute-start.140 = (f32[304,512]{1,0:T(8,128)S(1)}, f32[304,512]{1,0:T(8,128)S(1)}, u32[]{:S(2)}, u32[]{:S(2)}) collective-permute-start(f32[304,512]{1,0:T(8,128)S(1)} %maximum_select_fusion.52), channel_id=1, source_target_pairs={{0,4},{2,6},{4,0},{6,2},{8,12},{10,14},{12,8},{14,10},{1,5},{3,7},... | collective-permute-start | bytes 1867784 | tf_op jit(solution)/shard_map/ppermute | solution.py:1032
  356.1 34.9 %collective-permute-start.141 = (f32[320,512]{1,0:T(8,128)S(1)}, f32[320,512]{1,0:T(8,128)S(1)}, u32[]{:S(2)}, u32[]{:S(2)}) collective-permute-start(f32[320,512]{1,0:T(8,128)S(1)} %maximum_select_fusion.50), channel_id=1, source_target_pairs={{0,2},{2,0},{4,6},{6,4},{8,10},{10,8},{12,14},{14,12},{1,3},{3,1},... | collective-permute-start | bytes 1966088 | tf_op jit(solution)/shard_map/ppermute | solution.py:1032
  (46 other events, 486.6 us)

commit v5 on v4

--- a/solution.py
+++ b/solution.py
@@ -1200,6 +1200,7 @@
     small = jnp.concatenate(
         [jnp.where(is_first, embed_sum, none), jnp.where(is_first, none, small_second)]
     )
+    small = sums.wait(small)
     small = small + lax.ppermute(small, "section", [(0, 1), (1, 0)])
     small = jnp.concatenate([small, grad_env[:, :chan_count].reshape(-1, width)]).reshape(-1, half)
     head_own = jnp.concatenate([head_own, small])

time: 408 us -> 403 us (0.988)
  waiting for transfers between devices: 126 us -> 117 us
    ppermute x1, waiting for transfers between devices: 5.81 us -> 0.01 us  [fast_device(): small = small + lax.ppermute(small, 'section', [(0, 1), (1, 0)])]
    ppermute x30, waiting for transfers between devices: 93.7 us -> 88.5 us  [hop(): return lax.ppermute(value, 'edge', [(i, i ^ distance) for i in range(8)])]
    ppermute x9, starting transfers between devices: 13.7 us -> 18.3 us  [shifted(): lax.ppermute(value, axis, [(source, source + steps) for source in range(f...]
    unnamed x44 -> x52, local copies, waits for them, and re-layouts: 7 us -> 8.71 us
  transfers between devices with their start and end apart: 50 -> 50, of which waited for: 18 -> 20; matrix products, arithmetic and copies ran while one was open for 13% -> 13% of each run, Pallas kernels for 27% -> 27%
where the time goes in v5:
time: 403 us; the launch traced here: 397 us
  Pallas kernels  127 us (32%)
  waiting for transfers between devices  117 us (29%)
  starting transfers between devices  78.4 us (19%)
  local copies, waits for them, and re-layouts  37.9 us (9%)
  other arithmetic  26.9 us (7%)
  matrix products  5.46 us (1%)
    pallas_call x9, Pallas kernels, on_core(): pl.pallas_call(guarded, out_shape=tuple((jax.ShapeDtypeStruct(shape, F32)...  103 us
    ppermute x30, waiting for transfers between devices, hop(): return lax.ppermute(value, 'edge', [(i, i ^ distance) for i in range(8)])  88.5 us
    ppermute x30, starting transfers between devices, hop(): return lax.ppermute(value, 'edge', [(i, i ^ distance) for i in range(8)])  51.9 us
    ppermute x9, waiting for transfers between devices, shifted(): lax.ppermute(value, axis, [(source, source + steps) for source in range(f...  25.6 us
    pallas_call x3, Pallas kernels, outer_call(): pl.pallas_call(partial(outer_sum, split_left), out_shape=tuple((jax.Shape...  23 us
    ppermute x9, starting transfers between devices, shifted(): lax.ppermute(value, axis, [(source, source + steps) for source in range(f...  18.3 us
    unnamed x52, local copies, waits for them, and re-layouts  8.71 us
  transfers between devices with their start and end apart: 50, of which 20 were waited for; matrix products, arithmetic and copies ran while one was open for 13% of the time, Pallas kernels for 27%

profile of v5, /device:TPU:0, one launch (start us, length us, event | category | flops | bytes accessed | tf_op | source)
XLA Modules:
  0.0 396.8 jit_solution(5803246852418222654)
XLA Ops:
  32.2 11.5 %shard_map.206 = (f32[128,1152]{1,0:T(8,128)}, f32[128,1024]{1,0:T(8,128)}, f32[128,1280]{1,0:T(8,128)}, f32[128,1024]{1,0:T(8,128)}, f32[128,1024]{1,0:T(8,128)}) custom-call(s32[1]{0:T(128)} %bitcast.282.flag, f32[480,8]{1,0:T(8,128)} %copy.605.refs_0_, f32[1,128]{1,0:T(1,128)} %slice_bitcast_fusion.57.refs_1_, f32[8,128]{1,0:T(8,128)} %mul.9360.refs_2_, ...), custom_call_target="tpu_custom_call" | custom-call | flops 5435817984 | bytes 16777216 | tf_op jit(solution)/shard_map/pallas_call | solution.py:895
  45.0 15.6 %shard_map.207 = (f32[192,1152]{1,0:T(8,128)}, f32[192,1024]{1,0:T(8,128)}, f32[192,1280]{1,0:T(8,128)}, f32[192,1024]{1,0:T(8,128)}, f32[192,1024]{1,0:T(8,128)}) custom-call(s32[1]{0:T(128)} %bitcast.282.flag, f32[480,8]{1,0:T(8,128)} %copy.605.refs_0_, f32[1,192]{1,0:T(1,128)} %slice_bitcast_fusion.56.refs_1_, f32[8,128]{1,0:T(8,128)} %mul.9360.refs_2_, ...), custom_call_target="tpu_custom_call" | custom-call | flops 8153726976 | bytes 16777216 | tf_op jit(solution)/shard_map/pallas_call | solution.py:895
  62.9 13.4 %shard_map.208 = (f32[160,1152]{1,0:T(8,128)}, f32[160,1024]{1,0:T(8,128)}, f32[160,1280]{1,0:T(8,128)}, f32[160,1024]{1,0:T(8,128)}, f32[160,1024]{1,0:T(8,128)}) custom-call(s32[1]{0:T(128)} %bitcast.282.flag, f32[480,8]{1,0:T(8,128)} %copy.605.refs_0_, f32[1,160]{1,0:T(1,128)} %slice_bitcast_fusion.55.refs_1_, f32[8,128]{1,0:T(8,128)} %mul.9360.refs_2_, ...), custom_call_target="tpu_custom_call" | custom-call | flops 6794772480 | bytes 16777216 | tf_op jit(solution)/shard_map/pallas_call | solution.py:895
  82.3 10.8 %shard_map.210 = (f32[192,1152]{1,0:T(8,128)}, f32[192,1280]{1,0:T(8,128)}, f32[192,1024]{1,0:T(8,128)}, f32[192,1024]{1,0:T(8,128)}, f32[192,1024]{1,0:T(8,128)...) custom-call(s32[1]{0:T(128)S(6)} %sub.753.flag.chosen, ...), custom_call_target="tpu_custom_call" | custom-call | flops 12230590464 | bytes 16777216 | tf_op jit(solution)/shard_map/pallas_call | solution.py:895
  97.1 7.7 %shard_map.212 = (f32[160,1152]{1,0:T(8,128)}, f32[160,1280]{1,0:T(8,128)}, f32[160,1024]{1,0:T(8,128)}, f32[160,1024]{1,0:T(8,128)}, f32[160,1024]{1,0:T(8,128)...) custom-call(s32[1]{0:T(128)S(6)} %sub.753.flag.chosen, ...), custom_call_target="tpu_custom_call" | custom-call | flops 10192158720 | bytes 16777216 | tf_op jit(solution)/shard_map/pallas_call | solution.py:895
  106.9 12.2 %shard_map.211 = (f32[128,128]{1,0:T(8,128)}, f32[128,1024]{1,0:T(8,128)}, f32[128,1024]{1,0:T(8,128)}, f32[128,128]{1,0:T(8,128)}, f32[16,1024]{1,0:T(8,128)}) custom-call(s32[1]{0:T(128)} %bitcast.282.flag, f32[480,8]{1,0:T(8,128)} %copy.605.refs_0_, f32[1,128]{1,0:T(1,128)} %slice_bitcast_fusion.57.refs_1_, f32[8,128]{1,0:T(8,128)} %mul.9360.refs_2_, ...), custom_call_target="tpu_custom_call" | custom-call | flops 4076863488 | bytes 16777216 | tf_op jit(solution)/shard_map/pallas_call | solution.py:895
  119.1 13.3 %collective-permute-done.106.refs_6_.refs_4_ = f32[192,1152]{1,0:T(8,128)} collective-permute-done((f32[192,1152]{1,0:T(8,128)}, f32[192,1152]{1,0:T(8,128)}, u32[]{:S(2)}, u32[]{:S(2)}) %collective-permute-start.106) | collective-permute-done | bytes 884768 | tf_op jit(solution)/shard_map/ppermute | solution.py:40
  132.4 15.8 %shard_map.213 = (f32[192,128]{1,0:T(8,128)}, f32[192,1024]{1,0:T(8,128)}, f32[192,1024]{1,0:T(8,128)}, f32[192,128]{1,0:T(8,128)}, f32[16,1024]{1,0:T(8,128)}) custom-call(s32[1]{0:T(128)} %bitcast.282.flag, f32[480,8]{1,0:T(8,128)} %copy.605.refs_0_, f32[1,192]{1,0:T(1,128)} %slice_bitcast_fusion.56.refs_1_, f32[8,128]{1,0:T(8,128)} %mul.9360.refs_2_, ...), custom_call_target="tpu_custom_call" | custom-call | flops 6115295232 | bytes 16777216 | tf_op jit(solution)/shard_map/pallas_call | solution.py:895
  148.2 9.5 %collective-permute-done.108.refs_5_.refs_6_ = f32[160,1152]{1,0:T(8,128)S(1)} collective-permute-done((f32[160,1152]{1,0:T(8,128)}, f32[160,1152]{1,0:T(8,128)S(1)}, u32[]{:S(2)}, u32[]{:S(2)}) %collective-permute-start.108) | collective-permute-done | bytes 737312 | tf_op jit(solution)/shard_map/ppermute | solution.py:40
  158.6 7.0 %shard_map.214 = (f32[512,1024]{1,0:T(8,128)}, f32[512,1024]{1,0:T(8,128)}) custom-call(s32[1]{0:T(128)S(6)} %sub.753.flag.chosen, f32[128,1024]{1,0:T(8,128)} %get-tuple-element.1011.refs_0_, f32[192,1024]{1,0:T(8,128)} %get-tuple-element.1012.refs_1_, f32[160,1024]{1,0:T(8,128)} %get-tuple-element.1013.refs_2_, f32[128,1152]{1,0:T(8,128)} %copy-done.269, ...), custom_call_target="tpu_custom_call" | custom-call | flops 3019898880 | bytes 16777216 | tf_op jit(solution)/shard_map/pallas_call | solution.py:909
  167.5 14.3 %shard_map.215 = (f32[160,128]{1,0:T(8,128)}, f32[160,1024]{1,0:T(8,128)}, f32[160,1024]{1,0:T(8,128)}, f32[160,128]{1,0:T(8,128)}, f32[16,1024]{1,0:T(8,128)}) custom-call(s32[1]{0:T(128)} %bitcast.282.flag, f32[480,8]{1,0:T(8,128)} %copy.605.refs_0_, f32[1,160]{1,0:T(1,128)} %slice_bitcast_fusion.55.refs_1_, f32[8,128]{1,0:T(8,128)} %mul.9360.refs_2_, ...), custom_call_target="tpu_custom_call" | custom-call | flops 5096079360 | bytes 16777216 | tf_op jit(solution)/shard_map/pallas_call | solution.py:895
  188.8 9.1 %shard_map.216 = (f32[1280,512]{1,0:T(8,128)}, f32[1280,512]{1,0:T(8,128)}, f32[1024,128]{1,0:T(8,128)}) custom-call(s32[1]{0:T(128)S(6)} %sub.753.flag.chosen, f32[128,1280]{1,0:T(8,128)} %get-tuple-element.1018.refs_4_.refs_0_, f32[192,1280]{1,0:T(8,128)} %get-tuple-element.1024.refs_4_.refs_1_, f32[160,1280]{1,0:T(8,128)} %get-tuple-element.1038.refs_4_.refs_2_, ...), custom_call_target="tpu_custom_call" | custom-call | flops 3019898880 | bytes 16777216 | tf_op jit(solution)/shard_map/pallas_call | solution.py:909
  205.9 6.9 %shard_map.217 = (f32[1024,512]{1,0:T(8,128)}, f32[1024,512]{1,0:T(8,128)}) custom-call(s32[1]{0:T(128)S(6)} %sub.753.flag.chosen, f32[128,1024]{1,0:T(8,128)} %get-tuple-element.1060.refs_0_, f32[192,1024]{1,0:T(8,128)} %get-tuple-element.1061.refs_1_, f32[160,1024]{1,0:T(8,128)} %get-tuple-element.1062.refs_2_, f32[128,1024]{1,0:T(8,128)} %get-tuple-element.1063.refs_3_, ...), custom_call_target="tpu_custom_call" | custom-call | flops 3019898880 | bytes 16777216 | tf_op jit(solution)/shard_map/pallas_call | solution.py:909
  233.5 11.2 %collective-permute-done.118 = f32[320,512]{1,0:T(8,128)S(1)} collective-permute-done((f32[320,512]{1,0:T(8,128)S(1)}, f32[320,512]{1,0:T(8,128)S(1)}, u32[]{:S(2)}, u32[]{:S(2)}) %collective-permute-start.118) | collective-permute-done | bytes 655392 | tf_op jit(solution)/shard_map/ppermute | solution.py:1032
  258.1 8.7 %collective-permute-start.126 = (f32[64,1024]{1,0:T(8,128)S(1)}, f32[64,1024]{1,0:T(8,128)S(1)}, u32[]{:S(2)}, u32[]{:S(2)}) collective-permute-start(f32[64,1024]{1,0:T(8,128)S(1)} %dynamic-slice_add_fusion.11), channel_id=1, source_target_pairs={{0,12},{2,14},{4,8},{6,10},{8,4},{10,6},{12,0},{14,2},{1,13},{3,15... | collective-permute-start | bytes 786440 | tf_op jit(solution)/shard_map/ppermute | solution.py:1032
  271.9 10.7 %collective-permute-start.131 = (f32[64,1024]{1,0:T(8,128)S(1)}, f32[64,1024]{1,0:T(8,128)S(1)}, u32[]{:S(2)}, u32[]{:S(2)}) collective-permute-start(f32[64,1024]{1,0:T(8,128)S(1)} %add.1948), channel_id=1, source_target_pairs={{0,4},{2,6},{4,0},{6,2},{8,12},{10,14},{12,8},{14,10},{1,5},{3,7},... | collective-permute-start | bytes 786440 | tf_op jit(solution)/shard_map/ppermute | solution.py:1032
  286.0 15.2 %collective-permute-done.122 = f32[152,512]{1,0:T(8,128)S(1)} collective-permute-done((f32[152,512]{1,0:T(8,128)S(1)}, f32[152,512]{1,0:T(8,128)S(1)}, u32[]{:S(2)}, u32[]{:S(2)}) %collective-permute-start.122) | collective-permute-done | bytes 311328 | tf_op jit(solution)/shard_map/ppermute | solution.py:1032
  301.4 4.2 %collective-permute-start.144 = (f32[3,1152]{1,0:T(4,128)S(1)}, f32[3,1152]{1,0:T(4,128)S(1)}, u32[]{:S(2)}, u32[]{:S(2)}) collective-permute-start(f32[3,1152]{1,0:T(4,128)S(1)} %get-tuple-element.1960), channel_id=1, source_target_pairs={{0,2},{2,4},{4,6},{6,8},{8,10},{10,12},{12,14},{1,3},{3,5},{5,7},{... | collective-permute-start | bytes 41480 | tf_op jit(solution)/shard_map/ppermute | solution.py:40
  335.9 4.0 %collective-permute-done.132 = f32[152,512]{1,0:T(8,128)S(1)} collective-permute-done((f32[152,512]{1,0:T(8,128)S(1)}, f32[152,512]{1,0:T(8,128)S(1)}, u32[]{:S(2)}, u32[]{:S(2)}) %collective-permute-start.132) | collective-permute-done | bytes 311328 | tf_op jit(solution)/shard_map/ppermute | solution.py:1032
  340.4 6.5 %collective-permute-done.139 = f32[160,512]{1,0:T(8,128)S(1)} collective-permute-done((f32[160,512]{1,0:T(8,128)S(1)}, f32[160,512]{1,0:T(8,128)S(1)}, u32[]{:S(2)}, u32[]{:S(2)}) %collective-permute-start.139) | collective-permute-done | bytes 327712 | tf_op jit(solution)/shard_map/ppermute | solution.py:1032
  347.1 4.7 %collective-permute-done.138 = f32[152,512]{1,0:T(8,128)S(1)} collective-permute-done((f32[152,512]{1,0:T(8,128)S(1)}, f32[152,512]{1,0:T(8,128)S(1)}, u32[]{:S(2)}, u32[]{:S(2)}) %collective-permute-start.138) | collective-permute-done | bytes 311328 | tf_op jit(solution)/shard_map/ppermute | solution.py:1032
  354.2 8.9 %collective-permute-done.136 = f32[128,1024]{1,0:T(8,128)S(1)} collective-permute-done((f32[128,1024]{1,0:T(8,128)S(1)}, f32[128,1024]{1,0:T(8,128)S(1)}, u32[]{:S(2)}, u32[]{:S(2)}) %collective-permute-start.136) | collective-permute-done | bytes 524320 | tf_op jit(solution)/shard_map/ppermute | solution.py:1032
  364.9 11.6 %collective-permute-done.135 = f32[304,512]{1,0:T(8,128)S(1)} collective-permute-done((f32[304,512]{1,0:T(8,128)S(1)}, f32[304,512]{1,0:T(8,128)S(1)}, u32[]{:S(2)}, u32[]{:S(2)}) %collective-permute-start.135) | collective-permute-done | bytes 622624 | tf_op jit(solution)/shard_map/ppermute | solution.py:1032
  377.4 9.0 %collective-permute-done.141 = f32[320,512]{1,0:T(8,128)S(1)} collective-permute-done((f32[320,512]{1,0:T(8,128)S(1)}, f32[320,512]{1,0:T(8,128)S(1)}, u32[]{:S(2)}, u32[]{:S(2)}) %collective-permute-start.141) | collective-permute-done | bytes 655392 | tf_op jit(solution)/shard_map/ppermute | solution.py:1032
  (296 shorter events, 152.2 us)
Async XLA Ops:
  5.1 26.5 %collective-permute-start.100 = (f32[1024,512]{1,0:T(8,128)}, f32[1024,512]{1,0:T(8,128)}, u32[]{:S(2)}, u32[]{:S(2)}) collective-permute-start(f32[1024,512]{1,0:T(8,128)} %bitcast.1906), channel_id=1, source_target_pairs={{0,1},{1,0},{2,3},{3,2},{4,5},{5,4},{6,7},{7,6},{8,9},{9,8},{10,11... | collective-permute-start | bytes 6291464 | tf_op jit(solution)/shard_map/ppermute | solution.py:44
  5.1 26.5 %collective-permute-start.102 = (f32[512,1024]{1,0:T(8,128)}, f32[512,1024]{1,0:T(8,128)}, u32[]{:S(2)}, u32[]{:S(2)}) collective-permute-start(f32[512,1024]{1,0:T(8,128)} %bitcast.2016), channel_id=1, source_target_pairs={{0,1},{1,0},{2,3},{3,2},{4,5},{5,4},{6,7},{7,6},{8,9},{9,8},{10,11... | collective-permute-start | bytes 6291464 | tf_op jit(solution)/shard_map/ppermute | solution.py:44
  5.6 26.0 %collective-permute-start.101 = (f32[1216,512]{1,0:T(8,128)}, f32[1216,512]{1,0:T(8,128)}, u32[]{:S(2)}, u32[]{:S(2)}) collective-permute-start(f32[1216,512]{1,0:T(8,128)} %bitcast.1896), channel_id=1, source_target_pairs={{0,1},{1,0},{2,3},{3,2},{4,5},{5,4},{6,7},{7,6},{8,9},{9,8},{10,11... | collective-permute-start | bytes 7471112 | tf_op jit(solution)/shard_map/ppermute | solution.py:44
  43.7 34.0 %collective-permute-start.103 = (f32[128,1152]{1,0:T(8,128)}, f32[128,1152]{1,0:T(8,128)S(1)}, u32[]{:S(2)}, u32[]{:S(2)}) collective-permute-start(f32[128,1152]{1,0:T(8,128)} %get-tuple-element.1014), channel_id=1, source_target_pairs={{0,16},{1,17},{2,18},{3,19},{4,20},{5,21},{6,22},{7,23},{8,24},{9,... | collective-permute-start | bytes 1769480 | tf_op jit(solution)/shard_map/ppermute | solution.py:40
  60.6 21.7 %collective-permute-start.105 = (f32[192,1152]{1,0:T(8,128)}, f32[192,1152]{1,0:T(8,128)}, u32[]{:S(2)}, u32[]{:S(2)}) collective-permute-start(f32[192,1152]{1,0:T(8,128)} %get-tuple-element.1016), channel_id=1, source_target_pairs={{0,16},{1,17},{2,18},{3,19},{4,20},{5,21},{6,22},{7,23},{8,24},{9,... | collective-permute-start | bytes 2654216 | tf_op jit(solution)/shard_map/ppermute | solution.py:40
  80.1 26.0 %collective-permute-start.104 = (f32[128,1152]{1,0:T(8,128)}, f32[128,1152]{1,0:T(8,128)S(1)}, u32[]{:S(2)}, u32[]{:S(2)}) collective-permute-start(f32[128,1152]{1,0:T(8,128)} %get-tuple-element.1015), channel_id=1, source_target_pairs={{16,0},{17,1},{18,2},{19,3},{20,4},{21,5},{22,6},{23,7},{24,8},{25... | collective-permute-start | bytes 1769480 | tf_op jit(solution)/shard_map/ppermute | solution.py:40
  93.1 39.3 %collective-permute-start.106 = (f32[192,1152]{1,0:T(8,128)}, f32[192,1152]{1,0:T(8,128)}, u32[]{:S(2)}, u32[]{:S(2)}) collective-permute-start(f32[192,1152]{1,0:T(8,128)} %get-tuple-element.1017), channel_id=1, source_target_pairs={{16,0},{17,1},{18,2},{19,3},{20,4},{21,5},{22,6},{23,7},{24,8},{25... | collective-permute-start | bytes 2654216 | tf_op jit(solution)/shard_map/ppermute | solution.py:40
  104.8 52.9 %collective-permute-start.108 = (f32[160,1152]{1,0:T(8,128)}, f32[160,1152]{1,0:T(8,128)S(1)}, u32[]{:S(2)}, u32[]{:S(2)}) collective-permute-start(f32[160,1152]{1,0:T(8,128)} %get-tuple-element.1023), channel_id=1, source_target_pairs={{16,0},{17,1},{18,2},{19,3},{20,4},{21,5},{22,6},{23,7},{24,8},{25... | collective-permute-start | bytes 2211848 | tf_op jit(solution)/shard_map/ppermute | solution.py:40
  199.1 23.8 %collective-permute-start.114 = (f32[1280,512]{1,0:T(8,128)}, f32[1280,512]{1,0:T(8,128)}, u32[]{:S(2)}, u32[]{:S(2)}) collective-permute-start(f32[1280,512]{1,0:T(8,128)} %get-tuple-element.1056), channel_id=1, source_target_pairs={{0,1},{1,0},{2,3},{3,2},{4,5},{5,4},{6,7},{7,6},{8,9},{9,8},{10,11... | collective-permute-start | bytes 7864328 | tf_op jit(solution)/shard_map/ppermute | solution.py:44
  221.6 26.3 %collective-permute-start.117 = (f32[64,1024]{1,0:T(8,128)S(1)}, f32[64,1024]{1,0:T(8,128)S(1)}, u32[]{:S(2)}, u32[]{:S(2)}) collective-permute-start(f32[64,1024]{1,0:T(8,128)S(1)} %copy-done.289), channel_id=1, source_target_pairs={{0,4},{2,6},{4,0},{6,2},{8,12},{10,14},{12,8},{14,10},{1,5},{3,7},... | collective-permute-start | bytes 786440 | tf_op jit(solution)/shard_map/ppermute | solution.py:1032
  232.3 22.8 %collective-permute-start.120 = (f32[304,512]{1,0:T(8,128)S(1)}, f32[304,512]{1,0:T(8,128)S(1)}, u32[]{:S(2)}, u32[]{:S(2)}) collective-permute-start(f32[304,512]{1,0:T(8,128)S(1)} %get-tuple-element.1091), channel_id=1, source_target_pairs={{0,4},{2,6},{4,0},{6,2},{8,12},{10,14},{12,8},{14,10},{1,5},{3,7},... | collective-permute-start | bytes 1867784 | tf_op jit(solution)/shard_map/ppermute | solution.py:1032
  245.9 22.4 %collective-permute-start.116 = (f32[304,512]{1,0:T(8,128)S(1)}, f32[304,512]{1,0:T(8,128)S(1)}, u32[]{:S(2)}, u32[]{:S(2)}) collective-permute-start(f32[304,512]{1,0:T(8,128)S(1)} %get-tuple-element.1092), channel_id=1, source_target_pairs={{0,2},{2,0},{4,6},{6,4},{8,10},{10,8},{12,14},{14,12},{1,3},{3,1},... | collective-permute-start | bytes 1867784 | tf_op jit(solution)/shard_map/ppermute | solution.py:1032
  255.2 30.5 %collective-permute-start.124 = (f32[320,512]{1,0:T(8,128)S(1)}, f32[320,512]{1,0:T(8,128)S(1)}, u32[]{:S(2)}, u32[]{:S(2)}) collective-permute-start(f32[320,512]{1,0:T(8,128)S(1)} %constant_dynamic-slice_fusion.105), channel_id=1, source_target_pairs={{0,2},{2,0},{4,6},{6,4},{8,10},{10,8},{12,14},{14,12},{1,3},{3,1},... | collective-permute-start | bytes 1966088 | tf_op jit(solution)/shard_map/ppermute | solution.py:1032
  271.9 29.5 %collective-permute-start.131 = (f32[64,1024]{1,0:T(8,128)S(1)}, f32[64,1024]{1,0:T(8,128)S(1)}, u32[]{:S(2)}, u32[]{:S(2)}) collective-permute-start(f32[64,1024]{1,0:T(8,128)S(1)} %add.1948), channel_id=1, source_target_pairs={{0,4},{2,6},{4,0},{6,2},{8,12},{10,14},{12,8},{14,10},{1,5},{3,7},... | collective-permute-start | bytes 786440 | tf_op jit(solution)/shard_map/ppermute | solution.py:1032
  282.7 35.8 %collective-permute-start.129 = (f32[152,512]{1,0:T(8,128)S(1)}, f32[152,512]{1,0:T(8,128)S(1)}, u32[]{:S(2)}, u32[]{:S(2)}) collective-permute-start(f32[152,512]{1,0:T(8,128)S(1)} %dynamic-slice_add_fusion.8), channel_id=1, source_target_pairs={{0,12},{2,14},{4,8},{6,10},{8,4},{10,6},{12,0},{14,2},{1,13},{3,15... | collective-permute-start | bytes 933896 | tf_op jit(solution)/shard_map/ppermute | solution.py:1032
  285.9 26.0 %collective-permute-start.130 = (f32[160,512]{1,0:T(8,128)S(1)}, f32[160,512]{1,0:T(8,128)S(1)}, u32[]{:S(2)}, u32[]{:S(2)}) collective-permute-start(f32[160,512]{1,0:T(8,128)S(1)} %constant_dynamic-slice_fusion.102), channel_id=1, source_target_pairs={{0,4},{2,6},{4,0},{6,2},{8,12},{10,14},{12,8},{14,10},{1,5},{3,7},... | collective-permute-start | bytes 983048 | tf_op jit(solution)/shard_map/ppermute | solution.py:1032
  301.3 28.2 %collective-permute-start.127 = (f32[152,512]{1,0:T(8,128)S(1)}, f32[152,512]{1,0:T(8,128)S(1)}, u32[]{:S(2)}, u32[]{:S(2)}) collective-permute-start(f32[152,512]{1,0:T(8,128)S(1)} %dynamic-slice_add_fusion.9), channel_id=1, source_target_pairs={{0,12},{2,14},{4,8},{6,10},{8,4},{10,6},{12,0},{14,2},{1,13},{3,15... | collective-permute-start | bytes 933896 | tf_op jit(solution)/shard_map/ppermute | solution.py:1032
  312.3 20.7 %collective-permute-start.134 = (f32[160,512]{1,0:T(8,128)S(1)}, f32[160,512]{1,0:T(8,128)S(1)}, u32[]{:S(2)}, u32[]{:S(2)}) collective-permute-start(f32[160,512]{1,0:T(8,128)S(1)} %dynamic-slice_add_fusion.6), channel_id=1, source_target_pairs={{0,12},{2,14},{4,8},{6,10},{8,4},{10,6},{12,0},{14,2},{1,13},{3,15... | collective-permute-start | bytes 983048 | tf_op jit(solution)/shard_map/ppermute | solution.py:1032
  326.1 25.9 %collective-permute-start.137 = (f32[320,512]{1,0:T(8,128)S(1)}, f32[320,512]{1,0:T(8,128)S(1)}, u32[]{:S(2)}, u32[]{:S(2)}) collective-permute-start(f32[320,512]{1,0:T(8,128)S(1)} %get-tuple-element.1679), channel_id=1, source_target_pairs={{0,2},{2,0},{4,6},{6,4},{8,10},{10,8},{12,14},{14,12},{1,3},{3,1},... | collective-permute-start | bytes 1966088 | tf_op jit(solution)/shard_map/ppermute | solution.py:1032
  333.8 29.3 %collective-permute-start.136 = (f32[128,1024]{1,0:T(8,128)S(1)}, f32[128,1024]{1,0:T(8,128)S(1)}, u32[]{:S(2)}, u32[]{:S(2)}) collective-permute-start(f32[128,1024]{1,0:T(8,128)S(1)} %maximum_select_fusion.53), channel_id=1, source_target_pairs={{0,2},{2,0},{4,6},{6,4},{8,10},{10,8},{12,14},{14,12},{1,3},{3,1},... | collective-permute-start | bytes 1572872 | tf_op jit(solution)/shard_map/ppermute | solution.py:1032
  340.4 36.1 %collective-permute-start.142 = (f32[128,1024]{1,0:T(8,128)S(1)}, f32[128,1024]{1,0:T(8,128)S(1)}, u32[]{:S(2)}, u32[]{:S(2)}) collective-permute-start(f32[128,1024]{1,0:T(8,128)S(1)} %maximum_select_fusion.54), channel_id=1, source_target_pairs={{0,4},{2,6},{4,0},{6,2},{8,12},{10,14},{12,8},{14,10},{1,5},{3,7},... | collective-permute-start | bytes 1572872 | tf_op jit(solution)/shard_map/ppermute | solution.py:1032
  347.0 29.4 %collective-permute-start.135 = (f32[304,512]{1,0:T(8,128)S(1)}, f32[304,512]{1,0:T(8,128)S(1)}, u32[]{:S(2)}, u32[]{:S(2)}) collective-permute-start(f32[304,512]{1,0:T(8,128)S(1)} %get-tuple-element.1681), channel_id=1, source_target_pairs={{0,2},{2,0},{4,6},{6,4},{8,10},{10,8},{12,14},{14,12},{1,3},{3,1},... | collective-permute-start | bytes 1867784 | tf_op jit(solution)/shard_map/ppermute | solution.py:1032
  351.9 34.4 %collective-permute-start.140 = (f32[304,512]{1,0:T(8,128)S(1)}, f32[304,512]{1,0:T(8,128)S(1)}, u32[]{:S(2)}, u32[]{:S(2)}) collective-permute-start(f32[304,512]{1,0:T(8,128)S(1)} %maximum_select_fusion.52), channel_id=1, source_target_pairs={{0,4},{2,6},{4,0},{6,2},{8,12},{10,14},{12,8},{14,10},{1,5},{3,7},... | collective-permute-start | bytes 1867784 | tf_op jit(solution)/shard_map/ppermute | solution.py:1032
  352.1 34.3 %collective-permute-start.141 = (f32[320,512]{1,0:T(8,128)S(1)}, f32[320,512]{1,0:T(8,128)S(1)}, u32[]{:S(2)}, u32[]{:S(2)}) collective-permute-start(f32[320,512]{1,0:T(8,128)S(1)} %maximum_select_fusion.50), channel_id=1, source_target_pairs={{0,2},{2,0},{4,6},{6,4},{8,10},{10,8},{12,14},{14,12},{1,3},{3,1},... | collective-permute-start | bytes 1966088 | tf_op jit(solution)/shard_map/ppermute | solution.py:1032
  (50 other events, 501.5 us)

commit v6 on v5

--- a/solution.py
+++ b/solution.py
@@ -441,9 +441,11 @@
     return 0 if component == 0 else (1 if component < 4 else 2)
 
 
-def same_sum(same, parts):
-    high, middle, low = split_three(jnp.concatenate(parts, axis=1))
-    summed = dot_nn(same, high) + (dot_nn(same, middle) + dot_nn(same, low))
+def same_sum(same, parts, split=split_three):
+    pieces = split(jnp.concatenate(parts, axis=1))
+    summed = dot_nn(same, pieces[-1])
+    for piece in pieces[-2::-1]:
+        summed = dot_nn(same, piece) + summed
     return [summed[:, LANES * m : LANES * (m + 1)] for m in range(len(parts))]
 
 
@@ -564,7 +566,7 @@
 
 
 def env_pull(g, weight, d_env):
-    d_terms = same_sum(g["same"], d_env)
+    d_terms = same_sum(g["same"], d_env, split_two)
     d_weight, d_harm, inner = None, [], None
     for m in range(9):
         part = g["harm"][m] * d_terms[m]

time: 403 us -> 402 us (level)
  no operation moved by 1% of the time
where the time goes in v6:
time: 402 us; the launch traced here: 396 us
  Pallas kernels  127 us (32%)
  waiting for transfers between devices  117 us (29%)
  starting transfers between devices  78.4 us (20%)
  local copies, waits for them, and re-layouts  37.9 us (9%)
  other arithmetic  26.9 us (7%)
  matrix products  5.46 us (1%)
    pallas_call x9, Pallas kernels, on_core(): pl.pallas_call(guarded, out_shape=tuple((jax.ShapeDtypeStruct(shape, F32)...  102 us
    ppermute x30, waiting for transfers between devices, hop(): return lax.ppermute(value, 'edge', [(i, i ^ distance) for i in range(8)])  88.5 us
    ppermute x30, starting transfers between devices, hop(): return lax.ppermute(value, 'edge', [(i, i ^ distance) for i in range(8)])  51.9 us
    ppermute x9, waiting for transfers between devices, shifted(): lax.ppermute(value, axis, [(source, source + steps) for source in range(f...  25.5 us
    pallas_call x3, Pallas kernels, outer_call(): pl.pallas_call(partial(outer_sum, split_left), out_shape=tuple((jax.Shape...  23 us
    ppermute x9, starting transfers between devices, shifted(): lax.ppermute(value, axis, [(source, source + steps) for source in range(f...  18.3 us
    unnamed x52, local copies, waits for them, and re-layouts  8.71 us
  transfers between devices with their start and end apart: 50, of which 20 were waited for; matrix products, arithmetic and copies ran while one was open for 13% of the time, Pallas kernels for 27%

profile of v6, /device:TPU:0, one launch (start us, length us, event | category | flops | bytes accessed | tf_op | source)
XLA Modules:
  0.0 395.9 jit_solution(3565253114025780287)
XLA Ops:
  32.2 11.5 %shard_map.206 = (f32[128,1152]{1,0:T(8,128)}, f32[128,1024]{1,0:T(8,128)}, f32[128,1280]{1,0:T(8,128)}, f32[128,1024]{1,0:T(8,128)}, f32[128,1024]{1,0:T(8,128)}) custom-call(s32[1]{0:T(128)} %bitcast.282.flag, f32[480,8]{1,0:T(8,128)} %copy.605.refs_0_, f32[1,128]{1,0:T(1,128)} %slice_bitcast_fusion.57.refs_1_, f32[8,128]{1,0:T(8,128)} %mul.9360.refs_2_, ...), custom_call_target="tpu_custom_call" | custom-call | flops 5435817984 | bytes 16777216 | tf_op jit(solution)/shard_map/pallas_call | solution.py:897
  45.0 15.6 %shard_map.207 = (f32[192,1152]{1,0:T(8,128)}, f32[192,1024]{1,0:T(8,128)}, f32[192,1280]{1,0:T(8,128)}, f32[192,1024]{1,0:T(8,128)}, f32[192,1024]{1,0:T(8,128)}) custom-call(s32[1]{0:T(128)} %bitcast.282.flag, f32[480,8]{1,0:T(8,128)} %copy.605.refs_0_, f32[1,192]{1,0:T(1,128)} %slice_bitcast_fusion.56.refs_1_, f32[8,128]{1,0:T(8,128)} %mul.9360.refs_2_, ...), custom_call_target="tpu_custom_call" | custom-call | flops 8153726976 | bytes 16777216 | tf_op jit(solution)/shard_map/pallas_call | solution.py:897
  62.9 13.4 %shard_map.208 = (f32[160,1152]{1,0:T(8,128)}, f32[160,1024]{1,0:T(8,128)}, f32[160,1280]{1,0:T(8,128)}, f32[160,1024]{1,0:T(8,128)}, f32[160,1024]{1,0:T(8,128)}) custom-call(s32[1]{0:T(128)} %bitcast.282.flag, f32[480,8]{1,0:T(8,128)} %copy.605.refs_0_, f32[1,160]{1,0:T(1,128)} %slice_bitcast_fusion.55.refs_1_, f32[8,128]{1,0:T(8,128)} %mul.9360.refs_2_, ...), custom_call_target="tpu_custom_call" | custom-call | flops 6794772480 | bytes 16777216 | tf_op jit(solution)/shard_map/pallas_call | solution.py:897
  82.3 10.6 %shard_map.210 = (f32[192,1152]{1,0:T(8,128)}, f32[192,1280]{1,0:T(8,128)}, f32[192,1024]{1,0:T(8,128)}, f32[192,1024]{1,0:T(8,128)}, f32[192,1024]{1,0:T(8,128)...) custom-call(s32[1]{0:T(128)S(6)} %sub.753.flag.chosen, ...), custom_call_target="tpu_custom_call" | custom-call | flops 12230590464 | bytes 16777216 | tf_op jit(solution)/shard_map/pallas_call | solution.py:897
  97.1 7.6 %shard_map.212 = (f32[160,1152]{1,0:T(8,128)}, f32[160,1280]{1,0:T(8,128)}, f32[160,1024]{1,0:T(8,128)}, f32[160,1024]{1,0:T(8,128)}, f32[160,1024]{1,0:T(8,128)...) custom-call(s32[1]{0:T(128)S(6)} %sub.753.flag.chosen, ...), custom_call_target="tpu_custom_call" | custom-call | flops 10192158720 | bytes 16777216 | tf_op jit(solution)/shard_map/pallas_call | solution.py:897
  106.9 12.1 %shard_map.211 = (f32[128,128]{1,0:T(8,128)}, f32[128,1024]{1,0:T(8,128)}, f32[128,1024]{1,0:T(8,128)}, f32[128,128]{1,0:T(8,128)}, f32[16,1024]{1,0:T(8,128)}) custom-call(s32[1]{0:T(128)} %bitcast.282.flag, f32[480,8]{1,0:T(8,128)} %copy.605.refs_0_, f32[1,128]{1,0:T(1,128)} %slice_bitcast_fusion.57.refs_1_, f32[8,128]{1,0:T(8,128)} %mul.9360.refs_2_, ...), custom_call_target="tpu_custom_call" | custom-call | flops 4076863488 | bytes 16777216 | tf_op jit(solution)/shard_map/pallas_call | solution.py:897
  119.1 12.9 %collective-permute-done.106.refs_6_.refs_4_ = f32[192,1152]{1,0:T(8,128)} collective-permute-done((f32[192,1152]{1,0:T(8,128)}, f32[192,1152]{1,0:T(8,128)}, u32[]{:S(2)}, u32[]{:S(2)}) %collective-permute-start.106) | collective-permute-done | bytes 884768 | tf_op jit(solution)/shard_map/ppermute | solution.py:40
  132.0 15.5 %shard_map.213 = (f32[192,128]{1,0:T(8,128)}, f32[192,1024]{1,0:T(8,128)}, f32[192,1024]{1,0:T(8,128)}, f32[192,128]{1,0:T(8,128)}, f32[16,1024]{1,0:T(8,128)}) custom-call(s32[1]{0:T(128)} %bitcast.282.flag, f32[480,8]{1,0:T(8,128)} %copy.605.refs_0_, f32[1,192]{1,0:T(1,128)} %slice_bitcast_fusion.56.refs_1_, f32[8,128]{1,0:T(8,128)} %mul.9360.refs_2_, ...), custom_call_target="tpu_custom_call" | custom-call | flops 6115295232 | bytes 16777216 | tf_op jit(solution)/shard_map/pallas_call | solution.py:897
  147.5 9.6 %collective-permute-done.108.refs_5_.refs_6_ = f32[160,1152]{1,0:T(8,128)S(1)} collective-permute-done((f32[160,1152]{1,0:T(8,128)}, f32[160,1152]{1,0:T(8,128)S(1)}, u32[]{:S(2)}, u32[]{:S(2)}) %collective-permute-start.108) | collective-permute-done | bytes 737312 | tf_op jit(solution)/shard_map/ppermute | solution.py:40
  158.0 7.0 %shard_map.214 = (f32[512,1024]{1,0:T(8,128)}, f32[512,1024]{1,0:T(8,128)}) custom-call(s32[1]{0:T(128)S(6)} %sub.753.flag.chosen, f32[128,1024]{1,0:T(8,128)} %get-tuple-element.1011.refs_0_, f32[192,1024]{1,0:T(8,128)} %get-tuple-element.1012.refs_1_, f32[160,1024]{1,0:T(8,128)} %get-tuple-element.1013.refs_2_, f32[128,1152]{1,0:T(8,128)} %copy-done.269, ...), custom_call_target="tpu_custom_call" | custom-call | flops 3019898880 | bytes 16777216 | tf_op jit(solution)/shard_map/pallas_call | solution.py:911
  166.8 14.1 %shard_map.215 = (f32[160,128]{1,0:T(8,128)}, f32[160,1024]{1,0:T(8,128)}, f32[160,1024]{1,0:T(8,128)}, f32[160,128]{1,0:T(8,128)}, f32[16,1024]{1,0:T(8,128)}) custom-call(s32[1]{0:T(128)} %bitcast.282.flag, f32[480,8]{1,0:T(8,128)} %copy.605.refs_0_, f32[1,160]{1,0:T(1,128)} %slice_bitcast_fusion.55.refs_1_, f32[8,128]{1,0:T(8,128)} %mul.9360.refs_2_, ...), custom_call_target="tpu_custom_call" | custom-call | flops 5096079360 | bytes 16777216 | tf_op jit(solution)/shard_map/pallas_call | solution.py:897
  187.9 9.1 %shard_map.216 = (f32[1280,512]{1,0:T(8,128)}, f32[1280,512]{1,0:T(8,128)}, f32[1024,128]{1,0:T(8,128)}) custom-call(s32[1]{0:T(128)S(6)} %sub.753.flag.chosen, f32[128,1280]{1,0:T(8,128)} %get-tuple-element.1018.refs_4_.refs_0_, f32[192,1280]{1,0:T(8,128)} %get-tuple-element.1024.refs_4_.refs_1_, f32[160,1280]{1,0:T(8,128)} %get-tuple-element.1038.refs_4_.refs_2_, ...), custom_call_target="tpu_custom_call" | custom-call | flops 3019898880 | bytes 16777216 | tf_op jit(solution)/shard_map/pallas_call | solution.py:911
  205.1 6.9 %shard_map.217 = (f32[1024,512]{1,0:T(8,128)}, f32[1024,512]{1,0:T(8,128)}) custom-call(s32[1]{0:T(128)S(6)} %sub.753.flag.chosen, f32[128,1024]{1,0:T(8,128)} %get-tuple-element.1060.refs_0_, f32[192,1024]{1,0:T(8,128)} %get-tuple-element.1061.refs_1_, f32[160,1024]{1,0:T(8,128)} %get-tuple-element.1062.refs_2_, f32[128,1024]{1,0:T(8,128)} %get-tuple-element.1063.refs_3_, ...), custom_call_target="tpu_custom_call" | custom-call | flops 3019898880 | bytes 16777216 | tf_op jit(solution)/shard_map/pallas_call | solution.py:911
  232.7 11.2 %collective-permute-done.118 = f32[320,512]{1,0:T(8,128)S(1)} collective-permute-done((f32[320,512]{1,0:T(8,128)S(1)}, f32[320,512]{1,0:T(8,128)S(1)}, u32[]{:S(2)}, u32[]{:S(2)}) %collective-permute-start.118) | collective-permute-done | bytes 655392 | tf_op jit(solution)/shard_map/ppermute | solution.py:1034
  257.2 8.7 %collective-permute-start.126 = (f32[64,1024]{1,0:T(8,128)S(1)}, f32[64,1024]{1,0:T(8,128)S(1)}, u32[]{:S(2)}, u32[]{:S(2)}) collective-permute-start(f32[64,1024]{1,0:T(8,128)S(1)} %dynamic-slice_add_fusion.11), channel_id=1, source_target_pairs={{0,12},{2,14},{4,8},{6,10},{8,4},{10,6},{12,0},{14,2},{1,13},{3,15... | collective-permute-start | bytes 786440 | tf_op jit(solution)/shard_map/ppermute | solution.py:1034
  271.1 10.7 %collective-permute-start.131 = (f32[64,1024]{1,0:T(8,128)S(1)}, f32[64,1024]{1,0:T(8,128)S(1)}, u32[]{:S(2)}, u32[]{:S(2)}) collective-permute-start(f32[64,1024]{1,0:T(8,128)S(1)} %add.1948), channel_id=1, source_target_pairs={{0,4},{2,6},{4,0},{6,2},{8,12},{10,14},{12,8},{14,10},{1,5},{3,7},... | collective-permute-start | bytes 786440 | tf_op jit(solution)/shard_map/ppermute | solution.py:1034
  285.2 15.2 %collective-permute-done.122 = f32[152,512]{1,0:T(8,128)S(1)} collective-permute-done((f32[152,512]{1,0:T(8,128)S(1)}, f32[152,512]{1,0:T(8,128)S(1)}, u32[]{:S(2)}, u32[]{:S(2)}) %collective-permute-start.122) | collective-permute-done | bytes 311328 | tf_op jit(solution)/shard_map/ppermute | solution.py:1034
  300.6 4.2 %collective-permute-start.144 = (f32[3,1152]{1,0:T(4,128)S(1)}, f32[3,1152]{1,0:T(4,128)S(1)}, u32[]{:S(2)}, u32[]{:S(2)}) collective-permute-start(f32[3,1152]{1,0:T(4,128)S(1)} %get-tuple-element.1960), channel_id=1, source_target_pairs={{0,2},{2,4},{4,6},{6,8},{8,10},{10,12},{12,14},{1,3},{3,5},{5,7},{... | collective-permute-start | bytes 41480 | tf_op jit(solution)/shard_map/ppermute | solution.py:40
  335.1 4.0 %collective-permute-done.132 = f32[152,512]{1,0:T(8,128)S(1)} collective-permute-done((f32[152,512]{1,0:T(8,128)S(1)}, f32[152,512]{1,0:T(8,128)S(1)}, u32[]{:S(2)}, u32[]{:S(2)}) %collective-permute-start.132) | collective-permute-done | bytes 311328 | tf_op jit(solution)/shard_map/ppermute | solution.py:1034
  339.6 6.5 %collective-permute-done.139 = f32[160,512]{1,0:T(8,128)S(1)} collective-permute-done((f32[160,512]{1,0:T(8,128)S(1)}, f32[160,512]{1,0:T(8,128)S(1)}, u32[]{:S(2)}, u32[]{:S(2)}) %collective-permute-start.139) | collective-permute-done | bytes 327712 | tf_op jit(solution)/shard_map/ppermute | solution.py:1034
  346.3 4.7 %collective-permute-done.138 = f32[152,512]{1,0:T(8,128)S(1)} collective-permute-done((f32[152,512]{1,0:T(8,128)S(1)}, f32[152,512]{1,0:T(8,128)S(1)}, u32[]{:S(2)}, u32[]{:S(2)}) %collective-permute-start.138) | collective-permute-done | bytes 311328 | tf_op jit(solution)/shard_map/ppermute | solution.py:1034
  353.3 8.9 %collective-permute-done.136 = f32[128,1024]{1,0:T(8,128)S(1)} collective-permute-done((f32[128,1024]{1,0:T(8,128)S(1)}, f32[128,1024]{1,0:T(8,128)S(1)}, u32[]{:S(2)}, u32[]{:S(2)}) %collective-permute-start.136) | collective-permute-done | bytes 524320 | tf_op jit(solution)/shard_map/ppermute | solution.py:1034
  364.0 11.6 %collective-permute-done.135 = f32[304,512]{1,0:T(8,128)S(1)} collective-permute-done((f32[304,512]{1,0:T(8,128)S(1)}, f32[304,512]{1,0:T(8,128)S(1)}, u32[]{:S(2)}, u32[]{:S(2)}) %collective-permute-start.135) | collective-permute-done | bytes 622624 | tf_op jit(solution)/shard_map/ppermute | solution.py:1034
  376.6 9.0 %collective-permute-done.141 = f32[320,512]{1,0:T(8,128)S(1)} collective-permute-done((f32[320,512]{1,0:T(8,128)S(1)}, f32[320,512]{1,0:T(8,128)S(1)}, u32[]{:S(2)}, u32[]{:S(2)}) %collective-permute-start.141) | collective-permute-done | bytes 655392 | tf_op jit(solution)/shard_map/ppermute | solution.py:1034
  (296 shorter events, 152.4 us)
Async XLA Ops:
  5.1 26.5 %collective-permute-start.100 = (f32[1024,512]{1,0:T(8,128)}, f32[1024,512]{1,0:T(8,128)}, u32[]{:S(2)}, u32[]{:S(2)}) collective-permute-start(f32[1024,512]{1,0:T(8,128)} %bitcast.1906), channel_id=1, source_target_pairs={{0,1},{1,0},{2,3},{3,2},{4,5},{5,4},{6,7},{7,6},{8,9},{9,8},{10,11... | collective-permute-start | bytes 6291464 | tf_op jit(solution)/shard_map/ppermute | solution.py:44
  5.1 26.5 %collective-permute-start.102 = (f32[512,1024]{1,0:T(8,128)}, f32[512,1024]{1,0:T(8,128)}, u32[]{:S(2)}, u32[]{:S(2)}) collective-permute-start(f32[512,1024]{1,0:T(8,128)} %bitcast.2016), channel_id=1, source_target_pairs={{0,1},{1,0},{2,3},{3,2},{4,5},{5,4},{6,7},{7,6},{8,9},{9,8},{10,11... | collective-permute-start | bytes 6291464 | tf_op jit(solution)/shard_map/ppermute | solution.py:44
  5.6 26.0 %collective-permute-start.101 = (f32[1216,512]{1,0:T(8,128)}, f32[1216,512]{1,0:T(8,128)}, u32[]{:S(2)}, u32[]{:S(2)}) collective-permute-start(f32[1216,512]{1,0:T(8,128)} %bitcast.1896), channel_id=1, source_target_pairs={{0,1},{1,0},{2,3},{3,2},{4,5},{5,4},{6,7},{7,6},{8,9},{9,8},{10,11... | collective-permute-start | bytes 7471112 | tf_op jit(solution)/shard_map/ppermute | solution.py:44
  43.7 34.0 %collective-permute-start.103 = (f32[128,1152]{1,0:T(8,128)}, f32[128,1152]{1,0:T(8,128)S(1)}, u32[]{:S(2)}, u32[]{:S(2)}) collective-permute-start(f32[128,1152]{1,0:T(8,128)} %get-tuple-element.1014), channel_id=1, source_target_pairs={{0,16},{1,17},{2,18},{3,19},{4,20},{5,21},{6,22},{7,23},{8,24},{9,... | collective-permute-start | bytes 1769480 | tf_op jit(solution)/shard_map/ppermute | solution.py:40
  60.6 21.7 %collective-permute-start.105 = (f32[192,1152]{1,0:T(8,128)}, f32[192,1152]{1,0:T(8,128)}, u32[]{:S(2)}, u32[]{:S(2)}) collective-permute-start(f32[192,1152]{1,0:T(8,128)} %get-tuple-element.1016), channel_id=1, source_target_pairs={{0,16},{1,17},{2,18},{3,19},{4,20},{5,21},{6,22},{7,23},{8,24},{9,... | collective-permute-start | bytes 2654216 | tf_op jit(solution)/shard_map/ppermute | solution.py:40
  80.1 26.0 %collective-permute-start.104 = (f32[128,1152]{1,0:T(8,128)}, f32[128,1152]{1,0:T(8,128)S(1)}, u32[]{:S(2)}, u32[]{:S(2)}) collective-permute-start(f32[128,1152]{1,0:T(8,128)} %get-tuple-element.1015), channel_id=1, source_target_pairs={{16,0},{17,1},{18,2},{19,3},{20,4},{21,5},{22,6},{23,7},{24,8},{25... | collective-permute-start | bytes 1769480 | tf_op jit(solution)/shard_map/ppermute | solution.py:40
  92.9 39.1 %collective-permute-start.106 = (f32[192,1152]{1,0:T(8,128)}, f32[192,1152]{1,0:T(8,128)}, u32[]{:S(2)}, u32[]{:S(2)}) collective-permute-start(f32[192,1152]{1,0:T(8,128)} %get-tuple-element.1017), channel_id=1, source_target_pairs={{16,0},{17,1},{18,2},{19,3},{20,4},{21,5},{22,6},{23,7},{24,8},{25... | collective-permute-start | bytes 2654216 | tf_op jit(solution)/shard_map/ppermute | solution.py:40
  104.8 52.3 %collective-permute-start.108 = (f32[160,1152]{1,0:T(8,128)}, f32[160,1152]{1,0:T(8,128)S(1)}, u32[]{:S(2)}, u32[]{:S(2)}) collective-permute-start(f32[160,1152]{1,0:T(8,128)} %get-tuple-element.1023), channel_id=1, source_target_pairs={{16,0},{17,1},{18,2},{19,3},{20,4},{21,5},{22,6},{23,7},{24,8},{25... | collective-permute-start | bytes 2211848 | tf_op jit(solution)/shard_map/ppermute | solution.py:40
  198.3 23.8 %collective-permute-start.114 = (f32[1280,512]{1,0:T(8,128)}, f32[1280,512]{1,0:T(8,128)}, u32[]{:S(2)}, u32[]{:S(2)}) collective-permute-start(f32[1280,512]{1,0:T(8,128)} %get-tuple-element.1056), channel_id=1, source_target_pairs={{0,1},{1,0},{2,3},{3,2},{4,5},{5,4},{6,7},{7,6},{8,9},{9,8},{10,11... | collective-permute-start | bytes 7864328 | tf_op jit(solution)/shard_map/ppermute | solution.py:44
  220.7 26.3 %collective-permute-start.117 = (f32[64,1024]{1,0:T(8,128)S(1)}, f32[64,1024]{1,0:T(8,128)S(1)}, u32[]{:S(2)}, u32[]{:S(2)}) collective-permute-start(f32[64,1024]{1,0:T(8,128)S(1)} %copy-done.289), channel_id=1, source_target_pairs={{0,4},{2,6},{4,0},{6,2},{8,12},{10,14},{12,8},{14,10},{1,5},{3,7},... | collective-permute-start | bytes 786440 | tf_op jit(solution)/shard_map/ppermute | solution.py:1034
  231.5 22.8 %collective-permute-start.120 = (f32[304,512]{1,0:T(8,128)S(1)}, f32[304,512]{1,0:T(8,128)S(1)}, u32[]{:S(2)}, u32[]{:S(2)}) collective-permute-start(f32[304,512]{1,0:T(8,128)S(1)} %get-tuple-element.1091), channel_id=1, source_target_pairs={{0,4},{2,6},{4,0},{6,2},{8,12},{10,14},{12,8},{14,10},{1,5},{3,7},... | collective-permute-start | bytes 1867784 | tf_op jit(solution)/shard_map/ppermute | solution.py:1034
  245.1 22.4 %collective-permute-start.116 = (f32[304,512]{1,0:T(8,128)S(1)}, f32[304,512]{1,0:T(8,128)S(1)}, u32[]{:S(2)}, u32[]{:S(2)}) collective-permute-start(f32[304,512]{1,0:T(8,128)S(1)} %get-tuple-element.1092), channel_id=1, source_target_pairs={{0,2},{2,0},{4,6},{6,4},{8,10},{10,8},{12,14},{14,12},{1,3},{3,1},... | collective-permute-start | bytes 1867784 | tf_op jit(solution)/shard_map/ppermute | solution.py:1034
  254.4 30.5 %collective-permute-start.124 = (f32[320,512]{1,0:T(8,128)S(1)}, f32[320,512]{1,0:T(8,128)S(1)}, u32[]{:S(2)}, u32[]{:S(2)}) collective-permute-start(f32[320,512]{1,0:T(8,128)S(1)} %constant_dynamic-slice_fusion.105), channel_id=1, source_target_pairs={{0,2},{2,0},{4,6},{6,4},{8,10},{10,8},{12,14},{14,12},{1,3},{3,1},... | collective-permute-start | bytes 1966088 | tf_op jit(solution)/shard_map/ppermute | solution.py:1034
  271.1 29.5 %collective-permute-start.131 = (f32[64,1024]{1,0:T(8,128)S(1)}, f32[64,1024]{1,0:T(8,128)S(1)}, u32[]{:S(2)}, u32[]{:S(2)}) collective-permute-start(f32[64,1024]{1,0:T(8,128)S(1)} %add.1948), channel_id=1, source_target_pairs={{0,4},{2,6},{4,0},{6,2},{8,12},{10,14},{12,8},{14,10},{1,5},{3,7},... | collective-permute-start | bytes 786440 | tf_op jit(solution)/shard_map/ppermute | solution.py:1034
  281.9 35.8 %collective-permute-start.129 = (f32[152,512]{1,0:T(8,128)S(1)}, f32[152,512]{1,0:T(8,128)S(1)}, u32[]{:S(2)}, u32[]{:S(2)}) collective-permute-start(f32[152,512]{1,0:T(8,128)S(1)} %dynamic-slice_add_fusion.8), channel_id=1, source_target_pairs={{0,12},{2,14},{4,8},{6,10},{8,4},{10,6},{12,0},{14,2},{1,13},{3,15... | collective-permute-start | bytes 933896 | tf_op jit(solution)/shard_map/ppermute | solution.py:1034
  285.1 26.0 %collective-permute-start.130 = (f32[160,512]{1,0:T(8,128)S(1)}, f32[160,512]{1,0:T(8,128)S(1)}, u32[]{:S(2)}, u32[]{:S(2)}) collective-permute-start(f32[160,512]{1,0:T(8,128)S(1)} %constant_dynamic-slice_fusion.102), channel_id=1, source_target_pairs={{0,4},{2,6},{4,0},{6,2},{8,12},{10,14},{12,8},{14,10},{1,5},{3,7},... | collective-permute-start | bytes 983048 | tf_op jit(solution)/shard_map/ppermute | solution.py:1034
  300.5 28.2 %collective-permute-start.127 = (f32[152,512]{1,0:T(8,128)S(1)}, f32[152,512]{1,0:T(8,128)S(1)}, u32[]{:S(2)}, u32[]{:S(2)}) collective-permute-start(f32[152,512]{1,0:T(8,128)S(1)} %dynamic-slice_add_fusion.9), channel_id=1, source_target_pairs={{0,12},{2,14},{4,8},{6,10},{8,4},{10,6},{12,0},{14,2},{1,13},{3,15... | collective-permute-start | bytes 933896 | tf_op jit(solution)/shard_map/ppermute | solution.py:1034
  311.5 20.7 %collective-permute-start.134 = (f32[160,512]{1,0:T(8,128)S(1)}, f32[160,512]{1,0:T(8,128)S(1)}, u32[]{:S(2)}, u32[]{:S(2)}) collective-permute-start(f32[160,512]{1,0:T(8,128)S(1)} %dynamic-slice_add_fusion.6), channel_id=1, source_target_pairs={{0,12},{2,14},{4,8},{6,10},{8,4},{10,6},{12,0},{14,2},{1,13},{3,15... | collective-permute-start | bytes 983048 | tf_op jit(solution)/shard_map/ppermute | solution.py:1034
  325.3 25.9 %collective-permute-start.137 = (f32[320,512]{1,0:T(8,128)S(1)}, f32[320,512]{1,0:T(8,128)S(1)}, u32[]{:S(2)}, u32[]{:S(2)}) collective-permute-start(f32[320,512]{1,0:T(8,128)S(1)} %get-tuple-element.1679), channel_id=1, source_target_pairs={{0,2},{2,0},{4,6},{6,4},{8,10},{10,8},{12,14},{14,12},{1,3},{3,1},... | collective-permute-start | bytes 1966088 | tf_op jit(solution)/shard_map/ppermute | solution.py:1034
  333.0 29.3 %collective-permute-start.136 = (f32[128,1024]{1,0:T(8,128)S(1)}, f32[128,1024]{1,0:T(8,128)S(1)}, u32[]{:S(2)}, u32[]{:S(2)}) collective-permute-start(f32[128,1024]{1,0:T(8,128)S(1)} %maximum_select_fusion.53), channel_id=1, source_target_pairs={{0,2},{2,0},{4,6},{6,4},{8,10},{10,8},{12,14},{14,12},{1,3},{3,1},... | collective-permute-start | bytes 1572872 | tf_op jit(solution)/shard_map/ppermute | solution.py:1034
  339.5 36.1 %collective-permute-start.142 = (f32[128,1024]{1,0:T(8,128)S(1)}, f32[128,1024]{1,0:T(8,128)S(1)}, u32[]{:S(2)}, u32[]{:S(2)}) collective-permute-start(f32[128,1024]{1,0:T(8,128)S(1)} %maximum_select_fusion.54), channel_id=1, source_target_pairs={{0,4},{2,6},{4,0},{6,2},{8,12},{10,14},{12,8},{14,10},{1,5},{3,7},... | collective-permute-start | bytes 1572872 | tf_op jit(solution)/shard_map/ppermute | solution.py:1034
  346.2 29.4 %collective-permute-start.135 = (f32[304,512]{1,0:T(8,128)S(1)}, f32[304,512]{1,0:T(8,128)S(1)}, u32[]{:S(2)}, u32[]{:S(2)}) collective-permute-start(f32[304,512]{1,0:T(8,128)S(1)} %get-tuple-element.1681), channel_id=1, source_target_pairs={{0,2},{2,0},{4,6},{6,4},{8,10},{10,8},{12,14},{14,12},{1,3},{3,1},... | collective-permute-start | bytes 1867784 | tf_op jit(solution)/shard_map/ppermute | solution.py:1034
  351.1 34.4 %collective-permute-start.140 = (f32[304,512]{1,0:T(8,128)S(1)}, f32[304,512]{1,0:T(8,128)S(1)}, u32[]{:S(2)}, u32[]{:S(2)}) collective-permute-start(f32[304,512]{1,0:T(8,128)S(1)} %maximum_select_fusion.52), channel_id=1, source_target_pairs={{0,4},{2,6},{4,0},{6,2},{8,12},{10,14},{12,8},{14,10},{1,5},{3,7},... | collective-permute-start | bytes 1867784 | tf_op jit(solution)/shard_map/ppermute | solution.py:1034
  351.2 34.3 %collective-permute-start.141 = (f32[320,512]{1,0:T(8,128)S(1)}, f32[320,512]{1,0:T(8,128)S(1)}, u32[]{:S(2)}, u32[]{:S(2)}) collective-permute-start(f32[320,512]{1,0:T(8,128)S(1)} %maximum_select_fusion.50), channel_id=1, source_target_pairs={{0,2},{2,0},{4,6},{6,4},{8,10},{10,8},{12,14},{14,12},{1,3},{3,1},... | collective-permute-start | bytes 1966088 | tf_op jit(solution)/shard_map/ppermute | solution.py:1034
  (50 other events, 500.9 us)
